TPU v7x, 32 devices: a whole 2x2x4 slice. The times are simulated.
32 devices in a mesh: rows: 16 (over z, y, x), blk: 2 (over core).
Axes of the slice: x: 2, y: 2, z: 4, core: 2. Of those that a mesh axis runs over, the one named last changes fastest.
Arguments:
- tokens: bfloat16 [64, 512, 768], P(('rows', 'blk')), may hold values from -6 to 6
- lengths: int32 [64, 8], P(('rows', 'blk')), may hold values from 1 to 505, as said below
- attn_gain: bfloat16 [768], replicated, may hold values from 0.5 to 1.5
- w_query: bfloat16 [768, 768], replicated, may hold values from -0.0546875 to 0.0546875
- w_key: bfloat16 [768, 768], replicated, may hold values from -0.21875 to 0.21875
- w_value: bfloat16 [768, 768], replicated, may hold values from -0.21875 to 0.21875
- w_output: bfloat16 [768, 768], replicated, may hold values from -0.625 to 0.625
- bucket_bias_table: bfloat16 [32, 12], replicated, may hold values from -4 to 4
- ffn_gain: bfloat16 [768], replicated, may hold values from 0.5 to 1.5
- w_in: bfloat16 [768, 3072], replicated, may hold values from -0.21875 to 0.21875
- w_out: bfloat16 [3072, 768], replicated, may hold values from -0.15625 to 0.15625
- out_grad: bfloat16 [64, 512, 768], P(('rows', 'blk')), may hold values from -6 to 6
Outputs:
- mixed: bfloat16 [64, 512, 768], P(('rows', 'blk'))
- tokens_grad: bfloat16 [64, 512, 768], P(('rows', 'blk'))
- attn_gain_grad: float32 [768], replicated
- w_query_grad: float32 [768, 768], replicated
- w_key_grad: float32 [768, 768], replicated
- w_value_grad: float32 [768, 768], replicated
- w_output_grad: float32 [768, 768], replicated
- bias_table_grad: float32 [32, 12], replicated
- ffn_gain_grad: float32 [768], replicated
- w_in_grad: float32 [768, 3072], replicated
- w_out_grad: float32 [3072, 768], replicated
Inputs may be any that keep to these rules, and one draw needn't show every extreme that they name: `lengths`: each row's 8 entries are positive and sum to 512; the first 7 are query-passage pairs, the last is a padding run of at most 25 tokens (row 1 has exactly that many).
All inputs are finite; a program needn't handle non-finite values.
Results may differ from a plain program's by a relative error of at most 0.014.
The roundings to bfloat16 on the way count: a program that leaves them out, or rounds other values in their place, can miss the bound.
Values sent between devices are 32-bit elements; how exact they have to be, the bound alone decides.
No kernel may reach another device: no remote copies, remote signals or barrier semaphores. Data moves between devices by JAX's collectives and lax.ppermute only.
A program may use at most 320 MiB of HBM per device.

v0:
```python
import jax
import jax.numpy as jnp
import numpy as np
from jax import lax
from jax.sharding import PartitionSpec as P

far_steps = np.array([12, 16, 23, 32, 46, 64, 91], dtype=np.int32)
highest_precision = lax.Precision.HIGHEST


def bucket_of(relative, bucket_count):
    distance = jnp.abs(relative)
    beyond = jnp.sum((distance[..., None] >= jnp.asarray(far_steps)).astype(jnp.int32), axis=-1)
    inner = jnp.where(distance < bucket_count // 4, distance, bucket_count // 4 + beyond)
    return jnp.where(relative > 0, bucket_count // 2, 0) + inner


def segment_of(lengths, positions):
    ends = jnp.cumsum(lengths, axis=-1)
    return jnp.sum((positions[None, :, None] >= ends[:, None, :]).astype(jnp.int32), axis=-1)


def norm_rows(value, gain):
    return value * lax.rsqrt(jnp.mean(value * value, axis=-1, keepdims=True) + 1e-06) * gain


def gelu_tanh(value):
    return jax.nn.gelu(value, approximate=True)


def on_device(
    tokens,
    lengths,
    attn_gain,
    w_query,
    w_key,
    w_value,
    w_output,
    bucket_bias_table,
    ffn_gain,
    w_in,
    w_out,
    out_grad,
):
    row_count, row_length, model_width = tokens.shape
    bucket_count, head_count = bucket_bias_table.shape
    head_size = model_width // head_count
    seg_count = lengths.shape[1]
    inputs = tokens.astype(jnp.float32)
    gain_one = attn_gain.astype(jnp.float32)
    gain_two = ffn_gain.astype(jnp.float32)
    bucket_table = bucket_bias_table.astype(jnp.float32)
    positions = jnp.arange(row_length, dtype=jnp.int32)
    segments = segment_of(lengths, positions)
    key_valid = segments < seg_count - 1
    query_valid = key_valid.astype(jnp.float32)[..., None]
    allowed = (segments[:, :, None] == segments[:, None, :]) & key_valid[:, None, :]
    penalty = jnp.where(allowed, 0.0, -1000000000.0)[:, None]
    buckets = bucket_of(positions[None, :] - positions[:, None], bucket_count)
    bucket_indicator = (
        buckets[None] == jnp.arange(bucket_count, dtype=jnp.int32)[:, None, None]
    ).astype(jnp.float32)
    position_bias = jnp.einsum(
        "ced,ci->ied", bucket_indicator, bucket_table, precision=highest_precision
    )
    hidden_one = norm_rows(inputs, gain_one).astype(jnp.bfloat16)

    def project(weight):
        return jnp.einsum(
            "rtd,de->rte", hidden_one, weight, preferred_element_type=jnp.float32
        ).astype(jnp.bfloat16)

    query_heads = project(w_query).reshape(row_count, row_length, head_count, head_size)
    key_heads = project(w_key).reshape(row_count, row_length, head_count, head_size)
    value_heads = project(w_value).reshape(row_count, row_length, head_count, head_size)

    def score_of():
        products = jnp.einsum(
            "rqhd,rkhd->rhqk", query_heads, key_heads, preferred_element_type=jnp.float32
        )
        return products + position_bias[None] + penalty

    scores = score_of()
    top_score = jnp.max(scores, axis=-1, keepdims=True)
    exponent = jnp.exp(scores - top_score)
    total_exp = jnp.sum(exponent, axis=-1, keepdims=True)
    log_total = top_score + jnp.log(total_exp)
    attention = exponent / total_exp
    attended = jnp.einsum(
        "rhqk,rkhd->rqhd",
        attention.astype(jnp.bfloat16),
        value_heads,
        preferred_element_type=jnp.float32,
    )
    attended_low = (attended.reshape(row_count, row_length, model_width) * query_valid).astype(
        jnp.bfloat16
    )
    residual = inputs + jnp.einsum(
        "rtd,de->rte", attended_low, w_output, preferred_element_type=jnp.float32
    )
    hidden_two = norm_rows(residual, gain_two).astype(jnp.bfloat16)
    pre_act = jnp.einsum("rtd,df->rtf", hidden_two, w_in, preferred_element_type=jnp.float32)
    activated, gelu_pull = jax.vjp(gelu_tanh, pre_act)
    act_low = activated.astype(jnp.bfloat16)
    mixed = (
        residual + jnp.einsum("rtf,fd->rtd", act_low, w_out, preferred_element_type=jnp.float32)
    ).astype(jnp.bfloat16)
    grad_w_out = jnp.einsum("rtf,rtd->fd", act_low, out_grad, preferred_element_type=jnp.float32)
    grad_act = jnp.einsum("rtd,fd->rtf", out_grad, w_out, preferred_element_type=jnp.float32)
    grad_pre = gelu_pull(grad_act)[0].astype(jnp.bfloat16)
    grad_w_in = jnp.einsum("rtd,rtf->df", hidden_two, grad_pre, preferred_element_type=jnp.float32)
    grad_two = jnp.einsum("rtf,df->rtd", grad_pre, w_in, preferred_element_type=jnp.float32)
    _, norm_pull_two = jax.vjp(norm_rows, residual, gain_two)
    grad_resid_part, grad_gain_two = norm_pull_two(grad_two)
    ffn_totals = lax.psum((grad_gain_two, grad_w_in, grad_w_out), ("rows", "blk"))
    grad_resid = out_grad.astype(jnp.float32) + grad_resid_part
    grad_branch = grad_resid.astype(jnp.bfloat16)
    grad_w_output = jnp.einsum(
        "rtd,rte->de", attended_low, grad_branch, preferred_element_type=jnp.float32
    )
    grad_att = (
        jnp.einsum("rte,de->rtd", grad_branch, w_output, preferred_element_type=jnp.float32)
        * query_valid
    ).astype(jnp.bfloat16)
    grad_heads = grad_att.reshape(row_count, row_length, head_count, head_size)
    again = jnp.exp(score_of() - log_total)
    grad_probs = jnp.einsum(
        "rqhd,rkhd->rhqk", grad_heads, value_heads, preferred_element_type=jnp.float32
    )
    grad_value = jnp.einsum(
        "rhqk,rqhd->rkhd",
        again.astype(jnp.bfloat16),
        grad_heads,
        preferred_element_type=jnp.float32,
    )
    score_gradient = again * (grad_probs - jnp.sum(again * grad_probs, axis=-1, keepdims=True))
    table_gradient = jnp.einsum(
        "cul,xul->cx",
        bucket_indicator,
        jnp.sum(score_gradient, axis=0),
        precision=highest_precision,
    )
    grad_low = score_gradient.astype(jnp.bfloat16)
    grad_query = jnp.einsum(
        "rhqk,rkhd->rqhd", grad_low, key_heads, preferred_element_type=jnp.float32
    )
    grad_key = jnp.einsum(
        "rhqk,rqhd->rkhd", grad_low, query_heads, preferred_element_type=jnp.float32
    )
    grad_query = grad_query.reshape(row_count, row_length, model_width).astype(jnp.bfloat16)
    grad_key = grad_key.reshape(row_count, row_length, model_width).astype(jnp.bfloat16)
    grad_value = grad_value.reshape(row_count, row_length, model_width).astype(jnp.bfloat16)

    def weight_grad(grad_proj):
        return jnp.einsum("rtd,rte->de", hidden_one, grad_proj, preferred_element_type=jnp.float32)

    def back_proj(grad_proj, weight):
        return jnp.einsum("rte,de->rtd", grad_proj, weight, preferred_element_type=jnp.float32)

    grad_w_query = weight_grad(grad_query)
    grad_w_key = weight_grad(grad_key)
    grad_w_value = weight_grad(grad_value)
    grad_one = (
        back_proj(grad_query, w_query) + back_proj(grad_key, w_key) + back_proj(grad_value, w_value)
    )
    _, norm_pull_one = jax.vjp(norm_rows, inputs, gain_one)
    grad_input_part, grad_gain_one = norm_pull_one(grad_one)
    tokens_grad = (grad_resid + grad_input_part).astype(jnp.bfloat16)
    attn_totals = lax.psum(
        (grad_gain_one, grad_w_query, grad_w_key, grad_w_value, grad_w_output, table_gradient),
        ("rows", "blk"),
    )
    totals = (
        attn_totals[0],
        attn_totals[1],
        attn_totals[2],
        attn_totals[3],
        attn_totals[4],
        attn_totals[5],
        ffn_totals[0],
        ffn_totals[1],
        ffn_totals[2],
    )
    return (
        mixed,
        tokens_grad,
        totals[0],
        totals[1],
        totals[2],
        totals[3],
        totals[4],
        totals[5],
        totals[6],
        totals[7],
        totals[8],
    )


def solution(mesh):
    in_specs = (
        P(("rows", "blk"), None, None),
        P(("rows", "blk"), None),
        P(),
        P(),
        P(),
        P(),
        P(),
        P(),
        P(),
        P(),
        P(),
        P(("rows", "blk"), None, None),
    )
    out_specs = (
        P(("rows", "blk"), None, None),
        P(("rows", "blk"), None, None),
        P(),
        P(),
        P(),
        P(),
        P(),
        P(),
        P(),
        P(),
        P(),
    )
    return jax.shard_map(
        on_device, mesh=mesh, in_specs=in_specs, out_specs=out_specs, check_vma=False
    )
```

profile of v0, /device:TPU:0, one launch (start us, length us, event | category | flops | bytes accessed | tf_op | source)
XLA Modules:
  0.0 786.4 jit_solution(125354426434952880)
XLA Ops:
  38.1 9.8 %iota_compare_fusion = pred[32,512,512]{1,0,2:T(32,128)(4,1)} fusion(s32[512,512]{0,1:T(8,128)} %copy.104), kind=kLoop, calls=%fused_computation | loop fusion | flops 8388608 | bytes 9437184 | tf_op jit(solution)/shard_map/eq | solution.py:61
  47.9 46.4 %copy.105 = pred[32,512,512]{2,0,1:T(32,128)(4,1)} copy(pred[32,512,512]{1,0,2:T(32,128)(4,1)} %iota_compare_fusion) | data formatting | bytes 16777216 | tf_op jit(solution)/shard_map/eq | solution.py:61
  94.4 13.0 %convolution_bitcast_fusion = f32[12,512,512]{2,0,1:T(8,128)} fusion(pred[32,512,512]{2,0,1:T(32,128)(4,1)} %copy.105, bf16[32,12]{0,1:T(8,128)(2,1)S(1)} %copy-done.26), kind=kOutput, calls=%fused_computation.24 | convolution fusion | flops 201326592 | bytes 20972288 | tf_op jit(solution)/shard_map/ced,ci->ied/dot_general | solution.py:63
  107.4 17.8 %copy.106 = f32[12,512,512]{1,2,0:T(8,128)} copy(f32[12,512,512]{2,0,1:T(8,128)} %convolution_bitcast_fusion) | data formatting | bytes 25165824 | tf_op jit(solution)/shard_map/ced,ci->ied/dot_general | solution.py:63
  125.2 14.5 %fusion.69 = (f32[2,12,512]{2,1,0:T(8,128)S(1)}, f32[2,12,512,512]{2,3,1,0:T(8,128)}) fusion(f32[2,512,512]{1,2,0:T(8,128)} %and_select_fusion, f32[12,512,512]{1,2,0:T(8,128)} %copy.106, bf16[2,512,12,64]{1,3,2,0:T(8,128)(2,1)} %bitcast.100, bf16[2,512,12,64]{1,3,2,0:T(8,128)(2,1)} %bitcast.96), kind=kOutput, calls=%fused_computation.103 | convolution fusion | flops 824168448 | bytes 43040768 | tf_op jit(solution)/shard_map/rqhd,rkhd->rhqk/dot_general | solution.py:78
  139.7 10.4 %fusion = f32[2,12,512]{2,1,0:T(8,128)S(1)} fusion(f32[2,12,512,512]{2,3,1,0:T(8,128)} %get-tuple-element.29, f32[2,12,512]{2,1,0:T(8,128)S(1)} %get-tuple-element.28), kind=kLoop, calls=%fused_computation.7 | loop fusion | flops 12570624 | bytes 25264128 | tf_op jit(solution)/shard_map/reduce_sum | solution.py:86
  150.1 12.2 %fusion.14 = f32[2,12,64,512]{3,2,1,0:T(8,128)} fusion(bf16[2,512,12,64]{1,3,2,0:T(8,128)(2,1)S(1)} %bitcast.105, f32[2,12,512,512]{2,3,1,0:T(8,128)} %get-tuple-element.29, f32[2,12,512]{2,1,0:T(8,128)S(1)} %fusion, f32[2,12,512]{2,1,0:T(8,128)S(1)} %get-tuple-element.28), kind=kOutput, calls=%fused_computation.23 | convolution fusion | flops 824180736 | bytes 29982720 | tf_op jit(solution)/shard_map/rhqk,rkhd->rqhd/dot_general | solution.py:89
  169.7 11.5 %fusion.23 = f32[2,512,3072]{2,1,0:T(8,128)} fusion(bf16[768,3072]{1,0:T(8,128)(2,1)} %param.22, f32[2,512,768]{2,1,0:T(8,128)S(1)} %get-tuple-element.31, f32[768]{0:T(1024)S(1)} %convert_element_type.110, f32[2,512]{1,0:T(2,128)S(1)} %fusion.61), kind=kOutput, calls=%fused_computation.43 | convolution fusion | flops 4834197504 | bytes 20454400 | tf_op jit(solution)/shard_map/rtd,df->rtf/dot_general | solution.py:102
  181.2 12.5 %convolution_bitcast_fusion.1 = f32[3072,768]{1,0:T(8,128)} fusion(bf16[2,512,768]{2,1,0:T(8,128)(2,1)S(1)} %copy-done.17, f32[2,512,3072]{2,1,0:T(8,128)} %fusion.23), kind=kOutput, calls=%fused_computation.33 | convolution fusion | flops 4860149760 | bytes 23592960 | tf_op jit(solution)/shard_map/rtf,rtd->fd/dot_general | solution.py:108
  193.7 14.4 %fusion.10 = bf16[2,512,3072]{2,1,0:T(8,128)(2,1)S(1)} fusion(f32[2,512,3072]{2,1,0:T(8,128)} %fusion.23, bf16[2,512,768]{2,1,0:T(8,128)(2,1)S(1)} %copy-done.17, bf16[3072,768]{1,0:T(8,128)(2,1)} %param.23), kind=kOutput, calls=%fused_computation.19 | convolution fusion | flops 4894752768 | bytes 25165824 | tf_op jit(solution)/shard_map/rtd,fd->rtf/dot_general | solution.py:109
  208.0 7.8 multiply_reduce_fusion.1
  215.8 8.2 %convolution_bitcast_fusion.2 = f32[768,3072]{1,0:T(8,128)} fusion(bf16[2,512,3072]{2,1,0:T(8,128)(2,1)S(1)} %fusion.10, f32[2,512,768]{2,1,0:T(8,128)S(1)} %get-tuple-element.31, f32[768]{0:T(1024)S(1)} %convert_element_type.110, f32[2,512]{1,0:T(2,128)S(1)} %fusion.61), kind=kOutput, calls=%fused_computation.34 | convolution fusion | flops 4834197504 | bytes 18881536 | tf_op jit(solution)/shard_map/rtd,rtf->df/dot_general | solution.py:111
  234.2 13.7 %fusion.38 = bf16[2,12,64,512]{3,2,1,0:T(8,128)(2,1)} fusion(bf16[2,512,12,64]{1,3,2,0:T(8,128)(2,1)} %bitcast.98, f32[2,12,512,512]{2,3,1,0:T(8,128)} %get-tuple-element.29, f32[2,12,512]{2,1,0:T(8,128)S(1)} %log_add_fusion), kind=kOutput, calls=%fused_computation.70 | convolution fusion | flops 818675712 | bytes 28360704 | tf_op jit(solution)/shard_map/rhqk,rqhd->rkhd/dot_general | solution.py:130
  247.9 17.0 %multiply_reduce_fusion = (f32[2,12,512]{2,1,0:T(8,128)S(1)}, f32[2,12,512,512]{2,3,1,0:T(8,128)}) fusion(f32[2,12,512,512]{2,3,1,0:T(8,128)} %get-tuple-element.29, f32[2,12,512]{2,1,0:T(8,128)S(1)} %log_add_fusion, bf16[2,512,12,64]{1,3,2,0:T(8,128)(2,1)} %bitcast.99, bf16[2,512,12,64]{1,3,2,0:T(8,128)(2,1)} %bitcast.104), kind=kOutput, calls=%fused_computation.2 | convolution fusion | flops 824168448 | bytes 53575680 | tf_op jit(solution)/shard_map/rqhd,rkhd->rhqk/dot_general | solution.py:127
  264.9 27.0 %fusion.15 = (f32[12,512,512]{1,2,0:T(8,128)}, bf16[2,12,512,512]{2,3,1,0:T(8,128)(2,1)}) fusion(f32[2,12,512,512]{2,3,1,0:T(8,128)} %get-tuple-element.34, f32[2,12,512]{2,1,0:T(8,128)S(1)} %get-tuple-element.33, f32[2,12,512,512]{2,3,1,0:T(8,128)} %get-tuple-element.29, f32[2,12,512]{2,1,0:T(8,128)S(1)} %log_add_fusion), kind=kLoop, calls=%fused_computation.26 | loop fusion | flops 28311552 | bytes 75595776 | tf_op jit(solution)/shard_map/reduce_sum | solution.py:140
  291.9 8.6 %convolution_convert_fusion = bf16[2,12,64,512]{3,2,1,0:T(8,128)(2,1)S(1)} fusion(bf16[2,512,12,64]{1,3,2,0:T(8,128)(2,1)S(1)} %bitcast.101, bf16[2,12,512,512]{2,3,1,0:T(8,128)(2,1)} %get-tuple-element.27), kind=kOutput, calls=%fused_computation.68 | convolution fusion | flops 806092800 | bytes 15728640 | tf_op jit(solution)/shard_map/rhqk,rqhd->rkhd/dot_general | solution.py:147
  300.6 7.3 convolution_convert_fusion.1
  322.0 4.2 fusion.30
  326.3 24.9 %fusion.51 = f32[32,12]{0,1:T(8,128)S(1)} fusion(f32[12,512,512]{1,2,0:T(8,128)} %get-tuple-element.26, s32[512,512]{0,1:T(8,128)S(1)} %copy-done.8), kind=kOutput, calls=%fused_computation.84 | convolution fusion | flops 1216348160 | bytes 13633024 | tf_op jit(solution)/shard_map/cul,xul->cx/dot_general | solution.py:137
  351.2 43.0 %all-reduce = (f32[768]{0:T(1024)}, f32[32,12]{0,1:T(8,128)}, f32[768]{0:T(1024)}) all-reduce(f32[768]{0:T(1024)S(1)} %get-tuple-element.13, f32[32,12]{0,1:T(8,128)S(1)} %fusion.51, f32[768]{0:T(1024)S(1)} %get-tuple-element.11), channel_id=1, replica_groups=mesh['rows'=16,'blk'=2] {'rows','blk'}, use_global_device_ids=true, to_apply=%region_11.12 | all-reduce | flops 1920 | bytes 15360 | tf_op jit(solution)/shard_map/psum | solution.py:169
  394.2 5.0 fusion.33
  399.2 12.7 %add_convert_fusion = bf16[2,512,768]{2,1,0:T(8,128)(2,1)} fusion(f32[2,512,768]{2,1,0:T(8,128)S(1)} %copy-done.2, bf16[3072,768]{1,0:T(8,128)(2,1)} %param.23, f32[2,512,3072]{2,1,0:T(8,128)} %fusion.23), kind=kOutput, calls=%fused_computation.58 | convolution fusion | flops 4861722624 | bytes 22020096 | tf_op jit(solution)/shard_map/rtf,fd->rtd/dot_general | solution.py:106
  411.9 344.3 %all-reduce.4.cloned.1.call-done = (f32[768,768]{1,0:T(8,128)}, f32[768,768]{1,0:T(8,128)}, f32[768,768]{1,0:T(8,128)}, f32[768,768]{1,0:T(8,128)}, f32[768,3072]{1,0:T(8,128)}, /*index=5*/f32[3072,768]{1,0:T(8,128)}) async-done(((f32[768,768]{1,0:T(8,128)}, f32[768,768]{1,0:T(8,128)}, f32[768,768]{1,0:T(8,128)}, f32[768,768]{1,0:T(8,128)}, f32[768,3072]{1,0:T(8,128)}, /*index=5*/f32[3072,768]{1,0:T(8,128)}), ...) | async-done | bytes 28311568 | tf_op jit(solution)/shard_map/psum | solution.py:169
  766.0 9.3 %copy.158 = f32[768,3072]{1,0:T(8,128)} copy(f32[768,3072]{1,0:T(8,128)} %get-tuple-element.45) | data formatting | bytes 18874368
  (103 shorter events, 76.1 us)
Async XLA Ops:
  7.2 24.2 %copy-start = (bf16[768,768]{1,0:T(8,128)(2,1)S(1)}, bf16[768,768]{1,0:T(8,128)(2,1)}, u32[]{:S(2)}) copy-start(bf16[768,768]{1,0:T(8,128)(2,1)} %param.18) | copy-start | bytes 3538948
  7.2 749.0 %all-reduce.4.cloned.1.call-start = ((), (), s32[]{:S(2)}) async-start(), calls=%async_computation | async-start | bytes 56623104 | tf_op jit(solution)/shard_map/psum | solution.py:169
  10.0 21.4 %copy-start.20 = (f32[768]{0:T(1024)}, f32[768]{0:T(1024)S(1)}, u32[]{:S(2)}) copy-start(f32[768]{0:T(1024)S(1)} %convert_element_type.100) | copy-start | bytes 9220
  12.5 6.1 copy-start.24
  12.5 18.9 %copy-start.22 = (f32[2,512]{1,0:T(2,128)}, f32[2,512]{1,0:T(2,128)S(1)}, u32[]{:S(2)}) copy-start(f32[2,512]{1,0:T(2,128)S(1)} %fusion.60) | copy-start | bytes 12292
  12.5 6.0 copy-start.3
  47.9 46.4 %copy-start.26 = (bf16[32,12]{0,1:T(8,128)(2,1)S(1)}, bf16[32,12]{0,1:T(8,128)(2,1)}, u32[]{:S(2)}) copy-start(bf16[32,12]{0,1:T(8,128)(2,1)} %param.20) | copy-start | bytes 2308
  139.7 10.4 %copy-start.9 = (bf16[2,512,768]{1,2,0:T(8,128)(2,1)S(1)}, bf16[2,512,768]{1,2,0:T(8,128)(2,1)}, u32[]{:S(2)}) copy-start(bf16[2,512,768]{1,2,0:T(8,128)(2,1)} %copy.101) | copy-start | bytes 4718596
  169.7 54.4 %copy-start.1 = (f32[2,512,768]{2,1,0:T(8,128)}, f32[2,512,768]{2,1,0:T(8,128)S(1)}, u32[]{:S(2)}) copy-start(f32[2,512,768]{2,1,0:T(8,128)S(1)} %get-tuple-element.31) | copy-start | bytes 9437188
  169.7 11.5 %copy-start.17 = (bf16[2,512,768]{2,1,0:T(8,128)(2,1)S(1)}, bf16[2,512,768]{2,1,0:T(8,128)(2,1)}, u32[]{:S(2)}) copy-start(bf16[2,512,768]{2,1,0:T(8,128)(2,1)} %param.24) | copy-start | bytes 4718596
  264.9 27.0 %copy-start.5 = (bf16[2,512,768]{1,2,0:T(8,128)(2,1)S(1)}, bf16[2,512,768]{1,2,0:T(8,128)(2,1)}, u32[]{:S(2)}) copy-start(bf16[2,512,768]{1,2,0:T(8,128)(2,1)} %copy.102) | copy-start | bytes 4718596
  291.9 8.6 %copy-start.4 = (bf16[2,512,768]{1,2,0:T(8,128)(2,1)S(1)}, bf16[2,512,768]{1,2,0:T(8,128)(2,1)}, u32[]{:S(2)}) copy-start(bf16[2,512,768]{1,2,0:T(8,128)(2,1)} %copy.103) | copy-start | bytes 4718596
  300.5 10.5 %copy-start.18 = (bf16[2,12,64,512]{3,2,1,0:T(8,128)(2,1)}, bf16[2,12,64,512]{3,2,1,0:T(8,128)(2,1)S(1)}, u32[]{:S(2)}) copy-start(bf16[2,12,64,512]{3,2,1,0:T(8,128)(2,1)S(1)} %convolution_convert_fusion) | copy-start | bytes 4718596
  300.5 7.4 copy-start.10
  300.6 7.4 copy-start.21
  300.6 7.4 copy-start.23
  307.9 6.2 copy-start.12
  322.0 4.2 copy-start.8
  326.3 67.9 %copy-start.25 = (f32[2,512]{1,0:T(2,128)S(1)}, f32[2,512]{1,0:T(2,128)}, u32[]{:S(2)}) copy-start(f32[2,512]{1,0:T(2,128)} %copy-done.24) | copy-start | bytes 12292
  394.2 5.0 copy-start.2
  756.2 3.4 copy-start.16
  764.6 10.7 %slice-start = ((s8[9437184]{0:T(1024)(128)(4,1)}), s8[4194304]{0:T(1024)(128)(4,1)S(1)}, s32[]{:S(2)}) async-start(s8[9437184]{0:T(1024)(128)(4,1)} %bitcast.102), calls=%async_computation.1 | async-start | bytes 8388608
  766.0 9.3 %slice-start.1 = ((s8[9437184]{0:T(1024)(128)(4,1)}), s8[4194304]{0:T(1024)(128)(4,1)S(1)}, s32[]{:S(2)}) async-start(s8[9437184]{0:T(1024)(128)(4,1)} %bitcast.102), calls=%async_computation.2 | async-start | bytes 8388608
  766.0 9.3 %slice-start.2 = ((s8[9437184]{0:T(1024)(128)(4,1)}), s8[1048576]{0:T(1024)(128)(4,1)S(1)}, s32[]{:S(2)}) async-start(s8[9437184]{0:T(1024)(128)(4,1)} %bitcast.102), calls=%async_computation.3 | async-start | bytes 2097152
  (8 other events, 21.1 us)
Sparse Core Ops, SparseCore 0:
  317.3 438.8 all-reduce.3
where the time goes:
time: 795 us; the launch traced here: 786 us
  waiting for transfers between devices  344 us (43%)
  matrix products  216 us (27%)
  local copies, waits for them, and re-layouts  105 us (13%)
  other arithmetic  63.2 us (8%)
  blocking collectives  43 us (5%)
  between operations  14.8 us (2%)
    psum x1, waiting for transfers between devices, on_device(): lax.psum((grad_gain_one, grad_w_query, grad_w_key, grad_w_value, grad_w_o...  344 us
    eq x1, local copies, waits for them, and re-layouts, on_device(): buckets[None] == jnp.arange(bucket_count, dtype=jnp.int32)[:, None, None]  46.4 us
    psum x1, blocking collectives, on_device(): lax.psum((grad_gain_one, grad_w_query, grad_w_key, grad_w_value, grad_w_o...  43 us
    reduce_sum x1, other arithmetic, on_device(): jnp.sum(score_gradient, axis=0)  27 us
    dot_general x1, matrix products, on_device(): jnp.einsum('cul,xul->cx', bucket_indicator, jnp.sum(score_gradient, axis=...  24.9 us
    unnamed x68, local copies, waits for them, and re-layouts  24.1 us
    dot_general x1, local copies, waits for them, and re-layouts, on_device(): jnp.einsum('ced,ci->ied', bucket_indicator, bucket_table, precision=highe...  17.8 us
    dot_general x1, matrix products, on_device(): jnp.einsum('rqhd,rkhd->rhqk', grad_heads, value_heads, preferred_element_...  17 us
  transfers between devices with their start and end apart: 1, of which 1 were waited for; matrix products, arithmetic and copies ran while one was open for 7% of the time, Pallas kernels for 0%

commit v1 on v0

v1 whole, which is shorter than its diff:
```python
import functools
import jax
import jax.numpy as jnp
import numpy as np
from jax import lax
from jax.experimental import pallas as pl
from jax.experimental.pallas import tpu as pltpu
from jax.sharding import PartitionSpec as P

NT = (((1,), (1,)), ((), ()))
TN = (((0,), (0,)), ((), ()))
F32, BF16 = jnp.float32, jnp.bfloat16
TILE = 128
MASKED = -1000000000.0
EPS = 1e-06
far_steps = np.array([12, 16, 23, 32, 46, 64, 91], dtype=np.int32)


def dot(a, b, dims=None):
    if dims is None:
        return jnp.dot(a, b, preferred_element_type=F32)
    return lax.dot_general(a, b, dims, preferred_element_type=F32)


def bucket_of(relative, bucket_count):
    distance = np.abs(relative)
    beyond = np.sum(distance[..., None] >= far_steps, axis=-1)
    inner = np.where(distance < bucket_count // 4, distance, bucket_count // 4 + beyond)
    return np.where(relative > 0, bucket_count // 2, 0) + inner


def band_buckets(bucket_count):
    lanes = np.arange(4 * TILE)
    offsets = np.where(lanes < 2 * TILE, lanes, lanes - 4 * TILE)
    return bucket_of(-offsets, bucket_count)


def segments_along(len_ref, row, shape, axis):
    at = lax.broadcasted_iota(jnp.int32, shape, axis)
    total = jnp.zeros(shape, jnp.int32)
    end = jnp.int32(0)
    for j in range(len_ref.shape[1]):
        end = end + len_ref[row, j]
        total = total + jnp.where(at >= end, 1, 0)
    return total


def fill_mask(len_ref, row, mask_ref, last):
    seq = mask_ref.shape[0]
    of_q = segments_along(len_ref, row, (1, seq), 1)
    of_k = segments_along(len_ref, row, (seq, TILE), 0)
    of_k = jnp.where(of_k < last, of_k, -1)
    for j in range(seq // TILE):
        same = of_k == of_q[:, j * TILE : (j + 1) * TILE]
        mask_ref[:, j * TILE : (j + 1) * TILE] = jnp.where(same, 0.0, MASKED)
    return of_q < last


def band_of(vector):
    wide = jnp.broadcast_to(vector, (TILE, 4 * TILE))
    return pltpu.roll(wide, 0, 1, stride=1, stride_axis=0)


def bias_row(band, vector, ki, count):
    shape = (TILE, TILE)
    tiles = []
    for qi in range(count):
        step = ki - qi
        if step == 0:
            tiles.append(band[:, 0:TILE])
        elif step == -1:
            tiles.append(band[:, TILE : 2 * TILE])
        elif step == 1:
            tiles.append(band[:, 3 * TILE : 4 * TILE])
        elif step < 0:
            tiles.append(jnp.broadcast_to(vector[:, 2 * TILE - 1 : 2 * TILE], shape))
        else:
            tiles.append(jnp.broadcast_to(vector[:, 2 * TILE : 2 * TILE + 1], shape))
    return jnp.concatenate(tiles, axis=1)


def norm_scale(value):
    return lax.rsqrt(jnp.mean(value * value, axis=-1, keepdims=True) + EPS)


def attn_fwd_kernel(
    len_ref, tok_ref, gain1_ref, gain2_ref, wq_ref, wk_ref, wv_ref, wo_ref, band_ref,
    h1_ref, q_ref, k_ref, v_ref, att_ref, attT_ref, lse_ref, x1_ref, h2_ref,
    mask_ref, s_ref, p_ref,
):
    seq, width = tok_ref.shape[1:]
    heads = band_ref.shape[0]
    head = width // heads
    row = pl.program_id(0)
    valid = fill_mask(len_ref, row, mask_ref, len_ref.shape[1] - 1)
    tok = tok_ref[0].astype(F32)
    h1 = (tok * norm_scale(tok) * gain1_ref[...].astype(F32)).astype(BF16)
    h1_ref[0] = h1
    q_ref[0] = dot(h1, wq_ref[...]).astype(BF16)
    k_ref[0] = dot(h1, wk_ref[...]).astype(BF16)
    v_ref[0] = dot(h1, wv_ref[...]).astype(BF16)
    count = seq // TILE
    low_half = lax.broadcasted_iota(jnp.int32, (1, TILE), 1) < head

    def pair(p, carry):
        lanes = pl.ds(pl.multiple_of(p * TILE, TILE), TILE)
        qp, kp, vp = q_ref[0, :, lanes], k_ref[0, :, lanes], v_ref[0, :, lanes]
        vT = vp.T
        outs = []
        for a in range(2):
            qm = jnp.where(low_half if a == 0 else ~low_half, qp, jnp.zeros_like(qp))
            vector = band_ref[pl.ds(2 * p + a, 1), :]
            band = band_of(vector)
            top = None
            for ki in range(count):
                rows = slice(ki * TILE, (ki + 1) * TILE)
                s = dot(kp[rows], qm, NT) + bias_row(band, vector, ki, count) + mask_ref[rows, :]
                s_ref[a, rows, :] = s
                most = jnp.max(s, axis=0, keepdims=True)
                top = most if top is None else jnp.maximum(top, most)
            total = jnp.zeros_like(top)
            for ki in range(count):
                rows = slice(ki * TILE, (ki + 1) * TILE)
                e = jnp.exp(s_ref[a, rows, :] - top)
                total = total + jnp.sum(e, axis=0, keepdims=True)
                p_ref[a, rows, :] = e.astype(BF16)
            o = dot(vT[a * head : (a + 1) * head], p_ref[a])
            o = jnp.where(valid, o / total, 0.0)
            outs.append(o)
            lse_ref[0, pl.ds(2 * p + a, 1), :] = top + jnp.log(total)
        both = jnp.concatenate(outs, axis=0)
        attT_ref[0, lanes, :] = both.astype(BF16)
        att_ref[0, :, lanes] = both.T.astype(BF16)
        return carry

    lax.fori_loop(0, heads // 2, pair, 0)
    x1 = tok_ref[0].astype(F32) + dot(att_ref[0], wo_ref[...])
    x1_ref[0] = x1
    h2_ref[0] = (x1 * norm_scale(x1) * gain2_ref[...].astype(F32)).astype(BF16)


VMEM = 60 * 2**20


def params(**kw):
    return pltpu.CompilerParams(vmem_limit_bytes=VMEM, **kw)


def attn_fwd(tokens, lengths, gain1, gain2, wq, wk, wv, wo, band):
    rows, seq, width = tokens.shape
    heads = band.shape[0]
    full = lambda a: pl.BlockSpec(a.shape, lambda r, l: (0,) * a.ndim)
    per_row = lambda *s: pl.BlockSpec((1,) + s, lambda r, l: (r,) + (0,) * len(s))
    tall = jax.ShapeDtypeStruct((rows, seq, width), BF16)
    outs = [tall] * 5 + [
        jax.ShapeDtypeStruct((rows, width, seq), BF16),
        jax.ShapeDtypeStruct((rows, heads, seq), F32),
        jax.ShapeDtypeStruct((rows, seq, width), F32),
        tall,
    ]
    return pl.pallas_call(
        attn_fwd_kernel,
        grid_spec=pltpu.PrefetchScalarGridSpec(
            num_scalar_prefetch=1,
            grid=(rows,),
            in_specs=[per_row(seq, width), full(gain1), full(gain2), full(wq), full(wk), full(wv), full(wo), full(band)],
            out_specs=[per_row(seq, width)] * 5 + [per_row(width, seq), per_row(heads, seq), per_row(seq, width), per_row(seq, width)],
            scratch_shapes=[
                pltpu.VMEM((seq, seq), F32),
                pltpu.VMEM((2, seq, seq), F32),
                pltpu.VMEM((2, seq, seq), BF16),
            ],
        ),
        out_shape=outs,
        compiler_params=params(),
        name="attn_fwd",
    )(lengths, tokens, gain1, gain2, wq, wk, wv, wo, band)


GELU_C = float(np.sqrt(2.0 / np.pi))


def gelu_pair(v):
    v2 = v * v
    t = jnp.tanh(GELU_C * v * (1.0 + 0.044715 * v2))
    half = 0.5 * (1.0 + t)
    slope = half + (0.5 * GELU_C) * v * (1.0 - t * t) * (1.0 + (3 * 0.044715) * v2)
    return v * half, slope


def place(core, mine, other, keep, send, sems):
    return [
        (core == 0, [pltpu.make_async_copy(mine, keep, sems.at[0]), pltpu.make_async_copy(other, send, sems.at[1])]),
        (core != 0, [pltpu.make_async_copy(mine, send, sems.at[0]), pltpu.make_async_copy(other, keep, sems.at[1])]),
    ]


def start_all(cases):
    for condition, copies in cases:

        @pl.when(condition)
        def _():
            for copy in copies:
                copy.start()


def wait_all(cases):
    for condition, copies in cases:

        @pl.when(condition)
        def _():
            for copy in copies:
                copy.wait()


def ffn_kernel(first, steps, core_ref, h2_ref, dy_ref, win_ref, wout_ref, *refs):
    if first:
        keep_ref, send_ref, mix_ref, dtwo_ref, h2T_ref, gin_ref, gout_ref, sems = refs
    else:
        mix0_ref, dtwo0_ref, keep_ref, send_ref, mix_ref, dtwo_ref, h2T_ref, gin_ref, gout_ref, sems = refs
    step = pl.program_id(0)
    h2, dy = h2_ref[...], dy_ref[...]
    width = h2.shape[1]
    sub = win_ref.shape[1]
    size = gin_ref.shape[1]

    def moves(at):
        rows = pl.ds(pl.multiple_of(at * size, size), size)
        return place(core_ref[0], gin_ref.at[at], gout_ref.at[at], keep_ref.at[rows, :], send_ref.at[rows, :], sems.at[at])

    @pl.when(step == 0)
    def _():
        h2T_ref[...] = h2_ref[...].T

    pre = dot(h2, win_ref[...])
    act, slope = gelu_pair(pre)
    act = act.astype(BF16)
    gout = dot(act, dy, TN)
    for j in range(width // 256):
        gout_ref[step, j * sub : (j + 1) * sub, :] = gout[:, j * 256 : (j + 1) * 256]
    dpre = (dot(dy, wout_ref[...], NT) * slope).astype(BF16)
    gin = dot(h2T_ref[...], dpre)
    for j in range(sub // 256):
        gin_ref[step, j * width : (j + 1) * width, :] = gin[:, j * 256 : (j + 1) * 256]
    start_all(moves(step))
    mix = dot(act, wout_ref[...])
    dtwo = dot(dpre, win_ref[...], NT)

    @pl.when(step == 0)
    def _():
        mix_ref[...] = mix if first else mix0_ref[...] + mix
        dtwo_ref[...] = dtwo if first else dtwo0_ref[...] + dtwo

    @pl.when(step > 0)
    def _():
        mix_ref[...] += mix
        dtwo_ref[...] += dtwo

    @pl.when(step == steps - 1)
    def _():
        for at in range(steps):
            wait_all(moves(at))


def ffn_chunk(core, h2, dy, w_in, w_out, start, size, sub, acc=None):
    toks, width = h2.shape
    first = acc is None
    base = start // sub
    steps = size // sub
    piece = width * (sub // 256)
    full = lambda a: pl.BlockSpec(a.shape, lambda s, c: (0,) * a.ndim)
    in_specs = [full(h2), full(dy), pl.BlockSpec((width, sub), lambda s, c: (0, base + s)), pl.BlockSpec((sub, width), lambda s, c: (base + s, 0))]
    args = [core, h2, dy, w_in, w_out]
    aliases = {}
    if not first:
        in_specs += [full(acc[0]), full(acc[1])]
        args += list(acc)
        aliases = {5: 2, 6: 3}
    return pl.pallas_call(
        functools.partial(ffn_kernel, first, steps),
        grid_spec=pltpu.PrefetchScalarGridSpec(
            num_scalar_prefetch=1,
            grid=(steps,),
            in_specs=in_specs,
            out_specs=[
                pl.BlockSpec(memory_space=pl.ANY),
                pl.BlockSpec(memory_space=pl.ANY),
                pl.BlockSpec((toks, width), lambda s, c: (0, 0)),
                pl.BlockSpec((toks, width), lambda s, c: (0, 0)),
            ],
            scratch_shapes=[
                pltpu.VMEM((width, toks), BF16),
                pltpu.VMEM((steps, piece, 256), F32),
                pltpu.VMEM((steps, piece, 256), F32),
                pltpu.SemaphoreType.DMA((steps, 2)),
            ],
        ),
        out_shape=[jax.ShapeDtypeStruct((steps * piece, 256), F32)] * 2 + [jax.ShapeDtypeStruct((toks, width), F32)] * 2,
        input_output_aliases=aliases,
        compiler_params=params(),
        name="ffn",
    )(*args)


def resid_kernel(len_ref, x1_ref, mix_ref, dtwo_ref, dy_ref, gain_ref, attT_ref, wo_ref,
                 mixed_ref, dres_ref, datt_ref, gwo_ref, ggain_ref):
    step = pl.program_id(0)
    x1, dtwo = x1_ref[0], dtwo_ref[0]
    mixed_ref[0] = (x1 + mix_ref[0]).astype(BF16)
    s = norm_scale(x1)
    g = gain_ref[...].astype(F32) * dtwo
    dres = dy_ref[0].astype(F32) + s * g - x1 * (s * s * s * jnp.mean(x1 * g, axis=-1, keepdims=True))
    dres_ref[0] = dres
    dbranch = dres.astype(BF16)
    ggain = jnp.sum(dtwo * x1 * s, axis=0, keepdims=True)
    gwo = dot(attT_ref[0], dbranch)
    stripes = gwo_ref.shape[0]
    seq = x1.shape[0]
    seg = segments_along(len_ref, step, (seq, TILE), 0)[:, :1]
    datt = dot(dbranch, wo_ref[...], NT)
    datt_ref[0] = jnp.where(seg < len_ref.shape[1] - 1, datt, 0.0).astype(BF16)

    @pl.when(step == 0)
    def _():
        ggain_ref[...] = ggain
        for j in range(stripes):
            gwo_ref[j] = gwo[:, j * 256 : (j + 1) * 256]

    @pl.when(step > 0)
    def _():
        ggain_ref[...] += ggain
        for j in range(stripes):
            gwo_ref[j] += gwo[:, j * 256 : (j + 1) * 256]


def resid_bwd(lengths, x1, mix, dtwo, dy, gain, attT, wo):
    rows, seq, width = x1.shape
    full = lambda a: pl.BlockSpec(a.shape, lambda r, l: (0,) * a.ndim)
    tall = pl.BlockSpec((1, seq, width), lambda r, l: (r, 0, 0))
    return pl.pallas_call(
        resid_kernel,
        grid_spec=pltpu.PrefetchScalarGridSpec(
            num_scalar_prefetch=1,
            grid=(rows,),
            in_specs=[tall, tall, tall, tall, full(gain), pl.BlockSpec((1, width, seq), lambda r, l: (r, 0, 0)), full(wo)],
            out_specs=[tall, tall, tall, pl.BlockSpec((width // 256, width, 256), lambda r, l: (0, 0, 0)), pl.BlockSpec((1, width), lambda r, l: (0, 0))],
        ),
        out_shape=[
            jax.ShapeDtypeStruct((rows, seq, width), BF16),
            jax.ShapeDtypeStruct((rows, seq, width), F32),
            jax.ShapeDtypeStruct((rows, seq, width), BF16),
            jax.ShapeDtypeStruct((width // 256, width, 256), F32),
            jax.ShapeDtypeStruct((1, width), F32),
        ],
        compiler_params=params(),
        name="resid_bwd",
    )(lengths, x1, mix, dtwo, dy, gain, attT, wo)


def diagonal_sums(x):
    depth, lanes = x.shape
    total = x[0:8]
    for g in range(8, depth, 8):
        total = total + pltpu.roll(x[g : g + 8], lanes - g, 1)
    at = lax.broadcasted_iota(jnp.int32, (8, lanes), 0)
    for bit in (1, 2, 4):
        total = jnp.where((at & bit) != 0, pltpu.roll(total, lanes - bit, 1), total)
    return jnp.sum(total, axis=0, keepdims=True)


def attn_bwd_kernel(len_ref, q_ref, k_ref, v_ref, do_ref, lse_ref, band_ref,
                    dq_ref, dk_ref, dv_ref, diag_ref,
                    mask_ref, p_ref, pl_ref, dp_ref, ds_ref, near_ref, far_ref):
    pair, row = pl.program_id(0), pl.program_id(1)
    seq = q_ref.shape[1]
    head = TILE // 2
    count = seq // TILE
    fill_mask(len_ref, row, mask_ref, len_ref.shape[1] - 1)
    low_half = lax.broadcasted_iota(jnp.int32, (1, TILE), 1) < head
    qp, kp, vp, dop = q_ref[0], k_ref[0], v_ref[0], do_ref[0]
    kT = kp.T

    @pl.when(row == 0)
    def _():
        near_ref[...] = jnp.zeros_like(near_ref)
        far_ref[...] = jnp.zeros_like(far_ref)

    dqT, dk, dv = [], None, None
    for a in range(2):
        own = low_half if a == 0 else ~low_half
        qm = jnp.where(own, qp, jnp.zeros_like(qp))
        dom = jnp.where(own, dop, jnp.zeros_like(dop))
        vector = band_ref[0, a : a + 1, :]
        band = band_of(vector)
        lse = lse_ref[0, 0, a : a + 1, :]
        delta = jnp.zeros((1, seq), F32)
        for ki in range(count):
            rows = slice(ki * TILE, (ki + 1) * TILE)
            s = dot(kp[rows], qm, NT) + bias_row(band, vector, ki, count) + mask_ref[rows, :]
            prob = jnp.exp(s - lse)
            dp = dot(vp[rows], dom, NT)
            delta = delta + jnp.sum(prob * dp, axis=0, keepdims=True)
            p_ref[a, rows, :] = prob
            pl_ref[a, rows, :] = prob.astype(BF16)
            dp_ref[a, rows, :] = dp
        for ki in range(count):
            rows = slice(ki * TILE, (ki + 1) * TILE)
            ds = p_ref[a, rows, :] * (dp_ref[a, rows, :] - delta)
            ds_ref[a, rows, :] = ds.astype(BF16)
            for qi in range(count):
                tile = ds[:, qi * TILE : (qi + 1) * TILE]
                step = ki - qi
                if abs(step) <= 1:
                    at = (0 if step == 0 else 1 if step == -1 else 3) * TILE
                    near_ref[a, :, at : at + TILE] += tile
                else:
                    at = 0 if step < 0 else TILE
                    far_ref[a, :, at : at + TILE] += tile
        dva = dot(pl_ref[a], dom)
        dka = dot(ds_ref[a], qm)
        dv = dva if dv is None else dv + dva
        dk = dka if dk is None else dk + dka
        dqT.append(dot(kT[a * head : (a + 1) * head], ds_ref[a]))
    dv_ref[0] = dv.astype(BF16)
    dk_ref[0] = dk.astype(BF16)
    dq_ref[0] = jnp.concatenate(dqT, axis=0).T.astype(BF16)

    @pl.when(row == pl.num_programs(1) - 1)
    def _():
        for a in range(2):
            diag_ref[0, a : a + 1, : 4 * TILE] = diagonal_sums(near_ref[a])
            diag_ref[0, a : a + 1, 4 * TILE :] = jnp.sum(far_ref[a], axis=0, keepdims=True)


def attn_bwd(lengths, q, k, v, do, lse, band):
    rows, seq, width = q.shape
    pairs = width // TILE
    lse = lse.reshape(rows, pairs, 2, seq)
    band = band.reshape(pairs, 2, band.shape[1])
    tall = pl.BlockSpec((1, seq, TILE), lambda p, r, l: (r, 0, p))
    out = jax.ShapeDtypeStruct((rows, seq, width), BF16)
    return pl.pallas_call(
        attn_bwd_kernel,
        grid_spec=pltpu.PrefetchScalarGridSpec(
            num_scalar_prefetch=1,
            grid=(pairs, rows),
            in_specs=[tall] * 4 + [pl.BlockSpec((1, 1, 2, seq), lambda p, r, l: (r, p, 0, 0)), pl.BlockSpec((1, 2, 4 * TILE), lambda p, r, l: (p, 0, 0))],
            out_specs=[tall] * 3 + [pl.BlockSpec((1, 2, 6 * TILE), lambda p, r, l: (p, 0, 0))],
            scratch_shapes=[
                pltpu.VMEM((seq, seq), F32),
                pltpu.VMEM((2, seq, seq), F32),
                pltpu.VMEM((2, seq, seq), BF16),
                pltpu.VMEM((2, seq, seq), F32),
                pltpu.VMEM((2, seq, seq), BF16),
                pltpu.VMEM((2, TILE, 4 * TILE), F32),
                pltpu.VMEM((2, TILE, 2 * TILE), F32),
            ],
        ),
        out_shape=[out] * 3 + [jax.ShapeDtypeStruct((pairs, 2, 6 * TILE), F32)],
        compiler_params=params(),
        name="attn_bwd",
    )(lengths, q, k, v, do, lse, band)


def wgrad_kernel(core_ref, h1_ref, dq_ref, dk_ref, dv_ref, gwo_ref, keep_ref, send_ref, h1T_ref, g_ref, sems):
    width = h1_ref.shape[1]
    n = width // 256
    h1T_ref[...] = h1_ref[...].T
    for i, d in enumerate((dq_ref, dk_ref, dv_ref)):
        g = dot(h1T_ref[...], d[...])
        for j in range(n):
            at = (i * n + j) * width
            g_ref[at : at + width, :] = g[:, j * 256 : (j + 1) * 256]
    for j in range(n):
        at = (3 * n + j) * width
        g_ref[at : at + width, :] = gwo_ref[j]
    half = keep_ref.shape[0]
    moves = place(core_ref[0], g_ref.at[0:half, :], g_ref.at[half : 2 * half, :], keep_ref, send_ref, sems)
    start_all(moves)
    wait_all(moves)


def wgrads(core, h1, ds, gwo):
    toks, width = h1.shape
    n = width // 256
    whole = pl.BlockSpec(memory_space=pltpu.VMEM)
    return pl.pallas_call(
        wgrad_kernel,
        in_specs=[pl.BlockSpec(memory_space=pltpu.SMEM)] + [whole] * 5,
        out_specs=[pl.BlockSpec(memory_space=pl.ANY)] * 2,
        out_shape=[jax.ShapeDtypeStruct((2 * n * width, 256), F32)] * 2,
        scratch_shapes=[pltpu.VMEM((width, toks), BF16), pltpu.VMEM((4 * n * width, 256), F32), pltpu.SemaphoreType.DMA((2,))],
        compiler_params=params(),
        name="attn_wgrad",
    )(core, h1, *ds, gwo)


def tokgrad_kernel(tok_ref, dres_ref, gain_ref, dq_ref, dk_ref, dv_ref, wq_ref, wk_ref, wv_ref, out_ref, ggain_ref):
    step = pl.program_id(0)
    done = dot(dq_ref[...], wq_ref[...], NT) + dot(dk_ref[...], wk_ref[...], NT) + dot(dv_ref[...], wv_ref[...], NT)
    tok = tok_ref[...].astype(F32)
    s = norm_scale(tok)
    g = gain_ref[...].astype(F32) * done
    out_ref[...] = (dres_ref[...] + s * g - tok * (s * s * s * jnp.mean(tok * g, axis=-1, keepdims=True))).astype(BF16)
    ggain = jnp.sum(done * tok * s, axis=0, keepdims=True)

    @pl.when(step == 0)
    def _():
        ggain_ref[...] = ggain

    @pl.when(step > 0)
    def _():
        ggain_ref[...] += ggain


def tokgrad(tok, dres, gain, dq, dk, dv, wq, wk, wv, block=512):
    toks, width = tok.shape
    full = lambda a: pl.BlockSpec(a.shape, lambda s: (0,) * a.ndim)
    tall = pl.BlockSpec((block, width), lambda s: (s, 0))
    return pl.pallas_call(
        tokgrad_kernel,
        grid=(toks // block,),
        in_specs=[tall, tall, full(gain), tall, tall, tall, full(wq), full(wk), full(wv)],
        out_specs=[tall, pl.BlockSpec((1, width), lambda s: (0, 0))],
        out_shape=[jax.ShapeDtypeStruct((toks, width), BF16), jax.ShapeDtypeStruct((1, width), F32)],
        compiler_params=params(),
        name="tokgrad",
    )(tok, dres, gain, dq, dk, dv, wq, wk, wv)


def bit_orders(size):
    bits = list(range(size.bit_length() - 1))
    swapped = bits[1::-1] + bits[2:]
    return list(zip(bits, swapped))


def exchange(x, size, cores, bits):
    moves = [
        (r * cores + c, (r ^ (1 << bits[c % 2])) * cores + c) for r in range(size) for c in range(cores)
    ]
    return lax.ppermute(x, ("rows", "blk"), moves)


def swap_cores(x):
    return lax.ppermute(x, "blk", [(0, 1), (1, 0)])


def my_bit(bits):
    r, c = lax.axis_index("rows"), lax.axis_index("blk")
    return jnp.where(c % 2 == 0, (r >> bits[0]) & 1, (r >> bits[1]) & 1)


def reduce_scatter(keep, send, size):
    got = swap_cores(send)
    for bits in bit_orders(size):
        bit = my_bit(bits)
        half = keep.shape[0] // 2
        part = lambda a, at: lax.dynamic_slice_in_dim(a, at * half, half, 0)
        out = part(keep, 1 - bit) + part(got, 1 - bit)
        coming = exchange(out, size, 2, bits)
        keep = part(keep, bit) + part(got, bit)
        got = coming
    return keep + got


def all_gather(piece, size):
    orders = list(reversed(bit_orders(size)))
    for bits in orders:
        got = exchange(piece, size, 2, bits)
        bit = my_bit(bits)
        if bits is not orders[-1]:
            wide = jnp.concatenate([piece, piece], axis=0)
            piece = lax.dynamic_update_slice_in_dim(wide, got, (1 - bit) * got.shape[0], 0)
    return piece, got


def assemble_kernel(place_of, n_outs, where_ref, *refs):
    sources, outs, sems = refs[:4], refs[-1 - n_outs : -1], refs[-1]
    core, bit, far_bit = where_ref[0], where_ref[1], where_ref[2]
    owners = (core, core, 1 - core, 1 - core)
    halves = (bit, 1 - bit, far_bit, 1 - far_bit)
    for action in ("start", "wait"):
        for n, source in enumerate(sources):
            for owner in range(2):
                for half in range(2):

                    @pl.when((owners[n] == owner) & (halves[n] == half))
                    def _():
                        for j in range(source.shape[0] // 256):
                            out, row, col = place_of(owner, half, j)
                            copy = pltpu.make_async_copy(
                                source.at[j * 256 : (j + 1) * 256, :],
                                outs[out].at[row : row + 256, col : col + 256],
                                sems.at[n, j],
                            )
                            getattr(copy, action)()


def assemble(place_of, shapes, where, sources, earlier=()):
    any_place = pl.BlockSpec(memory_space=pl.ANY)
    count = sources[0].shape[0] // 256
    return pl.pallas_call(
        functools.partial(assemble_kernel, place_of, len(shapes)),
        in_specs=[pl.BlockSpec(memory_space=pltpu.SMEM)] + [any_place] * (4 + len(earlier)),
        out_specs=[any_place] * len(shapes),
        out_shape=[jax.ShapeDtypeStruct(s, F32) for s in shapes],
        scratch_shapes=[pltpu.SemaphoreType.DMA((4, count))],
        input_output_aliases={5 + i: i for i in range(len(earlier))},
        compiler_params=params(),
        name="assemble",
    )(where, *sources, *earlier)


def ffn_place(width, start, sub, count, owner, half, j):
    i = half * count + j
    if owner == 0:
        per = width // 256
        return 0, (i % per) * 256, start + (i // per) * 256
    per = sub // 256
    block = i // per
    stripe, step = block % (width // 256), block // (width // 256)
    return 1, start + step * sub + (i % per) * 256, stripe * 256


def attn_place(width, owner, half, j):
    per = width // 256
    return 2 * owner + half, (j % per) * 256, (j // per) * 256


def on_device(tokens, lengths, attn_gain, wq, wk, wv, wo, table, ffn_gain, w_in, w_out, out_grad, *, size, chunks=2, sub=512):
    rows, seq, width = tokens.shape
    buckets, heads = table.shape
    ff = w_in.shape[1]
    core = lax.axis_index("blk")
    core_arg = core.astype(jnp.int32).reshape(1)
    last = bit_orders(size)[0]
    row_id = lax.axis_index("rows")
    ends = [(row_id >> b) & 1 for b in last]
    where = jnp.stack([core, jnp.where(core == 0, ends[0], ends[1]), jnp.where(core == 0, ends[1], ends[0])]).astype(jnp.int32)
    lane_buckets = band_buckets(buckets)
    onehot = np.arange(buckets)[:, None] == lane_buckets[None, :]
    band = jnp.einsum("bh,bm->hm", table, jnp.asarray(onehot, BF16), preferred_element_type=F32)
    gain1, gain2 = attn_gain.reshape(1, width), ffn_gain.reshape(1, width)
    flat = lambda a: a.reshape(rows * seq, width)
    tall = lambda a: a.reshape(rows, seq, width)

    def total(keep, send):
        piece, got = all_gather(reduce_scatter(keep, send, size), size)
        return piece, got, swap_cores(piece), swap_cores(got)

    h1, q, k, v, att, attT, lse, x1, h2 = attn_fwd(tokens, lengths, gain1, gain2, wq, wk, wv, wo, band)
    part = ff // chunks
    acc, ffn_grads = None, ()
    for c in range(chunks):
        keep, send, mix, dtwo = ffn_chunk(core_arg, flat(h2), flat(out_grad), w_in, w_out, c * part, part, sub, acc)
        acc = (mix, dtwo)
        sources = total(keep, send)
        place_of = functools.partial(ffn_place, width, c * part, sub, sources[0].shape[0] // 256)
        ffn_grads = assemble(place_of, [w_in.shape, w_out.shape], where, sources, ffn_grads)
    mixed, dres, datt, gwo, ggain2 = resid_bwd(lengths, x1, tall(mix), tall(dtwo), out_grad, gain2, attT, wo)
    dq, dk, dv, diag = attn_bwd(lengths, q, k, v, datt, lse, band)
    sources = total(*wgrads(core_arg, flat(h1), [flat(dq), flat(dk), flat(dv)], gwo))
    attn_grads = assemble(functools.partial(attn_place, width), [wq.shape] * 4, where, sources)
    tgrad, ggain1 = tokgrad(flat(tokens), flat(dres), gain1, flat(dq), flat(dk), flat(dv), wq, wk, wv)
    far = bucket_of(np.array([-2 * TILE] * TILE + [2 * TILE] * TILE), buckets)
    spread = (np.concatenate([lane_buckets, far])[:, None] == np.arange(buckets)[None, :]).astype(np.float32)
    gtable = jnp.einsum("hm,mb->bh", diag.reshape(heads, 6 * TILE), jnp.asarray(spread), precision=lax.Precision.HIGHEST)
    ggain1, ggain2, gtable = lax.psum((ggain1, ggain2, gtable), ("rows", "blk"))
    return (mixed, tall(tgrad), ggain1[0], *attn_grads, gtable, ggain2[0], *ffn_grads)


def solution(mesh):
    split = P(("rows", "blk"))
    return jax.shard_map(
        functools.partial(on_device, size=mesh.shape["rows"]),
        mesh=mesh,
        in_specs=(split, split) + (P(),) * 9 + (split,),
        out_specs=(split, split) + (P(),) * 9,
        check_vma=False,
    )
```

time: 795 us -> 1430 us (1.80)
  Pallas kernels: 0 us -> 1020 us
  matrix products: 216 us -> 1.8 us
  local copies, waits for them, and re-layouts: 105 us -> 6.77 us
  waiting for transfers between devices: 344 us -> 254 us
  starting transfers between devices: 0.04 us -> 61.9 us
  other arithmetic: 63.2 us -> 39.1 us
    pallas_call x0 -> x10, Pallas kernels: none -> 1020 us  [the longest x3 864 us: assemble(): pl.pallas_call(functools.partial(assemble_kernel, place_of, len(shapes)),...]
    psum x1 -> x0, waiting for transfers between devices: 344 us -> none  [on_device(): lax.psum((grad_gain_one, grad_w_query, grad_w_key, grad_w_value, grad_w_o...]
    ppermute x0 -> x33, waiting for transfers between devices: none -> 254 us  [the longest x24 254 us: exchange(): return lax.ppermute(x, ('rows', 'blk'), moves)]
    dot_general x26 -> x2, matrix products: 216 us -> 1.8 us  [the longest x1 1.48 us: on_device(): jnp.einsum('bh,bm->hm', table, jnp.asarray(onehot, BF16), preferred_eleme...]
    ppermute x0 -> x33, starting transfers between devices: none -> 61.9 us  [the longest x24 43.3 us: exchange(): return lax.ppermute(x, ('rows', 'blk'), moves)]
    eq x1 -> x0, local copies, waits for them, and re-layouts: 46.4 us -> none  [on_device(): buckets[None] == jnp.arange(bucket_count, dtype=jnp.int32)[:, None, None]]
    reduce_sum x5 -> x0, other arithmetic: 41.5 us -> none  [the longest x1 27 us: on_device(): jnp.sum(score_gradient, axis=0)]
    add x3 -> x15, other arithmetic: 1.96 us -> 35.3 us  [the longest x9 32.2 us: reduce_scatter(): keep = part(keep, bit) + part(got, bit)]
  transfers between devices with their start and end apart: 1 -> 33, of which waited for: 1 -> 20; matrix products, arithmetic and copies ran while one was open for 7% -> 3% of each run, Pallas kernels for 0% -> 48%
where the time goes in v1:
time: 1430 us; the launch traced here: 1420 us
  Pallas kernels  1020 us (71%)
  waiting for transfers between devices  254 us (18%)
  starting transfers between devices  61.9 us (4%)
  blocking collectives  39.2 us (3%)
  other arithmetic  39.1 us (3%)
    pallas_call x3, Pallas kernels, assemble(): pl.pallas_call(functools.partial(assemble_kernel, place_of, len(shapes)),...  864 us
    ppermute x24, waiting for transfers between devices, exchange(): return lax.ppermute(x, ('rows', 'blk'), moves)  254 us
    pallas_call x2, Pallas kernels, ffn_chunk(): pl.pallas_call(functools.partial(ffn_kernel, first, steps), grid_spec=plt...  52 us
    ppermute x24, starting transfers between devices, exchange(): return lax.ppermute(x, ('rows', 'blk'), moves)  43.3 us
    pallas_call x1, Pallas kernels, attn_bwd(): pl.pallas_call(attn_bwd_kernel, grid_spec=pltpu.PrefetchScalarGridSpec(nu...  39.9 us
    psum x1, blocking collectives, on_device(): ggain1, ggain2, gtable = lax.psum((ggain1, ggain2, gtable), ('rows', 'blk'))  39.2 us
    add x9, other arithmetic, reduce_scatter(): keep = part(keep, bit) + part(got, bit)  32.2 us
    pallas_call x1, Pallas kernels, attn_fwd(): pl.pallas_call(attn_fwd_kernel, grid_spec=pltpu.PrefetchScalarGridSpec(nu...  28.6 us
  transfers between devices with their start and end apart: 33, of which 20 were waited for; matrix products, arithmetic and copies ran while one was open for 3% of the time, Pallas kernels for 48%

profile of v1, /device:TPU:0, one launch (start us, length us, event | category | flops | bytes accessed | tf_op | source)
XLA Modules:
  0.0 1421.7 jit_solution(16259427569380852888)
XLA Ops:
  4.7 28.6 %attn_fwd.1 = (bf16[2,512,768]{2,1,0:T(8,128)(2,1)}, bf16[2,512,768]{2,1,0:T(8,128)(2,1)}, bf16[2,512,768]{2,1,0:T(8,128)(2,1)}, bf16[2,512,768]{2,1,0:T(8,128)(...) custom-call(s32[2,8]{1,0:T(2,128)} %len_ref.5, ...), custom_call_target="tpu_custom_call" | custom-call | tf_op jit(solution)/shard_map/attn_fwd/pallas_call | solution.py:161
  33.3 24.9 %ffn.2 = (f32[4608,256]{1,0:T(8,128)}, f32[4608,256]{1,0:T(8,128)}, f32[1024,768]{1,0:T(8,128)}, f32[1024,768]{1,0:T(8,128)}) custom-call(s32[1]{0:T(128)} %bitcast.1.core_ref, bf16[1024,768]{1,0:T(8,128)(2,1)} %bitcast.32, bf16[1024,768]{1,0:T(8,128)(2,1)} %bitcast.21, bf16[768,3072]{1,0:T(8,128)(2,1)} %win_ref.3, bf16[3072,768]{1,0:T(8,128)(2,1)} %wout_ref.3), custom_call_target="tpu_custom_call" | custom-call | tf_op jit(solution)/shard_map/ffn/pallas_call | solution.py:279
  60.0 27.1 %ffn.3 = (f32[4608,256]{1,0:T(8,128)}, f32[4608,256]{1,0:T(8,128)}, f32[1024,768]{1,0:T(8,128)}, f32[1024,768]{1,0:T(8,128)}) custom-call(s32[1]{0:T(128)} %bitcast.1.core_ref, bf16[1024,768]{1,0:T(8,128)(2,1)} %bitcast.33, bf16[1024,768]{1,0:T(8,128)(2,1)} %bitcast.22, bf16[768,3072]{1,0:T(8,128)(2,1)} %win_ref.3, ...), custom_call_target="tpu_custom_call", output_to_operand_aliasing={{2}: (5, {}), {3}: (6, {})} | custom-call | tf_op jit(solution)/shard_map/ffn/pallas_call | solution.py:279
  87.2 11.5 resid_bwd.1
  98.7 39.9 %attn_bwd.1 = (bf16[2,512,768]{2,1,0:T(8,128)(2,1)}, bf16[2,512,768]{2,1,0:T(8,128)(2,1)}, bf16[2,512,768]{2,1,0:T(8,128)(2,1)}, f32[6,2,768]{2,1,0:T(2,128)}) custom-call(s32[2,8]{1,0:T(2,128)} %len_ref.5, bf16[2,512,768]{2,1,0:T(8,128)(2,1)} %get-tuple-element.57.q_ref, bf16[2,512,768]{2,1,0:T(8,128)(2,1)} %get-tuple-element.58.k_ref, ...), custom_call_target="tpu_custom_call" | custom-call | tf_op jit(solution)/shard_map/attn_bwd/pallas_call | solution.py:442
  138.6 11.1 attn_wgrad.1
  172.5 13.5 collective-permute-done.23
  191.2 32.7 %collective-permute-done.1 = f32[2304,256]{1,0:T(8,128)} collective-permute-done((f32[2304,256]{1,0:T(8,128)}, f32[2304,256]{1,0:T(8,128)}, u32[]{:S(2)}, u32[]{:S(2)}) %collective-permute-start.1) | collective-permute-done | bytes 2359328 | tf_op jit(solution)/shard_map/ppermute | solution.py:541
  229.0 32.8 %collective-permute-done.12 = f32[2304,256]{1,0:T(8,128)} collective-permute-done((f32[2304,256]{1,0:T(8,128)}, f32[2304,256]{1,0:T(8,128)}, u32[]{:S(2)}, u32[]{:S(2)}) %collective-permute-start.12) | collective-permute-done | bytes 2359328 | tf_op jit(solution)/shard_map/ppermute | solution.py:541
  288.4 16.4 %collective-permute-done.3 = f32[576,256]{1,0:T(8,128)} collective-permute-done((f32[576,256]{1,0:T(8,128)}, f32[576,256]{1,0:T(8,128)}, u32[]{:S(2)}, u32[]{:S(2)}) %collective-permute-start.3) | collective-permute-done | bytes 589856 | tf_op jit(solution)/shard_map/ppermute | solution.py:541
  307.5 12.6 collective-permute-done.14
  324.3 15.7 %collective-permute-done.4 = f32[288,256]{1,0:T(8,128)S(1)} collective-permute-done((f32[288,256]{1,0:T(8,128)S(1)}, f32[288,256]{1,0:T(8,128)S(1)}, u32[]{:S(2)}, u32[]{:S(2)}) %collective-permute-start.4) | collective-permute-done | bytes 294944 | tf_op jit(solution)/shard_map/ppermute | solution.py:541
  341.1 8.3 collective-permute-done.15
  349.7 12.4 collective-permute-done.27
  376.6 10.9 collective-permute-done.28
  390.9 9.2 collective-permute-done.6
  420.3 19.2 %collective-permute-done.18 = f32[1152,256]{1,0:T(8,128)S(1)} collective-permute-done((f32[1152,256]{1,0:T(8,128)S(1)}, f32[1152,256]{1,0:T(8,128)S(1)}, u32[]{:S(2)}, u32[]{:S(2)}) %collective-permute-start.18) | collective-permute-done | bytes 1179680 | tf_op jit(solution)/shard_map/ppermute | solution.py:541
  455.9 19.4 %collective-permute-done.30.refs_1_ = f32[2304,256]{1,0:T(8,128)} collective-permute-done((f32[2304,256]{1,0:T(8,128)S(1)}, f32[2304,256]{1,0:T(8,128)}, u32[]{:S(2)}, u32[]{:S(2)}) %collective-permute-start.30) | collective-permute-done | bytes 2359328 | tf_op jit(solution)/shard_map/ppermute | solution.py:541
  482.6 18.0 %collective-permute-done.19.refs_1_ = f32[2304,256]{1,0:T(8,128)} collective-permute-done((f32[2304,256]{1,0:T(8,128)}, f32[2304,256]{1,0:T(8,128)}, u32[]{:S(2)}, u32[]{:S(2)}) %collective-permute-start.19) | collective-permute-done | bytes 2359328 | tf_op jit(solution)/shard_map/ppermute | solution.py:541
  506.2 10.1 tokgrad.1
  517.4 39.2 %all-reduce = (f32[768]{0:T(1024)}, f32[32,12]{0,1:T(8,128)}, f32[768]{0:T(1024)}) all-reduce(f32[768]{0:T(1024)S(1)} %reduce, f32[32,12]{0,1:T(8,128)S(1)} %fusion, f32[768]{0:T(1024)S(1)} %reduce.1), channel_id=1, replica_groups=mesh['rows'=16,'blk'=2] {'rows','blk'}, use_global_device_ids=true, to_apply=%region_0.1 | all-reduce | flops 1920 | bytes 15360 | tf_op jit(solution)/shard_map/psum | solution.py:668
  557.2 288.0 %assemble.3 = (f32[768,768]{1,0:T(8,128)}, f32[768,768]{1,0:T(8,128)}, f32[768,768]{1,0:T(8,128)}, f32[768,768]{1,0:T(8,128)}) custom-call(s32[3]{0:T(128)} %pad_add_fusion.where_ref, f32[2304,256]{1,0:T(8,128)} %copy-done.5, f32[2304,256]{1,0:T(8,128)} %collective-permute-done.8.refs_1_, f32[2304,256]{1,0:T(8,128)} %copy-done.7, ...), custom_call_target="tpu_custom_call" | custom-call | tf_op jit(solution)/shard_map/assemble/pallas_call | solution.py:602
  845.2 288.0 %assemble.4 = (f32[768,3072]{1,0:T(8,128)}, f32[3072,768]{1,0:T(8,128)}) custom-call(s32[3]{0:T(128)} %pad_add_fusion.where_ref, f32[2304,256]{1,0:T(8,128)} %copy-done.4, f32[2304,256]{1,0:T(8,128)} %collective-permute-done.30.refs_1_, f32[2304,256]{1,0:T(8,128)} %collective-permute-done.31.refs_2_, f32[2304,256]{1,0:T(8,128)} %collective-permute-done.32.refs_3_), custom_call_target="tpu_custom_call" | custom-call | tf_op jit(solution)/shard_map/assemble/pallas_call | solution.py:602
  1133.2 288.0 %assemble.5 = (f32[768,3072]{1,0:T(8,128)}, f32[3072,768]{1,0:T(8,128)}) custom-call(s32[3]{0:T(128)} %pad_add_fusion.where_ref, f32[2304,256]{1,0:T(8,128)} %constant_dynamic-update-slice_fusion.5.refs_0_, f32[2304,256]{1,0:T(8,128)} %collective-permute-done.19.refs_1_, ...), custom_call_target="tpu_custom_call", output_to_operand_aliasing={{0}: (5, {}), {1}: (6, {})} | custom-call | tf_op jit(solution)/shard_map/assemble/pallas_call | solution.py:602
  (133 shorter events, 142.7 us)
Async XLA Ops:
  58.2 92.1 %collective-permute-start.22 = (f32[4608,256]{1,0:T(8,128)}, f32[4608,256]{1,0:T(8,128)}, u32[]{:S(2)}, u32[]{:S(2)}) collective-permute-start(f32[4608,256]{1,0:T(8,128)} %get-tuple-element.80), channel_id=1, source_target_pairs={{0,1},{1,0},{2,3},{3,2},{4,5},{5,4},{6,7},{7,6},{8,9},{9,8},{10,11... | collective-permute-start | bytes 14155784 | tf_op jit(solution)/shard_map/ppermute | solution.py:545
  156.3 29.7 %collective-permute-start.23 = (f32[2304,256]{1,0:T(8,128)}, f32[2304,256]{1,0:T(8,128)}, u32[]{:S(2)}, u32[]{:S(2)}) collective-permute-start(f32[2304,256]{1,0:T(8,128)} %get-tuple-element.89), channel_id=1, source_target_pairs={{0,2},{1,5},{2,0},{3,7},{4,6},{5,1},{6,4},{7,3},{8,10},{9,13},{10,... | collective-permute-start | bytes 7077896 | tf_op jit(solution)/shard_map/ppermute | solution.py:541
  164.1 59.8 %collective-permute-start.1 = (f32[2304,256]{1,0:T(8,128)}, f32[2304,256]{1,0:T(8,128)}, u32[]{:S(2)}, u32[]{:S(2)}) collective-permute-start(f32[2304,256]{1,0:T(8,128)} %get-tuple-element.93), channel_id=1, source_target_pairs={{0,2},{1,5},{2,0},{3,7},{4,6},{5,1},{6,4},{7,3},{8,10},{9,13},{10,... | collective-permute-start | bytes 7077896 | tf_op jit(solution)/shard_map/ppermute | solution.py:541
  170.9 90.9 %collective-permute-start.12 = (f32[2304,256]{1,0:T(8,128)}, f32[2304,256]{1,0:T(8,128)}, u32[]{:S(2)}, u32[]{:S(2)}) collective-permute-start(f32[2304,256]{1,0:T(8,128)} %get-tuple-element.91), channel_id=1, source_target_pairs={{0,2},{1,5},{2,0},{3,7},{4,6},{5,1},{6,4},{7,3},{8,10},{9,13},{10,... | collective-permute-start | bytes 7077896 | tf_op jit(solution)/shard_map/ppermute | solution.py:541
  189.2 77.6 %collective-permute-start.24 = (f32[1152,256]{1,0:T(8,128)}, f32[1152,256]{1,0:T(8,128)}, u32[]{:S(2)}, u32[]{:S(2)}) collective-permute-start(f32[1152,256]{1,0:T(8,128)} %get-tuple-element.95), channel_id=1, source_target_pairs={{0,4},{1,3},{2,6},{3,1},{4,0},{5,7},{6,2},{7,5},{8,12},{9,11},{10,... | collective-permute-start | bytes 3538952 | tf_op jit(solution)/shard_map/ppermute | solution.py:541
  227.0 43.8 %collective-permute-start.2 = (f32[1152,256]{1,0:T(8,128)}, f32[1152,256]{1,0:T(8,128)}, u32[]{:S(2)}, u32[]{:S(2)}) collective-permute-start(f32[1152,256]{1,0:T(8,128)} %get-tuple-element.99), channel_id=1, source_target_pairs={{0,4},{1,3},{2,6},{3,1},{4,0},{5,7},{6,2},{7,5},{8,12},{9,11},{10,... | collective-permute-start | bytes 3538952 | tf_op jit(solution)/shard_map/ppermute | solution.py:541
  273.0 31.7 %collective-permute-start.3 = (f32[576,256]{1,0:T(8,128)}, f32[576,256]{1,0:T(8,128)}, u32[]{:S(2)}, u32[]{:S(2)}) collective-permute-start(f32[576,256]{1,0:T(8,128)} %get-tuple-element.105), channel_id=1, source_target_pairs={{0,8},{1,9},{2,10},{3,11},{4,12},{5,13},{6,14},{7,15},{8,0},{9,1},... | collective-permute-start | bytes 1769480 | tf_op jit(solution)/shard_map/ppermute | solution.py:541
  283.5 36.6 %collective-permute-start.14 = (f32[576,256]{1,0:T(8,128)}, f32[576,256]{1,0:T(8,128)S(1)}, u32[]{:S(2)}, u32[]{:S(2)}) collective-permute-start(f32[576,256]{1,0:T(8,128)} %get-tuple-element.103), channel_id=1, source_target_pairs={{0,8},{1,9},{2,10},{3,11},{4,12},{5,13},{6,14},{7,15},{8,0},{9,1},... | collective-permute-start | bytes 1769480 | tf_op jit(solution)/shard_map/ppermute | solution.py:541
  285.8 34.8 %collective-permute-start.26 = (f32[288,256]{1,0:T(8,128)S(1)}, f32[288,256]{1,0:T(8,128)}, u32[]{:S(2)}, u32[]{:S(2)}) collective-permute-start(f32[288,256]{1,0:T(8,128)S(1)} %dynamic-slice_add_fusion.18), channel_id=1, source_target_pairs={{0,16},{1,17},{2,18},{3,19},{4,20},{5,21},{6,22},{7,23},{8,24},{9,... | collective-permute-start | bytes 884744 | tf_op jit(solution)/shard_map/ppermute | solution.py:541
  305.8 34.2 %collective-permute-start.4 = (f32[288,256]{1,0:T(8,128)S(1)}, f32[288,256]{1,0:T(8,128)S(1)}, u32[]{:S(2)}, u32[]{:S(2)}) collective-permute-start(f32[288,256]{1,0:T(8,128)S(1)} %dynamic-slice_add_fusion.20), channel_id=1, source_target_pairs={{0,16},{1,17},{2,18},{3,19},{4,20},{5,21},{6,22},{7,23},{8,24},{9,... | collective-permute-start | bytes 884744 | tf_op jit(solution)/shard_map/ppermute | solution.py:541
  320.2 29.3 %collective-permute-start.15 = (f32[288,256]{1,0:T(8,128)S(1)}, f32[288,256]{1,0:T(8,128)S(1)}, u32[]{:S(2)}, u32[]{:S(2)}) collective-permute-start(f32[288,256]{1,0:T(8,128)S(1)} %dynamic-slice_add_fusion.19), channel_id=1, source_target_pairs={{0,16},{1,17},{2,18},{3,19},{4,20},{5,21},{6,22},{7,23},{8,24},{9,... | collective-permute-start | bytes 884744 | tf_op jit(solution)/shard_map/ppermute | solution.py:541
  321.6 40.5 %collective-permute-start.27 = (f32[288,256]{1,0:T(8,128)S(1)}, f32[288,256]{1,0:T(8,128)S(1)}, u32[]{:S(2)}, u32[]{:S(2)}) collective-permute-start(f32[288,256]{1,0:T(8,128)S(1)} %add_add_fusion), channel_id=1, source_target_pairs={{0,16},{1,17},{2,18},{3,19},{4,20},{5,21},{6,22},{7,23},{8,24},{9,... | collective-permute-start | bytes 884744 | tf_op jit(solution)/shard_map/ppermute | solution.py:541
  341.0 30.7 %collective-permute-start.5 = (f32[288,256]{1,0:T(8,128)S(1)}, f32[288,256]{1,0:T(8,128)S(1)}, u32[]{:S(2)}, u32[]{:S(2)}) collective-permute-start(f32[288,256]{1,0:T(8,128)S(1)} %add_add_fusion.2), channel_id=1, source_target_pairs={{0,16},{1,17},{2,18},{3,19},{4,20},{5,21},{6,22},{7,23},{8,24},{9,... | collective-permute-start | bytes 884744 | tf_op jit(solution)/shard_map/ppermute | solution.py:541
  376.4 34.6 %collective-permute-start.17 = (f32[576,256]{1,0:T(8,128)S(1)}, f32[576,256]{1,0:T(8,128)S(1)}, u32[]{:S(2)}, u32[]{:S(2)}) collective-permute-start(f32[576,256]{1,0:T(8,128)S(1)} %constant_dynamic-update-slice_fusion), channel_id=1, source_target_pairs={{0,8},{1,9},{2,10},{3,11},{4,12},{5,13},{6,14},{7,15},{8,0},{9,1},... | collective-permute-start | bytes 1769480 | tf_op jit(solution)/shard_map/ppermute | solution.py:541
  387.6 32.5 %collective-permute-start.29 = (f32[1152,256]{1,0:T(8,128)S(1)}, f32[1152,256]{1,0:T(8,128)S(1)}, u32[]{:S(2)}, u32[]{:S(2)}) collective-permute-start(f32[1152,256]{1,0:T(8,128)S(1)} %constant_dynamic-update-slice_fusion.7), channel_id=1, source_target_pairs={{0,4},{1,3},{2,6},{3,1},{4,0},{5,7},{6,2},{7,5},{8,12},{9,11},{10,... | collective-permute-start | bytes 3538952 | tf_op jit(solution)/shard_map/ppermute | solution.py:541
  417.9 63.3 %collective-permute-start.9 = (f32[2304,256]{1,0:T(8,128)S(1)}, f32[2304,256]{1,0:T(8,128)S(1)}, u32[]{:S(2)}, u32[]{:S(2)}) collective-permute-start(f32[2304,256]{1,0:T(8,128)S(1)} %constant_dynamic-update-slice_fusion.2.refs_0_), channel_id=1, source_target_pairs={{0,1},{1,0},{2,3},{3,2},{4,5},{5,4},{6,7},{7,6},{8,9},{9,8},{10,11... | collective-permute-start | bytes 7077896 | tf_op jit(solution)/shard_map/ppermute | solution.py:545
  417.9 32.1 %collective-permute-start.8 = (f32[2304,256]{1,0:T(8,128)S(1)}, f32[2304,256]{1,0:T(8,128)}, u32[]{:S(2)}, u32[]{:S(2)}) collective-permute-start(f32[2304,256]{1,0:T(8,128)S(1)} %constant_dynamic-update-slice_fusion.2.refs_0_), channel_id=1, source_target_pairs={{0,2},{1,5},{2,0},{3,7},{4,6},{5,1},{6,4},{7,3},{8,10},{9,13},{10,... | collective-permute-start | bytes 7077896 | tf_op jit(solution)/shard_map/ppermute | solution.py:541
  420.2 55.1 %collective-permute-start.30 = (f32[2304,256]{1,0:T(8,128)S(1)}, f32[2304,256]{1,0:T(8,128)}, u32[]{:S(2)}, u32[]{:S(2)}) collective-permute-start(f32[2304,256]{1,0:T(8,128)S(1)} %constant_dynamic-update-slice_fusion.1.refs_0_), channel_id=1, source_target_pairs={{0,2},{1,5},{2,0},{3,7},{4,6},{5,1},{6,4},{7,3},{8,10},{9,13},{10,... | collective-permute-start | bytes 7077896 | tf_op jit(solution)/shard_map/ppermute | solution.py:541
  440.5 60.0 %collective-permute-start.19 = (f32[2304,256]{1,0:T(8,128)}, f32[2304,256]{1,0:T(8,128)}, u32[]{:S(2)}, u32[]{:S(2)}) collective-permute-start(f32[2304,256]{1,0:T(8,128)} %constant_dynamic-update-slice_fusion.5.refs_0_), channel_id=1, source_target_pairs={{0,2},{1,5},{2,0},{3,7},{4,6},{5,1},{6,4},{7,3},{8,10},{9,13},{10,... | collective-permute-start | bytes 7077896 | tf_op jit(solution)/shard_map/ppermute | solution.py:541
  442.9 402.3 %collective-permute-start.31 = (f32[2304,256]{1,0:T(8,128)S(1)}, f32[2304,256]{1,0:T(8,128)}, u32[]{:S(2)}, u32[]{:S(2)}) collective-permute-start(f32[2304,256]{1,0:T(8,128)S(1)} %constant_dynamic-update-slice_fusion.1.refs_0_), channel_id=1, source_target_pairs={{0,1},{1,0},{2,3},{3,2},{4,5},{5,4},{6,7},{7,6},{8,9},{9,8},{10,11... | collective-permute-start | bytes 7077896 | tf_op jit(solution)/shard_map/ppermute | solution.py:545
  450.0 107.2 %collective-permute-start.10 = (f32[2304,256]{1,0:T(8,128)}, f32[2304,256]{1,0:T(8,128)}, u32[]{:S(2)}, u32[]{:S(2)}) collective-permute-start(f32[2304,256]{1,0:T(8,128)} %collective-permute-done.8.refs_1_), channel_id=1, source_target_pairs={{0,1},{1,0},{2,3},{3,2},{4,5},{5,4},{6,7},{7,6},{8,9},{9,8},{10,11... | collective-permute-start | bytes 7077896 | tf_op jit(solution)/shard_map/ppermute | solution.py:545
  475.3 369.9 %collective-permute-start.32 = (f32[2304,256]{1,0:T(8,128)}, f32[2304,256]{1,0:T(8,128)}, u32[]{:S(2)}, u32[]{:S(2)}) collective-permute-start(f32[2304,256]{1,0:T(8,128)} %collective-permute-done.30.refs_1_), channel_id=1, source_target_pairs={{0,1},{1,0},{2,3},{3,2},{4,5},{5,4},{6,7},{7,6},{8,9},{9,8},{10,11... | collective-permute-start | bytes 7077896 | tf_op jit(solution)/shard_map/ppermute | solution.py:545
  482.6 650.6 %collective-permute-start.20 = (f32[2304,256]{1,0:T(8,128)}, f32[2304,256]{1,0:T(8,128)}, u32[]{:S(2)}, u32[]{:S(2)}) collective-permute-start(f32[2304,256]{1,0:T(8,128)} %constant_dynamic-update-slice_fusion.5.refs_0_), channel_id=1, source_target_pairs={{0,1},{1,0},{2,3},{3,2},{4,5},{5,4},{6,7},{7,6},{8,9},{9,8},{10,11... | collective-permute-start | bytes 7077896 | tf_op jit(solution)/shard_map/ppermute | solution.py:545
  500.6 632.7 %collective-permute-start.21 = (f32[2304,256]{1,0:T(8,128)}, f32[2304,256]{1,0:T(8,128)}, u32[]{:S(2)}, u32[]{:S(2)}) collective-permute-start(f32[2304,256]{1,0:T(8,128)} %collective-permute-done.19.refs_1_), channel_id=1, source_target_pairs={{0,1},{1,0},{2,3},{3,2},{4,5},{5,4},{6,7},{7,6},{8,9},{9,8},{10,11... | collective-permute-start | bytes 7077896 | tf_op jit(solution)/shard_map/ppermute | solution.py:545
  (26 other events, 799.2 us)

commit v2 on v1

v2 whole, which is shorter than its diff:
```python
import functools
import jax
import jax.numpy as jnp
import numpy as np
from jax import lax
from jax.experimental import pallas as pl
from jax.experimental.pallas import tpu as pltpu
from jax.sharding import PartitionSpec as P

NT = (((1,), (1,)), ((), ()))
TN = (((0,), (0,)), ((), ()))
F32, BF16 = jnp.float32, jnp.bfloat16
TILE = 128
MASKED = -1000000000.0
EPS = 1e-06
far_steps = np.array([12, 16, 23, 32, 46, 64, 91], dtype=np.int32)


def dot(a, b, dims=None):
    if dims is None:
        return jnp.dot(a, b, preferred_element_type=F32)
    return lax.dot_general(a, b, dims, preferred_element_type=F32)


def bucket_of(relative, bucket_count):
    distance = np.abs(relative)
    beyond = np.sum(distance[..., None] >= far_steps, axis=-1)
    inner = np.where(distance < bucket_count // 4, distance, bucket_count // 4 + beyond)
    return np.where(relative > 0, bucket_count // 2, 0) + inner


def band_buckets(bucket_count):
    lanes = np.arange(4 * TILE)
    offsets = np.where(lanes < 2 * TILE, lanes, lanes - 4 * TILE)
    return bucket_of(-offsets, bucket_count)


def segments_along(len_ref, row, shape, axis):
    at = lax.broadcasted_iota(jnp.int32, shape, axis)
    total = jnp.zeros(shape, jnp.int32)
    end = jnp.int32(0)
    for j in range(len_ref.shape[1]):
        end = end + len_ref[row, j]
        total = total + jnp.where(at >= end, 1, 0)
    return total


def fill_mask(len_ref, row, mask_ref, last):
    seq = mask_ref.shape[0]
    of_q = segments_along(len_ref, row, (1, seq), 1)
    of_k = segments_along(len_ref, row, (seq, TILE), 0)
    of_k = jnp.where(of_k < last, of_k, -1)
    for j in range(seq // TILE):
        same = of_k == of_q[:, j * TILE : (j + 1) * TILE]
        mask_ref[:, j * TILE : (j + 1) * TILE] = jnp.where(same, 0.0, MASKED)
    return of_q < last


def band_of(vector):
    wide = jnp.broadcast_to(vector, (TILE, 4 * TILE))
    return pltpu.roll(wide, 0, 1, stride=1, stride_axis=0)


def bias_row(band, vector, ki, count):
    shape = (TILE, TILE)
    tiles = []
    for qi in range(count):
        step = ki - qi
        if step == 0:
            tiles.append(band[:, 0:TILE])
        elif step == -1:
            tiles.append(band[:, TILE : 2 * TILE])
        elif step == 1:
            tiles.append(band[:, 3 * TILE : 4 * TILE])
        elif step < 0:
            tiles.append(jnp.broadcast_to(vector[:, 2 * TILE - 1 : 2 * TILE], shape))
        else:
            tiles.append(jnp.broadcast_to(vector[:, 2 * TILE : 2 * TILE + 1], shape))
    return jnp.concatenate(tiles, axis=1)


def norm_scale(value):
    return lax.rsqrt(jnp.mean(value * value, axis=-1, keepdims=True) + EPS)


def attn_fwd_kernel(
    len_ref, tok_ref, gain_ref, wq_ref, wk_ref, wv_ref, wo_ref, band_ref,
    h1_ref, q_ref, k_ref, v_ref, att_ref, attT_ref, lse_ref, x1_ref, h2_ref,
    mask_ref, s_ref, p_ref,
):
    seq, width = tok_ref.shape[1:]
    pairs = band_ref.shape[0]
    head = TILE // 2
    row = pl.program_id(0)
    valid = fill_mask(len_ref, row, mask_ref, len_ref.shape[1] - 1)
    tok = tok_ref[0].astype(F32)
    h1 = (tok * norm_scale(tok) * gain_ref[0:1, :]).astype(BF16)
    h1_ref[0] = h1
    q_ref[0] = dot(h1, wq_ref[...]).astype(BF16)
    k_ref[0] = dot(h1, wk_ref[...]).astype(BF16)
    v_ref[0] = dot(h1, wv_ref[...]).astype(BF16)
    count = seq // TILE
    low_half = lax.broadcasted_iota(jnp.int32, (1, TILE), 1) < head

    def pair(p, carry):
        lanes = pl.ds(pl.multiple_of(p * TILE, TILE), TILE)
        qp, kp, vp = q_ref[0, :, lanes], k_ref[0, :, lanes], v_ref[0, :, lanes]
        vT = vp.T
        outs = []
        for a in range(2):
            qm = jnp.where(low_half if a == 0 else ~low_half, qp, jnp.zeros_like(qp))
            vector = band_ref[p, a : a + 1, :]
            band = band_of(vector)
            top = None
            for ki in range(count):
                rows = slice(ki * TILE, (ki + 1) * TILE)
                s = dot(kp[rows], qm, NT) + bias_row(band, vector, ki, count) + mask_ref[rows, :]
                s_ref[a, rows, :] = s
                most = jnp.max(s, axis=0, keepdims=True)
                top = most if top is None else jnp.maximum(top, most)
            total = jnp.zeros_like(top)
            for ki in range(count):
                rows = slice(ki * TILE, (ki + 1) * TILE)
                e = jnp.exp(s_ref[a, rows, :] - top)
                total = total + jnp.sum(e, axis=0, keepdims=True)
                p_ref[a, rows, :] = e.astype(BF16)
            o = dot(vT[a * head : (a + 1) * head], p_ref[a])
            o = jnp.where(valid, o / total, 0.0)
            outs.append(o)
            lse_ref[0, p, a : a + 1, :] = top + jnp.log(total)
        both = jnp.concatenate(outs, axis=0)
        attT_ref[0, lanes, :] = both.astype(BF16)
        att_ref[0, :, lanes] = both.T.astype(BF16)
        return carry

    lax.fori_loop(0, pairs, pair, 0)
    x1 = tok_ref[0].astype(F32) + dot(att_ref[0], wo_ref[...])
    x1_ref[0] = x1
    h2_ref[0] = (x1 * norm_scale(x1) * gain_ref[1:2, :]).astype(BF16)


VMEM = 60 * 2**20
COST = pl.CostEstimate(flops=10**11, transcendentals=0, bytes_accessed=1)
ANYWHERE = pl.BlockSpec(memory_space=pl.ANY)


def params(limit=VMEM):
    return pltpu.CompilerParams(vmem_limit_bytes=limit)


def attn_fwd(tokens, lengths, gains, wq, wk, wv, wo, band):
    rows, seq, width = tokens.shape
    pairs = band.shape[0]
    full = lambda a: pl.BlockSpec(a.shape, lambda r, l: (0,) * a.ndim, pipeline_mode=pl.Buffered(1))
    per_row = lambda *s: pl.BlockSpec((1,) + s, lambda r, l: (r,) + (0,) * len(s))
    tall = jax.ShapeDtypeStruct((rows, seq, width), BF16)
    outs = [tall] * 5 + [
        jax.ShapeDtypeStruct((rows, width, seq), BF16),
        jax.ShapeDtypeStruct((rows, pairs, 2, seq), F32),
        jax.ShapeDtypeStruct((rows, seq, width), F32),
        tall,
    ]
    return pl.pallas_call(
        attn_fwd_kernel,
        grid_spec=pltpu.PrefetchScalarGridSpec(
            num_scalar_prefetch=1,
            grid=(rows,),
            in_specs=[per_row(seq, width), full(gains), full(wq), full(wk), full(wv), full(wo), full(band)],
            out_specs=[per_row(seq, width)] * 5 + [per_row(width, seq), per_row(pairs, 2, seq), per_row(seq, width), per_row(seq, width)],
            scratch_shapes=[
                pltpu.VMEM((seq, seq), F32),
                pltpu.VMEM((2, seq, seq), F32),
                pltpu.VMEM((2, seq, seq), BF16),
            ],
        ),
        out_shape=outs,
        cost_estimate=COST, compiler_params=params(32 * 2**20),
        name="attn_fwd",
    )(lengths, tokens, gains, wq, wk, wv, wo, band)


GELU_C = float(np.sqrt(2.0 / np.pi))


def gelu_pair(v):
    v2 = v * v
    t = jnp.tanh(GELU_C * v * (1.0 + 0.044715 * v2))
    half = 0.5 * (1.0 + t)
    slope = half + (0.5 * GELU_C) * v * (1.0 - t * t) * (1.0 + (3 * 0.044715) * v2)
    return v * half, slope


def place(core, mine, other, keep, send, sems):
    both = lambda a, b: [(src, dst, sems.at[n, i]) for n, pairs in enumerate((a, b)) for i, (src, dst) in enumerate(pairs)]
    return [(core == 0, both(mine(keep), other(send))), (core != 0, both(mine(send), other(keep)))]


def run_all(cases, action):
    for condition, copies in cases:

        @pl.when(condition)
        def _():
            for src, dst, sem in copies:
                getattr(pltpu.make_async_copy(src, dst, sem), action)()


def ffn_kernel(steps, slabs, n_acc, info_ref, h2_ref, dy_ref, win_ref, wout_ref, *refs):
    acc, refs = refs[:n_acc], refs[n_acc:]
    if slabs:
        keep_ref, send_ref, mix_ref, dtwo_ref, h2T_ref, gin_ref, gout_ref, sems = refs[-8:]
    else:
        gin_ref, gout_ref, mix_ref, dtwo_ref, h2T_ref = refs[-5:]
    step = pl.program_id(0)
    h2, dy = h2_ref[...], dy_ref[...]
    width = h2.shape[1]
    sub = win_ref.shape[1]
    wide, tall = width // 256, sub // 256
    if slabs:
        in_rows, out_rows = width // slabs, sub * steps // slabs
        piece = in_rows * tall * steps
        here = slabs // steps

    def moves(at):
        def of_in(ref):
            return [
                (
                    gin_ref.at[at, i * in_rows * tall : (i + 1) * in_rows * tall, :],
                    ref.at[pl.ds(pl.multiple_of(i * piece + at * (in_rows * tall), 8), in_rows * tall), :],
                )
                for i in range(slabs)
            ]

        def of_out(ref):
            return [(gout_ref.at[at], ref.at[pl.ds(pl.multiple_of(at * (here * piece), 8), here * piece), :])]

        return place(info_ref[0], of_in, of_out, keep_ref, send_ref, sems.at[at])

    @pl.when(step == 0)
    def _():
        h2T_ref[...] = h2_ref[...].T

    pre = dot(h2, win_ref[...])
    act, slope = gelu_pair(pre)
    act = act.astype(BF16)
    gout = dot(act, dy, TN)
    if slabs:
        for i in range(here):
            for j in range(wide):
                at = (i * wide + j) * out_rows
                gout_ref[step, at : at + out_rows, :] = gout[i * out_rows : (i + 1) * out_rows, j * 256 : (j + 1) * 256]
    else:
        gout_ref[...] = gout
    dpre = (dot(dy, wout_ref[...], NT) * slope).astype(BF16)
    gin = dot(h2T_ref[...], dpre)
    if slabs:
        for i in range(slabs):
            for j in range(tall):
                at = (i * tall + j) * in_rows
                gin_ref[step, at : at + in_rows, :] = gin[i * in_rows : (i + 1) * in_rows, j * 256 : (j + 1) * 256]
        run_all(moves(step), "start")
    else:
        gin_ref[...] = gin
    mix = dot(act, wout_ref[...])
    dtwo = dot(dpre, win_ref[...], NT)

    @pl.when(step == 0)
    def _():
        mix_ref[...] = acc[0][...] + mix if n_acc else mix
        dtwo_ref[...] = acc[1][...] + dtwo if n_acc else dtwo

    @pl.when(step > 0)
    def _():
        mix_ref[...] += mix
        dtwo_ref[...] += dtwo

    if slabs:

        @pl.when(step == steps - 1)
        def _():
            for at in range(steps):
                run_all(moves(at), "wait")


def ffn_chunk(info, slabs, h2, dy, w_in, w_out, start, size, sub, acc, after):
    toks, width = h2.shape
    base = start // sub
    steps = size // sub
    piece = width * (sub // 256)
    full = lambda a: pl.BlockSpec(a.shape, lambda s, c: (0,) * a.ndim, pipeline_mode=pl.Buffered(1))
    total = pl.BlockSpec((toks, width), lambda s, c: (0, 0))
    total_shape = jax.ShapeDtypeStruct((toks, width), F32)
    if slabs:
        out_specs = [ANYWHERE, ANYWHERE]
        out_shape = [jax.ShapeDtypeStruct((steps * piece, 256), F32)] * 2
        scratch = [
            pltpu.VMEM((steps, piece, 256), F32),
            pltpu.VMEM((steps, piece, 256), F32),
            pltpu.SemaphoreType.DMA((steps, 2, slabs)),
        ]
    else:
        out_specs = [pl.BlockSpec((width, sub), lambda s, c: (0, s)), pl.BlockSpec((sub, width), lambda s, c: (s, 0))]
        out_shape = [jax.ShapeDtypeStruct((width, size), F32), jax.ShapeDtypeStruct((size, width), F32)]
        scratch = []
    return pl.pallas_call(
        functools.partial(ffn_kernel, steps, slabs, len(acc)),
        grid_spec=pltpu.PrefetchScalarGridSpec(
            num_scalar_prefetch=1,
            grid=(steps,),
            in_specs=[full(h2), full(dy), pl.BlockSpec((width, sub), lambda s, c: (0, base + s)), pl.BlockSpec((sub, width), lambda s, c: (base + s, 0))]
            + [full(a) for a in acc]
            + [ANYWHERE] * len(after),
            out_specs=out_specs + [total, total],
            scratch_shapes=[pltpu.VMEM((width, toks), BF16)] + scratch,
        ),
        out_shape=out_shape + [total_shape, total_shape],
        cost_estimate=COST, compiler_params=params(52 * 2**20),
        name="ffn",
    )(info, h2, dy, w_in, w_out, *acc, *after)


def resid_kernel(len_ref, x1_ref, mix_ref, dtwo_ref, dy_ref, gain_ref, attT_ref, wo_ref,
                 mixed_ref, dres_ref, datt_ref, gwo_ref, ggain_ref):
    step = pl.program_id(0)
    x1, dtwo = x1_ref[0], dtwo_ref[0]
    mixed_ref[0] = (x1 + mix_ref[0]).astype(BF16)
    s = norm_scale(x1)
    g = gain_ref[1:2, :] * dtwo
    dres = dy_ref[0].astype(F32) + s * g - x1 * (s * s * s * jnp.mean(x1 * g, axis=-1, keepdims=True))
    dres_ref[0] = dres
    dbranch = dres.astype(BF16)
    ggain = jnp.sum(dtwo * x1 * s, axis=0, keepdims=True)
    gwo = dot(attT_ref[0], dbranch)
    seq = x1.shape[0]
    seg = segments_along(len_ref, step, (seq, TILE), 0)[:, :1]
    datt = dot(dbranch, wo_ref[...], NT)
    datt_ref[0] = jnp.where(seg < len_ref.shape[1] - 1, datt, 0.0).astype(BF16)

    @pl.when(step == 0)
    def _():
        ggain_ref[...] = ggain
        gwo_ref[...] = gwo

    @pl.when(step > 0)
    def _():
        ggain_ref[...] += ggain
        gwo_ref[...] += gwo


def resid_bwd(lengths, x1, mix, dtwo, dy, gain, attT, wo):
    rows, seq, width = x1.shape
    full = lambda a: pl.BlockSpec(a.shape, lambda r, l: (0,) * a.ndim)
    tall = pl.BlockSpec((1, seq, width), lambda r, l: (r, 0, 0))
    return pl.pallas_call(
        resid_kernel,
        grid_spec=pltpu.PrefetchScalarGridSpec(
            num_scalar_prefetch=1,
            grid=(rows,),
            in_specs=[tall, tall, tall, tall, full(gain), pl.BlockSpec((1, width, seq), lambda r, l: (r, 0, 0)), full(wo)],
            out_specs=[tall, tall, tall, pl.BlockSpec((width, width), lambda r, l: (0, 0)), pl.BlockSpec((1, width), lambda r, l: (0, 0))],
        ),
        out_shape=[
            jax.ShapeDtypeStruct((rows, seq, width), BF16),
            jax.ShapeDtypeStruct((rows, seq, width), F32),
            jax.ShapeDtypeStruct((rows, seq, width), BF16),
            jax.ShapeDtypeStruct((width, width), F32),
            jax.ShapeDtypeStruct((1, width), F32),
        ],
        cost_estimate=COST, compiler_params=params(40 * 2**20),
        name="resid_bwd",
    )(lengths, x1, mix, dtwo, dy, gain, attT, wo)


def diagonal_sums(x):
    depth, lanes = x.shape
    total = x[0:8]
    for g in range(8, depth, 8):
        total = total + pltpu.roll(x[g : g + 8], lanes - g, 1)
    at = lax.broadcasted_iota(jnp.int32, (8, lanes), 0)
    for bit in (1, 2, 4):
        total = jnp.where((at & bit) != 0, pltpu.roll(total, lanes - bit, 1), total)
    return jnp.sum(total, axis=0, keepdims=True)


def attn_bwd_kernel(len_ref, q_ref, k_ref, v_ref, do_ref, lse_ref, band_ref, *rest):
    (
        dq_ref, dk_ref, dv_ref, diag_ref,
        mask_ref, p_ref, pl_ref, dp_ref, ds_ref, near_ref, far_ref,
    ) = rest[-11:]
    pair, row = pl.program_id(0), pl.program_id(1)
    seq = q_ref.shape[1]
    head = TILE // 2
    count = seq // TILE
    fill_mask(len_ref, row, mask_ref, len_ref.shape[1] - 1)
    low_half = lax.broadcasted_iota(jnp.int32, (1, TILE), 1) < head
    qp, kp, vp, dop = q_ref[0], k_ref[0], v_ref[0], do_ref[0]
    kT = kp.T

    @pl.when(row == 0)
    def _():
        near_ref[...] = jnp.zeros_like(near_ref)
        far_ref[...] = jnp.zeros_like(far_ref)

    dqT, dk, dv = [], None, None
    for a in range(2):
        own = low_half if a == 0 else ~low_half
        qm = jnp.where(own, qp, jnp.zeros_like(qp))
        dom = jnp.where(own, dop, jnp.zeros_like(dop))
        vector = band_ref[0, a : a + 1, :]
        band = band_of(vector)
        lse = lse_ref[0, 0, a : a + 1, :]
        delta = jnp.zeros((1, seq), F32)
        for ki in range(count):
            rows = slice(ki * TILE, (ki + 1) * TILE)
            s = dot(kp[rows], qm, NT) + bias_row(band, vector, ki, count) + mask_ref[rows, :]
            prob = jnp.exp(s - lse)
            dp = dot(vp[rows], dom, NT)
            delta = delta + jnp.sum(prob * dp, axis=0, keepdims=True)
            p_ref[a, rows, :] = prob
            pl_ref[a, rows, :] = prob.astype(BF16)
            dp_ref[a, rows, :] = dp
        for ki in range(count):
            rows = slice(ki * TILE, (ki + 1) * TILE)
            ds = p_ref[a, rows, :] * (dp_ref[a, rows, :] - delta)
            ds_ref[a, rows, :] = ds.astype(BF16)
            for qi in range(count):
                tile = ds[:, qi * TILE : (qi + 1) * TILE]
                step = ki - qi
                if abs(step) <= 1:
                    at = (0 if step == 0 else 1 if step == -1 else 3) * TILE
                    near_ref[a, :, at : at + TILE] += tile
                else:
                    at = 0 if step < 0 else TILE
                    far_ref[a, :, at : at + TILE] += tile
        dva = dot(pl_ref[a], dom)
        dka = dot(ds_ref[a], qm)
        dv = dva if dv is None else dv + dva
        dk = dka if dk is None else dk + dka
        dqT.append(dot(kT[a * head : (a + 1) * head], ds_ref[a]))
    dv_ref[0] = dv.astype(BF16)
    dk_ref[0] = dk.astype(BF16)
    dq_ref[0] = jnp.concatenate(dqT, axis=0).T.astype(BF16)

    @pl.when(row == pl.num_programs(1) - 1)
    def _():
        for a in range(2):
            diag_ref[0, a : a + 1, : 4 * TILE] = diagonal_sums(near_ref[a])
            diag_ref[0, a : a + 1, 4 * TILE :] = jnp.sum(far_ref[a], axis=0, keepdims=True)


def attn_bwd(lengths, q, k, v, do, lse, band, first, pairs, after):
    rows, seq, width = q.shape
    tall = pl.BlockSpec((1, seq, TILE), lambda p, r, l: (r, 0, first + p))
    tall_out = pl.BlockSpec((1, seq, TILE), lambda p, r, l: (r, 0, p))
    out = jax.ShapeDtypeStruct((rows, seq, pairs * TILE), BF16)
    return pl.pallas_call(
        attn_bwd_kernel,
        grid_spec=pltpu.PrefetchScalarGridSpec(
            num_scalar_prefetch=1,
            grid=(pairs, rows),
            in_specs=[tall] * 4
            + [pl.BlockSpec((1, 1, 2, seq), lambda p, r, l: (r, first + p, 0, 0)), pl.BlockSpec((1, 2, 4 * TILE), lambda p, r, l: (first + p, 0, 0))]
            + [ANYWHERE] * len(after),
            out_specs=[tall_out] * 3 + [pl.BlockSpec((1, 2, 6 * TILE), lambda p, r, l: (p, 0, 0))],
            scratch_shapes=[
                pltpu.VMEM((seq, seq), F32),
                pltpu.VMEM((2, seq, seq), F32),
                pltpu.VMEM((2, seq, seq), BF16),
                pltpu.VMEM((2, seq, seq), F32),
                pltpu.VMEM((2, seq, seq), BF16),
                pltpu.VMEM((2, TILE, 4 * TILE), F32),
                pltpu.VMEM((2, TILE, 2 * TILE), F32),
            ],
        ),
        out_shape=[out] * 3 + [jax.ShapeDtypeStruct((pairs, 2, 6 * TILE), F32)],
        cost_estimate=COST, compiler_params=params(24 * 2**20),
        name="attn_bwd",
    )(lengths, q, k, v, do, lse, band, *after)


def wgrad_kernel(slabs, n_more, info_ref, h1_ref, dq_ref, dk_ref, dv_ref, *refs):
    more, refs = refs[:n_more], refs[n_more:]
    keep_ref, send_ref, h1T_ref, g_ref, sems = refs[-5:]
    width, cols = h1_ref.shape[1], g_ref.shape[2]
    stripes = keep_ref.shape[0] * 2 // width
    rows = width // 2 // slabs

    def put(j, block):
        for c in range(2):
            for s in range(slabs):
                at, begin = (s * stripes + j) * rows, (c * slabs + s) * rows
                g_ref[c, at : at + rows, :] = block[begin : begin + rows]

    h1T_ref[...] = h1_ref[...].T
    for j, d in enumerate((dq_ref, dk_ref, dv_ref)):
        put(j, dot(h1T_ref[...], d[...]))
    for j in range(stripes - 3):
        put(3 + j, more[0][:, j * cols : (j + 1) * cols])
    moves = place(
        info_ref[0], lambda ref: [(g_ref.at[0], ref)], lambda ref: [(g_ref.at[1], ref)], keep_ref, send_ref, sems
    )
    run_all(moves, "start")
    run_all(moves, "wait")


def wgrads(info, slabs, h1, ds, more, after):
    toks, width = h1.shape
    cols = ds[0].shape[1]
    half = width // 2 * (3 + sum(m.shape[1] // cols for m in more))
    whole = pl.BlockSpec(memory_space=pltpu.VMEM)
    return pl.pallas_call(
        functools.partial(wgrad_kernel, slabs, len(more)),
        in_specs=[pl.BlockSpec(memory_space=pltpu.SMEM)] + [whole] * (4 + len(more)) + [ANYWHERE] * len(after),
        out_specs=[ANYWHERE] * 2,
        out_shape=[jax.ShapeDtypeStruct((half, cols), F32)] * 2,
        scratch_shapes=[pltpu.VMEM((width, toks), BF16), pltpu.VMEM((2, half, cols), F32), pltpu.SemaphoreType.DMA((2, 1))],
        cost_estimate=COST, compiler_params=params(24 * 2**20),
        name="attn_wgrad",
    )(info, h1, *ds, *more, *after)


def tokgrad_kernel(halves, tok_ref, dres_ref, gain_ref, wq_ref, wk_ref, wv_ref, *refs):
    out_ref, ggain_ref = refs[-2:]
    step = pl.program_id(0)
    done = None
    for i, w in enumerate((wq_ref, wk_ref, wv_ref)):
        d = jnp.concatenate([refs[h * 3 + i][...] for h in range(halves)], axis=1)
        term = dot(d, w[...], NT)
        done = term if done is None else done + term
    tok = tok_ref[...].astype(F32)
    s = norm_scale(tok)
    g = gain_ref[0:1, :] * done
    out_ref[...] = (dres_ref[...] + s * g - tok * (s * s * s * jnp.mean(tok * g, axis=-1, keepdims=True))).astype(BF16)
    ggain = jnp.sum(done * tok * s, axis=0, keepdims=True)

    @pl.when(step == 0)
    def _():
        ggain_ref[...] = ggain

    @pl.when(step > 0)
    def _():
        ggain_ref[...] += ggain


def tokgrad(tok, dres, gains, ds, wq, wk, wv, after, block=512):
    toks, width = tok.shape
    full = lambda a: pl.BlockSpec(a.shape, lambda s: (0,) * a.ndim, pipeline_mode=pl.Buffered(1))
    tall = pl.BlockSpec((block, width), lambda s: (s, 0))
    return pl.pallas_call(
        functools.partial(tokgrad_kernel, len(ds) // 3),
        grid=(toks // block,),
        in_specs=[tall, tall, full(gains), full(wq), full(wk), full(wv)]
        + [pl.BlockSpec((block, d.shape[1]), lambda s: (s, 0)) for d in ds]
        + [ANYWHERE] * len(after),
        out_specs=[tall, pl.BlockSpec((1, width), lambda s: (0, 0))],
        out_shape=[jax.ShapeDtypeStruct((toks, width), BF16), jax.ShapeDtypeStruct((1, width), F32)],
        cost_estimate=COST, compiler_params=params(32 * 2**20),
        name="tokgrad",
    )(tok, dres, gains, wq, wk, wv, *ds, *after)


class Route:
    def __init__(self, size, even, odd):
        self.size, self.even, self.odd = size, even, odd
        self.count = len(even)
        core, row = lax.axis_index("blk"), lax.axis_index("rows")
        one = lambda group: sum(((row >> b) & 1) << (len(group) - 1 - i) for i, b in enumerate(group))
        at = lambda c, phase: jnp.where(c == 0, one(even[phase]), one(odd[phase])).astype(jnp.int32)
        self.at = [at(core, phase) for phase in range(self.count)]
        self.far = at(1 - core, 0)
        self.ways = [1 << len(group) for group in even]

    def exchange(self, x, phase, step):
        def other(r, group):
            for i, b in enumerate(group):
                r ^= ((step >> (len(group) - 1 - i)) & 1) << b
            return r

        moves = [
            (r * 2 + c, other(r, (self.even, self.odd)[c][phase]) * 2 + c) for r in range(self.size) for c in range(2)
        ]
        return lax.ppermute(x, ("rows", "blk"), moves)


def swap_cores(x):
    return lax.ppermute(x, "blk", [(0, 1), (1, 0)])


def following(values, after):
    if not after:
        return values
    return lax.optimization_barrier((tuple(values), tuple(after)))[0]


class Sum:
    def __init__(self, route, keep, send):
        self.route = route
        self.parts = [keep, swap_cores(send)]
        self.begins = [0, 0]
        self.shares = [keep.shape[0]]
        for ways in route.ways:
            if self.shares[-1] % (8 * ways):
                break
            self.shares.append(self.shares[-1] // ways)
        self.divided = len(self.shares) - 1
        self.phase = 0
        self.steps = (
            [self.send] * self.divided
            + [self.finish]
            + [self.add] * (route.count - self.divided)
            + [self.join] * (self.divided - 1)
            + [self.swap]
        )

    def advance(self, after):
        return self.steps.pop(0)(after) if self.steps else after

    def total(self, places, rows):
        out = None
        for begin, part in zip(self.begins, self.parts):
            at = 0
            for phase in range(begin, len(places)):
                at = at * self.route.ways[phase] + places[phase]
            share = lax.dynamic_slice_in_dim(part, at * rows, rows, 0) if part.shape[0] > rows else part
            out = share if out is None else out + share
        return out

    def send(self, after):
        phase = self.phase
        places = following(self.route.at[: phase + 1], after)
        outs = []
        for step in range(1, self.route.ways[phase]):
            outs.append(self.total([*places[:phase], places[phase] ^ step], self.shares[phase + 1]))
        for step, out in enumerate(outs):
            self.parts.append(self.route.exchange(out, phase, step + 1))
            self.begins.append(phase + 1)
        self.phase += 1
        return outs

    def finish(self, after):
        self.piece = self.total(following(self.route.at[: self.phase], after), self.shares[self.phase])
        return self.gather()

    def gather(self):
        if self.divided <= self.phase < self.route.count:
            phase = self.phase
        else:
            phase = self.phase = min(self.phase, self.divided) - 1
        self.got = [self.route.exchange(self.piece, phase, step) for step in range(1, self.route.ways[phase])]
        if self.phase == 0:
            self.far_piece = swap_cores(self.piece)
        return [self.piece]

    def add(self, after):
        got = following(self.got, after)
        self.piece = functools.reduce(lambda a, b: a + b, got, self.piece)
        self.phase += 1
        return self.gather()

    def join(self, after):
        (at,) = following((self.route.at[self.phase],), after)
        pieces = [self.piece, *self.got]
        rows = []
        for slot in range(len(pieces)):
            row = pieces[-1]
            for step in range(len(pieces) - 1):
                row = jnp.where(at == slot ^ step, pieces[step], row)
            rows.append(row)
        self.piece = jnp.concatenate(rows)
        return self.gather()

    def swap(self, after):
        (got,) = following(self.got, after)
        self.sources = (self.piece, got, self.far_piece, swap_cores(got))
        return [got]


class SmallSum:
    @staticmethod
    def steps_of(route, phase):
        return [1 << i for i in range(len(route.even[phase]))]

    def __init__(self, route, values):
        self.route = route
        self.shapes = [v.shape for v in values]
        flat = jnp.concatenate([v.reshape(-1) for v in values])
        self.sum = jnp.pad(flat, (0, -flat.shape[0] % 2048)).reshape(-1, 256)
        self.steps = [
            functools.partial(route.exchange, phase=p, step=step) for p in range(route.count) for step in SmallSum.steps_of(route, p)
        ] + [swap_cores]
        self.got = self.steps.pop(0)(self.sum)

    def advance(self, after):
        if self.got is None:
            return after
        mine, got = following((self.sum, self.got), after)
        self.sum = mine + got
        self.got = self.steps.pop(0)(self.sum) if self.steps else None
        return [self.sum]

    def values(self):
        while self.got is not None:
            self.advance(())
        flat, at, out = self.sum.reshape(-1), 0, []
        for shape in self.shapes:
            size = int(np.prod(shape))
            out.append(flat[at : at + size].reshape(shape))
            at += size
        return out


def assemble_kernel(spread, n_outs, info_ref, *refs):
    sources, outs = refs[:4], refs[-n_outs:]
    target, half = pl.program_id(0), pl.program_id(1)
    for n in range(4):
        for t in range(2):

            @pl.when((info_ref[2 + n] == 2 * target + half) & (target == t))
            def _():
                spread(t, sources[n], outs)


def assemble(info, slabs, spread, outs, blocks, sources, group, earlier, after):
    rows, cols = sources[0].shape
    count = slabs // 2 // group

    def source_spec(n):
        def index(t, h, j, i):
            stage, now = i[2 + n], 2 * t + h
            return jnp.where(now < stage, 0, jnp.where(now == stage, j, count - 1)), 0

        return pl.BlockSpec((rows // count, cols), index)

    def out_spec(target, block, row, column):
        def index(t, h, j, i):
            if target is None:
                return row + (2 * t + h) * count + j, column
            return row + jnp.where(t == target, h * count + j, 0 if target else 2 * count - 1), column

        return pl.BlockSpec(block, index)

    return pl.pallas_call(
        functools.partial(assemble_kernel, spread, len(outs)),
        grid_spec=pltpu.PrefetchScalarGridSpec(
            num_scalar_prefetch=1,
            grid=(2, 2, count),
            in_specs=[source_spec(n) for n in range(4)] + [ANYWHERE] * (len(earlier) + len(after)),
            out_specs=[out_spec(*b) for b in blocks],
        ),
        out_shape=[jax.ShapeDtypeStruct(s, F32) for s in outs],
        input_output_aliases={5 + i: i for i in range(len(earlier))},
        cost_estimate=COST, compiler_params=params(24 * 2**20),
        name="assemble",
    )(info, *sources, *earlier, *after)


def ffn_spread(width, size, slabs, group, target, source, outs):
    n, total = (size // 256, width) if target == 0 else (width // 256, size)
    rows = total // slabs
    for s in range(group):
        for j in range(n):
            at = (s * n + j) * rows
            outs[target][s * rows : (s + 1) * rows, j * 256 : (j + 1) * 256] = source[at : at + rows, :]


def attn_spread(columns, slabs, group, target, source, outs):
    n = len(columns)
    rows = source.shape[0] // (group * n)
    for s in range(group):
        for j, (out, column) in enumerate(columns):
            at = (s * n + j) * rows
            outs[out][s * rows : (s + 1) * rows, column : column + source.shape[1]] = source[at : at + rows, :]


ORDER = "F0 s0 F1 s0 R s1 s0 B0 W0 s0 s1 B1 s0 s1 s2 W1 T s3 s1 m s2 s0 m s2 s1 m s2 s3 m s1 s0 s3 s2 s0 s3 s2 s3 s1 s1 s3 s2 s2 s3 s3"


def on_device(tokens, lengths, attn_gain, wq, wk, wv, wo, table, ffn_gain, w_in, w_out, out_grad, *, size):
    rows, seq, width = tokens.shape
    buckets, heads = table.shape
    pairs = heads // 2
    ff = w_in.shape[1]
    slabs = 16
    bits = list(range(2, size.bit_length() - 1))
    rest = [tuple(bits[i : i + 2][::-1]) for i in range(0, len(bits), 2)]
    route = Route(size, [(0,), (1,)] + rest, [(1,), (0,)] + rest)
    core = lax.axis_index("blk")
    b, far = route.at[0], route.far
    info = jnp.stack(
        [core, lax.axis_index("rows"), 2 * core + b, 2 * core + 1 - b, 2 * (1 - core) + far, 2 * (1 - core) + 1 - far]
    ).astype(jnp.int32)
    lane_buckets = band_buckets(buckets)
    onehot = np.arange(buckets)[:, None] == lane_buckets[None, :]
    band = jnp.einsum(
        "bpa,bm->pam", table.reshape(buckets, pairs, 2), jnp.asarray(onehot, BF16), preferred_element_type=F32
    )
    gains = jnp.stack([attn_gain, ffn_gain]).astype(F32)
    flat = lambda a: a.reshape(rows * seq, a.shape[2])
    tall = lambda a: a.reshape(rows, seq, width)
    chunks, sub = 2, 768
    part = ff // chunks
    ends = bucket_of(np.array([-2 * TILE] * TILE + [2 * TILE] * TILE), buckets)
    spread = (np.concatenate([lane_buckets, ends])[:, None] == np.arange(buckets)[None, :]).astype(np.float32)

    h1, q, k, v, att, attT, lse, x1, h2 = attn_fwd(tokens, lengths, gains, wq, wk, wv, wo, band)
    acc, sums, after, ds, diags = (), [], (), [], []
    ffn_grads, attn_grads = (), ()

    def put(which, after):
        nonlocal ffn_grads, attn_grads
        group = 4
        sources = sums[which].sources
        if which < chunks:
            ffn_grads = assemble(
                info, slabs, functools.partial(ffn_spread, width, part, slabs, group), [w_in.shape, w_out.shape],
                [(0, (width // slabs * group, part), 0, which), (1, (part // slabs * group, width), which * (slabs // group), 0)],
                sources, group, tuple(ffn_grads), after,
            )
            return (ffn_grads[0],)
        half = which - chunks
        block = width // 2 // slabs * group
        columns = [(0, 0), (1, 0), (2, 0)] + [(3, 0), (3, width // 2)] * (half == 0)
        blocks = [(None, (block, width // 2), 0, half)] * 3 + [(None, (block, width), 0, 0)] * (half == 0)
        made = assemble(
            info, slabs, functools.partial(attn_spread, columns, slabs, group), [wq.shape] * len(blocks), blocks,
            sources, group, tuple(attn_grads[:3]), after,
        )
        attn_grads = list(made) + list(attn_grads[3:])
        return (made[0],)

    for at, op in enumerate(ORDER.split()):
        which = int(op[1]) if len(op) > 1 else 0
        if op[0] == "F":
            x, y, *acc = ffn_chunk(info, slabs, flat(h2), flat(out_grad), w_in, w_out, which * part, part, sub, acc, after)
            sums.append(Sum(route, x, y))
            after = (x,)
        elif op == "R":
            mixed, dres, datt, gwo, ggain2 = resid_bwd(lengths, x1, tall(acc[0]), tall(acc[1]), out_grad, gains, attT, wo)
            after = (mixed,)
        elif op[0] == "B":
            half = pairs // 2
            dq, dk, dv, diag = attn_bwd(lengths, q, k, v, datt, lse, band, which * half, half, after)
            ds += [flat(dq), flat(dk), flat(dv)]
            diags.append(diag)
            after = (dq,)
        elif op[0] == "W":
            keep, send = wgrads(info, slabs, flat(h1), ds[-3:], [] if which else [gwo], after)
            sums.append(Sum(route, keep, send))
            after = (keep,)
        elif op == "T":
            tgrad, ggain1 = tokgrad(flat(tokens), flat(dres), gains, ds, wq, wk, wv, after)
            diag = jnp.concatenate(diags).reshape(heads, 6 * TILE)
            gtable = jnp.einsum("hm,mb->bh", diag, jnp.asarray(spread), precision=lax.Precision.HIGHEST)
            small = SmallSum(route, (ggain1, ggain2, gtable))
            after = (ggain1,)
        elif op == "m":
            after = small.advance(after)
        else:
            after = sums[which].advance(after)
            if ORDER.split()[at:].count(op) == 1:
                while sums[which].steps:
                    after = sums[which].advance(after)
                after = put(which, after)
    ggain1, ggain2, gtable = small.values()
    return (mixed, tall(tgrad), ggain1[0], *attn_grads, gtable, ggain2[0], *ffn_grads)


def solution(mesh):
    split = P(("rows", "blk"))
    return jax.shard_map(
        functools.partial(on_device, size=mesh.shape["rows"]),
        mesh=mesh,
        in_specs=(split, split) + (P(),) * 9 + (split,),
        out_specs=(split, split) + (P(),) * 9,
        check_vma=False,
    )
```

time: 1430 us -> 430 us (0.30)
  Pallas kernels: 1020 us -> 173 us
  waiting for transfers between devices: 254 us -> 58.2 us
  local copies, waits for them, and re-layouts: 6.77 us -> 51.2 us
  blocking collectives: 39.2 us -> 0 us
  other arithmetic: 39.1 us -> 61.9 us
    pallas_call x7 -> x9, Pallas kernels: 937 us -> 101 us  [the longest x2 53.4 us: ffn_chunk(): pl.pallas_call(functools.partial(ffn_kernel, steps, slabs, len(acc)), gri...]
    ppermute x24 -> x44, waiting for transfers between devices: 254 us -> 44 us  [exchange(): return lax.ppermute(x, ('rows', 'blk'), moves)]
    unnamed x34 -> x172, local copies, waits for them, and re-layouts: 1.48 us -> 45.7 us
    psum x1 -> x0, blocking collectives: 39.2 us -> none  [on_device(): ggain1, ggain2, gtable = lax.psum((ggain1, ggain2, gtable), ('rows', 'blk'))]
    ppermute x24 -> x44, starting transfers between devices: 43.3 us -> 74.5 us  [exchange(): return lax.ppermute(x, ('rows', 'blk'), moves)]
    ppermute x9 -> x13, starting transfers between devices: 18.6 us -> 1.62 us  [swap_cores(): return lax.ppermute(x, 'blk', [(0, 1), (1, 0)])]
    add x15 -> x21, other arithmetic: 35.3 us -> 46.2 us  [the longest x16 43.6 us: total(): out = share if out is None else out + share]
    pallas_call x1 -> x2, Pallas kernels: 39.9 us -> 40.1 us  [attn_bwd(): pl.pallas_call(attn_bwd_kernel, grid_spec=pltpu.PrefetchScalarGridSpec(nu...]
  transfers between devices with their start and end apart: 33 -> 57, of which waited for: 20 -> 16; matrix products, arithmetic and copies ran while one was open for 3% -> 15% of each run, Pallas kernels for 48% -> 27%
where the time goes in v2:
time: 430 us; the launch traced here: 425 us
  Pallas kernels  173 us (40%)
  starting transfers between devices  76.1 us (18%)
  other arithmetic  61.9 us (14%)
  waiting for transfers between devices  58.2 us (14%)
  local copies, waits for them, and re-layouts  51.2 us (12%)
    ppermute x44, starting transfers between devices, exchange(): return lax.ppermute(x, ('rows', 'blk'), moves)  74.5 us
    pallas_call x2, Pallas kernels, ffn_chunk(): pl.pallas_call(functools.partial(ffn_kernel, steps, slabs, len(acc)), gri...  53.4 us
    unnamed x172, local copies, waits for them, and re-layouts  45.7 us
    ppermute x44, waiting for transfers between devices, exchange(): return lax.ppermute(x, ('rows', 'blk'), moves)  44 us
    add x16, other arithmetic, total(): out = share if out is None else out + share  43.6 us
    pallas_call x2, Pallas kernels, attn_bwd(): pl.pallas_call(attn_bwd_kernel, grid_spec=pltpu.PrefetchScalarGridSpec(nu...  40.1 us
    pallas_call x4, Pallas kernels, assemble(): pl.pallas_call(functools.partial(assemble_kernel, spread, len(outs)), gri...  33 us
    pallas_call x1, Pallas kernels, attn_fwd(): pl.pallas_call(attn_fwd_kernel, grid_spec=pltpu.PrefetchScalarGridSpec(nu...  23.8 us
  transfers between devices with their start and end apart: 57, of which 16 were waited for; matrix products, arithmetic and copies ran while one was open for 15% of the time, Pallas kernels for 27%

profile of v2, /device:TPU:0, one launch (start us, length us, event | category | flops | bytes accessed | tf_op | source)
XLA Modules:
  0.0 424.5 jit_solution(3437236944244713503)
XLA Ops:
  11.0 23.8 %attn_fwd.1 = (bf16[2,512,768]{2,1,0:T(8,128)(2,1)S(1)}, bf16[2,512,768]{2,1,0:T(8,128)(2,1)S(1)}, bf16[2,512,768]{2,1,0:T(8,128)(2,1)S(1)}, bf16[2,512,768]{2,1...) custom-call(s32[2,8]{1,0:T(2,128)S(1)} %copy-done.22, ...), custom_call_target="tpu_custom_call" | custom-call | flops 99999997952 | bytes 1 | tf_op jit(solution)/shard_map/attn_fwd/pallas_call | solution.py:163
  41.0 25.8 %ffn.2 = (f32[4608,256]{1,0:T(8,128)}, f32[4608,256]{1,0:T(8,128)}, f32[1024,768]{1,0:T(8,128)}, f32[1024,768]{1,0:T(8,128)}) custom-call(s32[6]{0:T(128)S(1)} %stack.39.info_ref, bf16[1024,768]{1,0:T(8,128)(2,1)S(1)} %bitcast.40, bf16[1024,768]{1,0:T(8,128)(2,1)} %bitcast.34, bf16[768,3072]{1,0:T(8,128)(2,1)} %win_ref.3, bf16[3072,768]{1,0:T(8,128)(2,1)} %wout_ref.3), custom_call_target="tpu_custom_call" | custom-call | flops 99999997952 | bytes 1 | tf_op jit(solution)/shard_map/ffn/pallas_call | solution.py:304
  67.3 7.9 %collective-permute-done = f32[4608,256]{1,0:T(8,128)} collective-permute-done((f32[4608,256]{1,0:T(8,128)}, f32[4608,256]{1,0:T(8,128)}, u32[]{:S(2)}, u32[]{:S(2)}) %collective-permute-start) | collective-permute-done | bytes 4718624 | tf_op jit(solution)/shard_map/ppermute | solution.py:585
  75.2 4.1 dynamic-slice_add_fusion.1.refs_2_
  82.1 27.6 %ffn.3 = (f32[4608,256]{1,0:T(8,128)}, f32[4608,256]{1,0:T(8,128)}, f32[1024,768]{1,0:T(8,128)}, f32[1024,768]{1,0:T(8,128)}) custom-call(s32[6]{0:T(128)S(1)} %stack.39.info_ref, bf16[1024,768]{1,0:T(8,128)(2,1)S(1)} %bitcast.41, bf16[1024,768]{1,0:T(8,128)(2,1)} %bitcast.35, bf16[768,3072]{1,0:T(8,128)(2,1)} %win_ref.3, bf16[3072,768]{1,0:T(8,128)(2,1)} %wout_ref.3, ...), custom_call_target="tpu_custom_call" | custom-call | flops 99999997952 | bytes 1 | tf_op jit(solution)/shard_map/ffn/pallas_call | solution.py:304
  116.7 8.3 %resid_bwd.1 = (bf16[2,512,768]{2,1,0:T(8,128)(2,1)}, f32[2,512,768]{2,1,0:T(8,128)S(1)}, bf16[2,512,768]{2,1,0:T(8,128)(2,1)S(1)}, f32[768,768]{1,0:T(8,128)S(1)}, f32[1,768]{1,0:T(1,128)S(1)}) custom-call(s32[2,8]{1,0:T(2,128)S(1)} %copy-done.22, f32[2,512,768]{2,1,0:T(8,128)S(1)} %copy-done.45, f32[2,512,768]{2,1,0:T(8,128)} %bitcast.56, ...), custom_call_target="tpu_custom_call" | custom-call | flops 99999997952 | bytes 1 | tf_op jit(solution)/shard_map/resid_bwd/pallas_call | solution.py:353
  128.1 4.7 %dynamic-slice_add_fusion = f32[2304,256]{1,0:T(8,128)} fusion(f32[4608,256]{1,0:T(8,128)} %collective-permute-done.1, s32[]{:T(128)S(6)} %select_n.503, f32[4608,256]{1,0:T(8,128)} %get-tuple-element.130), kind=kLoop, calls=%fused_computation.2 | loop fusion | flops 589824 | bytes 7077892 | tf_op jit(solution)/shard_map/add | solution.py:624
  143.0 20.0 %attn_bwd.2 = (bf16[2,512,384]{2,1,0:T(8,128)(2,1)S(1)}, bf16[2,512,384]{2,1,0:T(8,128)(2,1)S(1)}, bf16[2,512,384]{2,1,0:T(8,128)(2,1)S(1)}, f32[3,2,768]{2,1,0:T(2,128)S(1)}) custom-call(s32[2,8]{1,0:T(2,128)S(1)} %copy-done.23, bf16[2,512,768]{2,1,0:T(8,128)(2,1)S(1)} %copy-done.51, bf16[2,512,768]{2,1,0:T(8,128)(2,1)S(1)} %copy-done.54, ...), custom_call_target="tpu_custom_call" | custom-call | flops 99999997952 | bytes 1 | tf_op jit(solution)/shard_map/attn_bwd/pallas_call | solution.py:455
  163.1 3.9 attn_wgrad.2
  171.4 3.7 collective-permute-start.10
  182.7 20.1 %attn_bwd.3 = (bf16[2,512,384]{2,1,0:T(8,128)(2,1)S(1)}, bf16[2,512,384]{2,1,0:T(8,128)(2,1)S(1)}, bf16[2,512,384]{2,1,0:T(8,128)(2,1)S(1)}, f32[3,2,768]{2,1,0:T(2,128)S(1)}) custom-call(s32[2,8]{1,0:T(2,128)S(1)} %copy-done.23, bf16[2,512,768]{2,1,0:T(8,128)(2,1)S(1)} %copy-done.52, bf16[2,512,768]{2,1,0:T(8,128)(2,1)S(1)} %copy-done.55, ...), custom_call_target="tpu_custom_call" | custom-call | flops 99999997952 | bytes 1 | tf_op jit(solution)/shard_map/attn_bwd/pallas_call | solution.py:455
  214.4 4.8 %attn_wgrad.3 = (f32[1152,384]{1,0:T(8,128)S(1)}, f32[1152,384]{1,0:T(8,128)}) custom-call(s32[6]{0:T(128)S(1)} %copy-done.9, bf16[1024,768]{1,0:T(8,128)(2,1)S(1)} %bitcast.39, bf16[1024,384]{1,0:T(8,128)(2,1)S(1)} %bitcast.48, bf16[1024,384]{1,0:T(8,128)(2,1)S(1)} %bitcast.50, bf16[1024,384]{1,0:T(8,128)(2,1)S(1)} %bitcast.52, ...), custom_call_target="tpu_custom_call" | custom-call | flops 99999997952 | bytes 1 | tf_op jit(solution)/shard_map/attn_wgrad/pallas_call | solution.py:510
  239.7 6.2 %tokgrad.1 = (bf16[1024,768]{1,0:T(8,128)(2,1)}, f32[1,768]{1,0:T(1,128)S(1)}) custom-call(bf16[1024,768]{1,0:T(8,128)(2,1)S(1)} %bitcast.36, f32[1024,768]{1,0:T(8,128)S(1)} %bitcast.37, f32[2,768]{1,0:T(2,128)S(1)} %copy-done.7, bf16[768,768]{1,0:T(8,128)(2,1)S(1)} %copy-done.17, bf16[768,768]{1,0:T(8,128)(2,1)S(1)} %copy-done.19, ...), custom_call_target="tpu_custom_call" | custom-call | flops 99999997952 | bytes 1 | tf_op jit(solution)/shard_map/tokgrad/pallas_call | solution.py:548
  271.2 9.1 %collective-permute-done.23 = f32[288,256]{1,0:T(8,128)} collective-permute-done((f32[288,256]{1,0:T(8,128)}, f32[288,256]{1,0:T(8,128)}, u32[]{:S(2)}, u32[]{:S(2)}) %collective-permute-start.23) | collective-permute-done | bytes 294944 | tf_op jit(solution)/shard_map/ppermute | solution.py:581
  287.3 5.7 %collective-permute-start.27 = (f32[120,384]{1,0:T(8,128)S(1)}, f32[120,384]{1,0:T(8,128)}, u32[]{:S(2)}, u32[]{:S(2)}) collective-permute-start(f32[120,384]{1,0:T(8,128)S(1)} %copy-done.79), channel_id=1, source_target_pairs={{0,8},{1,9},{2,10},{3,11},{4,12},{5,13},{6,14},{7,15},{8,0},{9,1},... | collective-permute-start | bytes 552968 | tf_op jit(solution)/shard_map/ppermute | solution.py:581
  301.6 9.9 %collective-permute-done.28 = f32[120,384]{1,0:T(8,128)} collective-permute-done((f32[120,384]{1,0:T(8,128)}, f32[120,384]{1,0:T(8,128)}, u32[]{:S(2)}, u32[]{:S(2)}) %collective-permute-start.28) | collective-permute-done | bytes 184352 | tf_op jit(solution)/shard_map/ppermute | solution.py:581
  326.7 4.3 %collective-permute-done.37 = f32[288,384]{1,0:T(8,128)S(1)} collective-permute-done((f32[288,384]{1,0:T(8,128)S(1)}, f32[288,384]{1,0:T(8,128)S(1)}, u32[]{:S(2)}, u32[]{:S(2)}) %collective-permute-start.37) | collective-permute-done | bytes 442400 | tf_op jit(solution)/shard_map/ppermute | solution.py:581
  336.1 4.2 collective-permute-start.33
  341.6 3.7 collective-permute-start.42
  349.3 11.4 %assemble.4 = (f32[768,3072]{1,0:T(8,128)}, f32[3072,768]{1,0:T(8,128)}) custom-call(s32[6]{0:T(128)S(1)} %copy-done.9, f32[2304,256]{1,0:T(8,128)} %pad_maximum_fusion.refs_0_, f32[2304,256]{1,0:T(8,128)} %collective-permute-done.34.refs_1_, f32[2304,256]{1,0:T(8,128)} %collective-permute-done.35.refs_2_, f32[2304,256]{1,0:T(8,128)} %collective-permute-done.36.refs_3_, ...), custom_call_target="tpu_custom_call" | custom-call | flops 99999997952 | bytes 1 | tf_op jit(solution)/shard_map/assemble/pallas_call | solution.py:741
  380.2 9.5 %assemble.5 = (f32[768,3072]{1,0:T(8,128)}, f32[3072,768]{1,0:T(8,128)}) custom-call(s32[6]{0:T(128)S(1)} %copy-done.9, f32[2304,256]{1,0:T(8,128)S(1)} %pad_maximum_fusion.1.refs_0_, f32[2304,256]{1,0:T(8,128)} %collective-permute-done.33.refs_1_.refs_6_, ...), custom_call_target="tpu_custom_call", output_to_operand_aliasing={{0}: (5, {}), {1}: (6, {})} | custom-call | flops 99999997952 | bytes 1 | tf_op jit(solution)/shard_map/assemble/pallas_call | solution.py:741
  391.5 8.5 %collective-permute-done.52.refs_1_.refs_4_ = f32[960,384]{1,0:T(8,128)} collective-permute-done((f32[960,384]{1,0:T(8,128)}, f32[960,384]{1,0:T(8,128)}, u32[]{:S(2)}, u32[]{:S(2)}) %collective-permute-start.52) | collective-permute-done | bytes 1474592 | tf_op jit(solution)/shard_map/ppermute | solution.py:581
  403.5 8.1 %assemble.6 = (f32[768,768]{1,0:T(8,128)}, f32[768,768]{1,0:T(8,128)}, f32[768,768]{1,0:T(8,128)}, f32[768,768]{1,0:T(8,128)}) custom-call(s32[6]{0:T(128)S(1)} %copy-done.9, f32[960,384]{1,0:T(8,128)} %pad_maximum_fusion.2.refs_0_, f32[960,384]{1,0:T(8,128)} %collective-permute-done.52.refs_1_.refs_4_, f32[960,384]{1,0:T(8,128)} %collective-permute-done.53.refs_2_, ...), custom_call_target="tpu_custom_call" | custom-call | flops 99999997952 | bytes 1 | tf_op jit(solution)/shard_map/assemble/pallas_call | solution.py:741
  420.1 4.0 assemble.7
  (332 shorter events, 183.6 us)
Async XLA Ops:
  79.3 30.6 %collective-permute-start.2 = (f32[2304,256]{1,0:T(8,128)}, f32[2304,256]{1,0:T(8,128)}, u32[]{:S(2)}, u32[]{:S(2)}) collective-permute-start(f32[2304,256]{1,0:T(8,128)} %dynamic-slice_add_fusion.1.refs_2_), channel_id=1, source_target_pairs={{0,2},{1,5},{2,0},{3,7},{4,6},{5,1},{6,4},{7,3},{8,10},{9,13},{10,... | collective-permute-start | bytes 7077896 | tf_op jit(solution)/shard_map/ppermute | solution.py:581
  132.7 43.1 %collective-permute-start.7 = (f32[2304,256]{1,0:T(8,128)}, f32[2304,256]{1,0:T(8,128)}, u32[]{:S(2)}, u32[]{:S(2)}) collective-permute-start(f32[2304,256]{1,0:T(8,128)} %dynamic-slice_add_fusion), channel_id=1, source_target_pairs={{0,2},{1,5},{2,0},{3,7},{4,6},{5,1},{6,4},{7,3},{8,10},{9,13},{10,... | collective-permute-start | bytes 7077896 | tf_op jit(solution)/shard_map/ppermute | solution.py:581
  137.1 31.5 %collective-permute-start.4 = (f32[288,256]{1,0:T(8,128)}, f32[288,256]{1,0:T(8,128)}, u32[]{:S(2)}, u32[]{:S(2)}) collective-permute-start(f32[288,256]{1,0:T(8,128)} %get-tuple-element.231.rest_0_), channel_id=1, source_target_pairs={{0,8},{1,9},{2,10},{3,11},{4,12},{5,13},{6,14},{7,15},{8,0},{9,1},... | collective-permute-start | bytes 884744 | tf_op jit(solution)/shard_map/ppermute | solution.py:581
  138.7 30.0 %collective-permute-start.5 = (f32[288,256]{1,0:T(8,128)}, f32[288,256]{1,0:T(8,128)}, u32[]{:S(2)}, u32[]{:S(2)}) collective-permute-start(f32[288,256]{1,0:T(8,128)} %get-tuple-element.230.rest_1_), channel_id=1, source_target_pairs={{0,16},{1,17},{2,18},{3,19},{4,20},{5,21},{6,22},{7,23},{8,24},{9,... | collective-permute-start | bytes 884744 | tf_op jit(solution)/shard_map/ppermute | solution.py:581
  141.3 27.4 %collective-permute-start.6 = (f32[288,256]{1,0:T(8,128)}, f32[288,256]{1,0:T(8,128)}, u32[]{:S(2)}, u32[]{:S(2)}) collective-permute-start(f32[288,256]{1,0:T(8,128)} %get-tuple-element.229.rest_2_), channel_id=1, source_target_pairs={{0,24},{1,25},{2,26},{3,27},{4,28},{5,29},{6,30},{7,31},{8,16},{9,... | collective-permute-start | bytes 884744 | tf_op jit(solution)/shard_map/ppermute | solution.py:581
  168.7 43.2 %collective-permute-start.12 = (f32[1920,384]{1,0:T(8,128)}, f32[1920,384]{1,0:T(8,128)}, u32[]{:S(2)}, u32[]{:S(2)}) collective-permute-start(f32[1920,384]{1,0:T(8,128)} %copy-done.10), channel_id=1, source_target_pairs={{0,1},{1,0},{2,3},{3,2},{4,5},{5,4},{6,7},{7,6},{8,9},{9,8},{10,11... | collective-permute-start | bytes 8847368 | tf_op jit(solution)/shard_map/ppermute | solution.py:585
  171.4 34.0 %collective-permute-start.10 = (f32[288,256]{1,0:T(8,128)S(1)}, f32[288,256]{1,0:T(8,128)}, u32[]{:S(2)}, u32[]{:S(2)}) collective-permute-start(f32[288,256]{1,0:T(8,128)S(1)} %add_add_fusion.1), channel_id=1, source_target_pairs={{0,24},{1,25},{2,26},{3,27},{4,28},{5,29},{6,30},{7,31},{8,16},{9,... | collective-permute-start | bytes 884744 | tf_op jit(solution)/shard_map/ppermute | solution.py:581
  175.1 30.3 %collective-permute-start.8 = (f32[288,256]{1,0:T(8,128)S(1)}, f32[288,256]{1,0:T(8,128)}, u32[]{:S(2)}, u32[]{:S(2)}) collective-permute-start(f32[288,256]{1,0:T(8,128)S(1)} %add_add_fusion.1), channel_id=1, source_target_pairs={{0,16},{1,17},{2,18},{3,19},{4,20},{5,21},{6,22},{7,23},{8,24},{9,... | collective-permute-start | bytes 884744 | tf_op jit(solution)/shard_map/ppermute | solution.py:581
  175.1 30.3 %collective-permute-start.9 = (f32[288,256]{1,0:T(8,128)S(1)}, f32[288,256]{1,0:T(8,128)}, u32[]{:S(2)}, u32[]{:S(2)}) collective-permute-start(f32[288,256]{1,0:T(8,128)S(1)} %add_add_fusion.1), channel_id=1, source_target_pairs={{0,8},{1,9},{2,10},{3,11},{4,12},{5,13},{6,14},{7,15},{8,0},{9,1},... | collective-permute-start | bytes 884744 | tf_op jit(solution)/shard_map/ppermute | solution.py:581
  179.2 29.6 %collective-permute-start.11 = (f32[1152,256]{1,0:T(8,128)}, f32[1152,256]{1,0:T(8,128)}, u32[]{:S(2)}, u32[]{:S(2)}) collective-permute-start(f32[1152,256]{1,0:T(8,128)} %dynamic-slice_add_fusion.3.rest_0_), channel_id=1, source_target_pairs={{0,4},{1,3},{2,6},{3,1},{4,0},{5,7},{6,2},{7,5},{8,12},{9,11},{10,... | collective-permute-start | bytes 3538952 | tf_op jit(solution)/shard_map/ppermute | solution.py:581
  219.3 42.2 %collective-permute-start.20 = (f32[1152,256]{1,0:T(8,128)}, f32[1152,256]{1,0:T(8,128)}, u32[]{:S(2)}, u32[]{:S(2)}) collective-permute-start(f32[1152,256]{1,0:T(8,128)} %pad_maximum_fusion.3), channel_id=1, source_target_pairs={{0,4},{1,3},{2,6},{3,1},{4,0},{5,7},{6,2},{7,5},{8,12},{9,11},{10,... | collective-permute-start | bytes 3538952 | tf_op jit(solution)/shard_map/ppermute | solution.py:581
  221.6 26.9 %collective-permute-start.15 = (f32[288,256]{1,0:T(8,128)}, f32[288,256]{1,0:T(8,128)S(1)}, u32[]{:S(2)}, u32[]{:S(2)}) collective-permute-start(f32[288,256]{1,0:T(8,128)} %get-tuple-element.228), channel_id=1, source_target_pairs={{0,8},{1,9},{2,10},{3,11},{4,12},{5,13},{6,14},{7,15},{8,0},{9,1},... | collective-permute-start | bytes 884744 | tf_op jit(solution)/shard_map/ppermute | solution.py:581
  223.0 26.8 %collective-permute-start.16 = (f32[288,256]{1,0:T(8,128)}, f32[288,256]{1,0:T(8,128)S(1)}, u32[]{:S(2)}, u32[]{:S(2)}) collective-permute-start(f32[288,256]{1,0:T(8,128)} %get-tuple-element.227), channel_id=1, source_target_pairs={{0,16},{1,17},{2,18},{3,19},{4,20},{5,21},{6,22},{7,23},{8,24},{9,... | collective-permute-start | bytes 884744 | tf_op jit(solution)/shard_map/ppermute | solution.py:581
  225.9 23.9 %collective-permute-start.17 = (f32[288,256]{1,0:T(8,128)}, f32[288,256]{1,0:T(8,128)}, u32[]{:S(2)}, u32[]{:S(2)}) collective-permute-start(f32[288,256]{1,0:T(8,128)} %get-tuple-element.226), channel_id=1, source_target_pairs={{0,24},{1,25},{2,26},{3,27},{4,28},{5,29},{6,30},{7,31},{8,16},{9,... | collective-permute-start | bytes 884744 | tf_op jit(solution)/shard_map/ppermute | solution.py:581
  226.1 26.8 %collective-permute-start.19 = (f32[960,384]{1,0:T(8,128)}, f32[960,384]{1,0:T(8,128)}, u32[]{:S(2)}, u32[]{:S(2)}) collective-permute-start(f32[960,384]{1,0:T(8,128)} %copy-done.3), channel_id=1, source_target_pairs={{0,2},{1,5},{2,0},{3,7},{4,6},{5,1},{6,4},{7,3},{8,10},{9,13},{10,... | collective-permute-start | bytes 4423688 | tf_op jit(solution)/shard_map/ppermute | solution.py:581
  257.2 23.0 %collective-permute-start.23 = (f32[288,256]{1,0:T(8,128)}, f32[288,256]{1,0:T(8,128)}, u32[]{:S(2)}, u32[]{:S(2)}) collective-permute-start(f32[288,256]{1,0:T(8,128)} %add_add_fusion), channel_id=1, source_target_pairs={{0,16},{1,17},{2,18},{3,19},{4,20},{5,21},{6,22},{7,23},{8,24},{9,... | collective-permute-start | bytes 884744 | tf_op jit(solution)/shard_map/ppermute | solution.py:581
  265.1 56.8 %collective-permute-start.34 = (f32[2304,256]{1,0:T(8,128)}, f32[2304,256]{1,0:T(8,128)}, u32[]{:S(2)}, u32[]{:S(2)}) collective-permute-start(f32[2304,256]{1,0:T(8,128)} %pad_maximum_fusion.refs_0_), channel_id=1, source_target_pairs={{0,2},{1,5},{2,0},{3,7},{4,6},{5,1},{6,4},{7,3},{8,10},{9,13},{10,... | collective-permute-start | bytes 7077896 | tf_op jit(solution)/shard_map/ppermute | solution.py:581
  283.4 36.8 %collective-permute-start.32 = (f32[1152,256]{1,0:T(8,128)}, f32[1152,256]{1,0:T(8,128)}, u32[]{:S(2)}, u32[]{:S(2)}) collective-permute-start(f32[1152,256]{1,0:T(8,128)} %pad_maximum_fusion.4), channel_id=1, source_target_pairs={{0,4},{1,3},{2,6},{3,1},{4,0},{5,7},{6,2},{7,5},{8,12},{9,11},{10,... | collective-permute-start | bytes 3538952 | tf_op jit(solution)/shard_map/ppermute | solution.py:581
  285.7 31.1 %collective-permute-start.30 = (f32[576,384]{1,0:T(8,128)}, f32[576,384]{1,0:T(8,128)}, u32[]{:S(2)}, u32[]{:S(2)}) collective-permute-start(f32[576,384]{1,0:T(8,128)} %dynamic-slice_add_fusion.5), channel_id=1, source_target_pairs={{0,2},{1,5},{2,0},{3,7},{4,6},{5,1},{6,4},{7,3},{8,10},{9,13},{10,... | collective-permute-start | bytes 2654216 | tf_op jit(solution)/shard_map/ppermute | solution.py:581
  311.5 35.1 %collective-permute-start.35 = (f32[2304,256]{1,0:T(8,128)}, f32[2304,256]{1,0:T(8,128)}, u32[]{:S(2)}, u32[]{:S(2)}) collective-permute-start(f32[2304,256]{1,0:T(8,128)} %pad_maximum_fusion.refs_0_), channel_id=1, source_target_pairs={{0,1},{1,0},{2,3},{3,2},{4,5},{5,4},{6,7},{7,6},{8,9},{9,8},{10,11... | collective-permute-start | bytes 7077896 | tf_op jit(solution)/shard_map/ppermute | solution.py:585
  321.9 26.0 %collective-permute-start.36 = (f32[2304,256]{1,0:T(8,128)}, f32[2304,256]{1,0:T(8,128)}, u32[]{:S(2)}, u32[]{:S(2)}) collective-permute-start(f32[2304,256]{1,0:T(8,128)} %collective-permute-done.34.refs_1_), channel_id=1, source_target_pairs={{0,1},{1,0},{2,3},{3,2},{4,5},{5,4},{6,7},{7,6},{8,9},{9,8},{10,11... | collective-permute-start | bytes 7077896 | tf_op jit(solution)/shard_map/ppermute | solution.py:585
  336.1 39.3 %collective-permute-start.33 = (f32[2304,256]{1,0:T(8,128)S(1)}, f32[2304,256]{1,0:T(8,128)}, u32[]{:S(2)}, u32[]{:S(2)}) collective-permute-start(f32[2304,256]{1,0:T(8,128)S(1)} %pad_maximum_fusion.1.refs_0_), channel_id=1, source_target_pairs={{0,2},{1,5},{2,0},{3,7},{4,6},{5,1},{6,4},{7,3},{8,10},{9,13},{10,... | collective-permute-start | bytes 7077896 | tf_op jit(solution)/shard_map/ppermute | solution.py:581
  375.5 24.5 %collective-permute-start.52 = (f32[960,384]{1,0:T(8,128)}, f32[960,384]{1,0:T(8,128)}, u32[]{:S(2)}, u32[]{:S(2)}) collective-permute-start(f32[960,384]{1,0:T(8,128)} %pad_maximum_fusion.2.refs_0_), channel_id=1, source_target_pairs={{0,2},{1,5},{2,0},{3,7},{4,6},{5,1},{6,4},{7,3},{8,10},{9,13},{10,... | collective-permute-start | bytes 4423688 | tf_op jit(solution)/shard_map/ppermute | solution.py:581
  377.1 24.4 %collective-permute-start.53 = (f32[960,384]{1,0:T(8,128)}, f32[960,384]{1,0:T(8,128)}, u32[]{:S(2)}, u32[]{:S(2)}) collective-permute-start(f32[960,384]{1,0:T(8,128)} %pad_maximum_fusion.2.refs_0_), channel_id=1, source_target_pairs={{0,1},{1,0},{2,3},{3,2},{4,5},{5,4},{6,7},{7,6},{8,9},{9,8},{10,11... | collective-permute-start | bytes 4423688 | tf_op jit(solution)/shard_map/ppermute | solution.py:585
  (118 other events, 1142.3 us)

commit v3 on v2

v3 whole, which is shorter than its diff:
```python
import functools
import jax
import jax.numpy as jnp
import numpy as np
from jax import lax
from jax.experimental import pallas as pl
from jax.experimental.pallas import tpu as pltpu
from jax.sharding import PartitionSpec as P

NT = (((1,), (1,)), ((), ()))
TN = (((0,), (0,)), ((), ()))
F32, BF16 = jnp.float32, jnp.bfloat16
TILE = 128
MASKED = -1000000000.0
EPS = 1e-06
far_steps = np.array([12, 16, 23, 32, 46, 64, 91], dtype=np.int32)


def dot(a, b, dims=None):
    if dims is None:
        return jnp.dot(a, b, preferred_element_type=F32)
    return lax.dot_general(a, b, dims, preferred_element_type=F32)


def bucket_of(relative, bucket_count):
    distance = np.abs(relative)
    beyond = np.sum(distance[..., None] >= far_steps, axis=-1)
    inner = np.where(distance < bucket_count // 4, distance, bucket_count // 4 + beyond)
    return np.where(relative > 0, bucket_count // 2, 0) + inner


def band_buckets(bucket_count):
    lanes = np.arange(4 * TILE)
    offsets = np.where(lanes < 2 * TILE, lanes, lanes - 4 * TILE)
    return bucket_of(-offsets, bucket_count)


def segments_along(len_ref, row, shape, axis, start=0):
    at = lax.broadcasted_iota(jnp.int32, shape, axis) + start
    total = jnp.zeros(shape, jnp.int32)
    end = jnp.int32(0)
    for j in range(len_ref.shape[1]):
        end = end + len_ref[row, j]
        total = total + jnp.where(at >= end, 1, 0)
    return total


def fill_mask(len_ref, row, mask_ref, last):
    seq = mask_ref.shape[0]
    of_q = segments_along(len_ref, row, (1, seq), 1)
    of_k = segments_along(len_ref, row, (seq, TILE), 0)
    of_k = jnp.where(of_k < last, of_k, -1)
    for j in range(seq // TILE):
        same = of_k == of_q[:, j * TILE : (j + 1) * TILE]
        mask_ref[:, j * TILE : (j + 1) * TILE] = jnp.where(same, 0.0, MASKED)
    return of_q < last


def band_of(vector):
    wide = jnp.broadcast_to(vector, (TILE, 4 * TILE))
    return pltpu.roll(wide, 0, 1, stride=1, stride_axis=0)


def bias_row(band, vector, ki, count):
    shape = (TILE, TILE)
    tiles = []
    for qi in range(count):
        step = ki - qi
        if step == 0:
            tiles.append(band[:, 0:TILE])
        elif step == -1:
            tiles.append(band[:, TILE : 2 * TILE])
        elif step == 1:
            tiles.append(band[:, 3 * TILE : 4 * TILE])
        elif step < 0:
            tiles.append(jnp.broadcast_to(vector[:, 2 * TILE - 1 : 2 * TILE], shape))
        else:
            tiles.append(jnp.broadcast_to(vector[:, 2 * TILE : 2 * TILE + 1], shape))
    return jnp.concatenate(tiles, axis=1)


def norm_scale(value):
    return lax.rsqrt(jnp.mean(value * value, axis=-1, keepdims=True) + EPS)


def row_of(gain_ref):
    return gain_ref[...].astype(F32).reshape(1, gain_ref.shape[0])


VMEM = 63 * 2**20
ANYWHERE = pl.BlockSpec(memory_space=pl.ANY)
FLOPS = 10**11
LITTLE = pl.CostEstimate(flops=1, transcendentals=0, bytes_accessed=1)
COST = pl.CostEstimate(flops=FLOPS, transcendentals=0, bytes_accessed=1)


def params(limit=VMEM):
    return pltpu.CompilerParams(vmem_limit_bytes=limit)


def attn_fwd_kernel(
    len_ref, tok_ref, gain1_ref, gain2_ref, wq_ref, wk_ref, wv_ref, wo_ref, band_ref,
    h1T_ref, q_ref, k_ref, v_ref, attT_ref, lse_ref, x1_ref, h2_ref,
    att_ref, mask_ref, s_ref, p_ref,
):
    seq, width = tok_ref.shape[1:]
    pairs = width // TILE
    head = TILE // 2
    row = pl.program_id(0)
    valid = fill_mask(len_ref, row, mask_ref, len_ref.shape[1] - 1)
    tok = tok_ref[0].astype(F32)
    h1 = (tok * norm_scale(tok) * row_of(gain1_ref)).astype(BF16)
    h1T_ref[0] = h1.T
    q_ref[0] = dot(h1, wq_ref[...]).astype(BF16)
    k_ref[0] = dot(h1, wk_ref[...]).astype(BF16)
    v_ref[0] = dot(h1, wv_ref[...]).astype(BF16)
    count = seq // TILE
    low_half = lax.broadcasted_iota(jnp.int32, (1, TILE), 1) < head

    def pair(p, carry):
        lanes = pl.ds(pl.multiple_of(p * TILE, TILE), TILE)
        qp, kp, vp = q_ref[0, :, lanes], k_ref[0, :, lanes], v_ref[0, :, lanes]
        vT = vp.T
        tops = []
        for a in range(2):
            qm = jnp.where(low_half if a == 0 else ~low_half, qp, jnp.zeros_like(qp))
            vector = band_ref[pl.ds(2 * p + a, 1), :]
            band = band_of(vector)
            top = None
            for ki in range(count):
                rows = slice(ki * TILE, (ki + 1) * TILE)
                s = dot(kp[rows], qm, NT) + bias_row(band, vector, ki, count) + mask_ref[rows, :]
                s_ref[a, rows, :] = s
                most = jnp.max(s, axis=0, keepdims=True)
                top = most if top is None else jnp.maximum(top, most)
            tops.append(top)
        totals = []
        for a, top in enumerate(tops):
            total = jnp.zeros_like(top)
            for ki in range(count):
                rows = slice(ki * TILE, (ki + 1) * TILE)
                e = jnp.exp(s_ref[a, rows, :] - top)
                total = total + jnp.sum(e, axis=0, keepdims=True)
                p_ref[a, rows, :] = e.astype(BF16)
            totals.append(total)
        outs = []
        for a, (top, total) in enumerate(zip(tops, totals)):
            o = dot(vT[a * head : (a + 1) * head], p_ref[a])
            outs.append(jnp.where(valid, o / total, 0.0))
            lse_ref[0, pl.ds(2 * p + a, 1), :] = top + jnp.log(total)
        both = jnp.concatenate(outs, axis=0)
        attT_ref[0, lanes, :] = both.astype(BF16)
        att_ref[:, lanes] = both.T.astype(BF16)
        return carry

    lax.fori_loop(0, pairs, pair, 0, unroll=6)
    x1 = tok_ref[0].astype(F32) + dot(att_ref[...], wo_ref[...])
    x1_ref[0] = x1
    h2_ref[0] = (x1 * norm_scale(x1) * row_of(gain2_ref)).astype(BF16)


def attn_fwd(tokens, lengths, gain1, gain2, wq, wk, wv, wo, band):
    rows, seq, width = tokens.shape
    heads = band.shape[0]
    full = lambda a: pl.BlockSpec(a.shape, lambda r, l: (0,) * a.ndim, pipeline_mode=pl.Buffered(1))
    per_row = lambda *s: pl.BlockSpec((1,) + s, lambda r, l: (r,) + (0,) * len(s))
    tall = jax.ShapeDtypeStruct((rows, seq, width), BF16)
    turned = jax.ShapeDtypeStruct((rows, width, seq), BF16)
    return pl.pallas_call(
        attn_fwd_kernel,
        grid_spec=pltpu.PrefetchScalarGridSpec(
            num_scalar_prefetch=1,
            grid=(rows,),
            in_specs=[per_row(seq, width)] + [full(a) for a in (gain1, gain2, wq, wk, wv, wo, band)],
            out_specs=[per_row(width, seq)]
            + [per_row(seq, width)] * 3
            + [per_row(width, seq), per_row(heads, seq), per_row(seq, width), per_row(seq, width)],
            scratch_shapes=[
                pltpu.VMEM((seq, width), BF16),
                pltpu.VMEM((seq, seq), F32),
                pltpu.VMEM((2, seq, seq), F32),
                pltpu.VMEM((2, seq, seq), BF16),
            ],
        ),
        out_shape=[turned, tall, tall, tall, turned]
        + [jax.ShapeDtypeStruct((rows, heads, seq), F32), jax.ShapeDtypeStruct((rows, seq, width), F32), tall],
        cost_estimate=COST,
        compiler_params=params(),
        name="attn_fwd",
    )(lengths, tokens, gain1, gain2, wq, wk, wv, wo, band)


GELU_C = float(np.sqrt(2.0 / np.pi))


def gelu_pair(v):
    v2 = v * v
    t = jnp.tanh(GELU_C * v * (1.0 + 0.044715 * v2))
    half = 0.5 * (1.0 + t)
    slope = half + (0.5 * GELU_C) * v * (1.0 - t * t) * (1.0 + (3 * 0.044715) * v2)
    return v * half, slope


def place(core, mine, other, keep, send, sems):
    both = lambda a, b: [(src, dst, sems.at[n, i]) for n, pairs in enumerate((a, b)) for i, (src, dst) in enumerate(pairs)]
    return [(core == 0, both(mine(keep), other(send))), (core != 0, both(mine(send), other(keep)))]


def run_all(cases, action):
    for condition, copies in cases:

        @pl.when(condition)
        def _():
            for src, dst, sem in copies:
                getattr(pltpu.make_async_copy(src, dst, sem), action)()


def ffn_kernel(steps, slabs, first, last, info_ref, len_ref, h2_ref, dy_ref, win_ref, wout_ref, *refs):
    refs = list(refs)
    acc_in = [] if first else [refs.pop(0), refs.pop(0)]
    if last:
        x1_ref, gain_ref, attT_ref, wo_ref = refs[:4]
        keep_ref, send_ref, mixed_out, dres_out, datt_out, gwo_ref, ggain_ref = refs[-19:-12]
        mix_ref, dtwo_ref, h2T_ref, act_ref, dpre_ref, gin_ref, gout_ref, sems, acc_sems, mixed_ref, dres_ref, datt_ref = refs[-12:]
    else:
        keep_ref, send_ref = refs[-13:-11]
        acc_out = refs[-11:-9]
        mix_ref, dtwo_ref, h2T_ref, act_ref, dpre_ref, gin_ref, gout_ref, sems, acc_sems = refs[-9:]
    step = pl.program_id(0)
    toks, width = h2_ref.shape
    sub = win_ref.shape[1]
    wide, tall = width // 256, sub // 256
    in_rows, out_rows = width // slabs, sub * steps // slabs
    piece = in_rows * tall * steps
    here = slabs // steps
    totals = (mix_ref, dtwo_ref)

    def moves(at):
        def of_in(ref):
            return [
                (
                    gin_ref.at[at, i * in_rows * tall : (i + 1) * in_rows * tall, :],
                    ref.at[pl.ds(pl.multiple_of(i * piece + at * (in_rows * tall), 8), in_rows * tall), :],
                )
                for i in range(slabs)
            ]

        def of_out(ref):
            return [(gout_ref.at[at], ref.at[pl.ds(pl.multiple_of(at * (here * piece), 8), here * piece), :])]

        return place(info_ref[0], of_in, of_out, keep_ref, send_ref, sems.at[at])

    @pl.when(step == 0)
    def _():
        for i, ref in enumerate(acc_in):
            pltpu.make_async_copy(ref, totals[i], acc_sems.at[i]).start()
        h2T_ref[...] = h2_ref[...].T

    for c in range(0, sub, 256):
        cols = slice(c, c + 256)
        pre = dot(h2_ref[...], win_ref[:, cols])
        dact = dot(dy_ref[...], wout_ref[cols, :], NT)
        act, slope = gelu_pair(pre)
        act_ref[:, cols] = act.astype(BF16)
        dpre_ref[:, cols] = (dact * slope).astype(BF16)
    mix = dot(act_ref[...], wout_ref[...])
    dtwo = dot(dpre_ref[...], win_ref[...], NT)

    @pl.when(step == 0)
    def _():
        if first:
            mix_ref[...] = mix
            dtwo_ref[...] = dtwo
        else:
            for i, ref in enumerate(acc_in):
                pltpu.make_async_copy(ref, totals[i], acc_sems.at[i]).wait()
            mix_ref[...] += mix
            dtwo_ref[...] += dtwo

    @pl.when(step > 0)
    def _():
        mix_ref[...] += mix
        dtwo_ref[...] += dtwo

    if not last:

        @pl.when(step == steps - 1)
        def _():
            for i in range(2):
                pltpu.make_async_copy(totals[i], acc_out[i], acc_sems.at[2 + i]).start()

    gout = dot(act_ref[...], dy_ref[...], TN)
    for i in range(here):
        for j in range(wide):
            at = (i * wide + j) * out_rows
            gout_ref[step, at : at + out_rows, :] = gout[i * out_rows : (i + 1) * out_rows, j * 256 : (j + 1) * 256]
    gin = dot(h2T_ref[...], dpre_ref[...])
    for i in range(slabs):
        for j in range(tall):
            at = (i * tall + j) * in_rows
            gin_ref[step, at : at + in_rows, :] = gin[i * in_rows : (i + 1) * in_rows, j * 256 : (j + 1) * 256]
    run_all(moves(step), "start")

    @pl.when(step == steps - 1)
    def _():
        if last:
            rows = len_ref.shape[0]
            seq = toks // rows
            block = 256
            copies = []
            ggain = None
            for b in range(toks // block):
                here_toks = slice(b * block, (b + 1) * block)
                x1, back = x1_ref[here_toks, :], dtwo_ref[here_toks, :]
                mixed_ref[here_toks, :] = (x1 + mix_ref[here_toks, :]).astype(BF16)
                s = norm_scale(x1)
                g = row_of(gain_ref) * back
                dres = dy_ref[here_toks, :].astype(F32) + s * g - x1 * (s * s * s * jnp.mean(x1 * g, axis=-1, keepdims=True))
                dres_ref[here_toks, :] = dres
                some = jnp.sum(back * x1 * s, axis=0, keepdims=True)
                ggain = some if ggain is None else ggain + some
                dbranch = dres.astype(BF16)
                act_ref[here_toks, :] = dbranch
                datt = dot(dbranch, wo_ref[...], NT)
                seg = segments_along(len_ref, b * block // seq, (block, TILE), 0, b * block % seq)[:, :1]
                datt_ref[here_toks, :] = jnp.where(seg < len_ref.shape[1] - 1, datt, 0.0).astype(BF16)
                for n, (src, dst) in enumerate(((mixed_ref, mixed_out), (dres_ref, dres_out), (datt_ref, datt_out))):
                    copies.append(pltpu.make_async_copy(src.at[here_toks, :], dst.at[here_toks, :], acc_sems.at[4 + 3 * b + n]))
                    copies[-1].start()
            ggain_ref[...] = ggain
            gwo = None
            for r in range(rows):
                part = dot(attT_ref[r], act_ref[r * seq : (r + 1) * seq, :])
                gwo = part if gwo is None else gwo + part
            gwo_ref[...] = gwo
            for copy in copies:
                copy.wait()
        else:
            for i in range(2):
                pltpu.make_async_copy(totals[i], acc_out[i], acc_sems.at[2 + i]).wait()
        for at in range(steps):
            run_all(moves(at), "wait")


def ffn_chunk(info, lengths, slabs, h2, dy, w_in, w_out, start, size, sub, acc, after, rest=None):
    toks, width = h2.shape
    base = start // sub
    steps = size // sub
    piece = width * (sub // 256)
    full = lambda a: pl.BlockSpec(a.shape, lambda s, *_: (0,) * a.ndim, pipeline_mode=pl.Buffered(1))
    f32 = lambda *s: jax.ShapeDtypeStruct(s, F32)
    out_specs = [ANYWHERE] * 2
    out_shape = [f32(steps * piece, 256)] * 2
    scratch = [
        pltpu.VMEM((toks, width), F32),
        pltpu.VMEM((toks, width), F32),
        pltpu.VMEM((width, toks), BF16),
        pltpu.VMEM((toks, sub), BF16),
        pltpu.VMEM((toks, sub), BF16),
        pltpu.VMEM((steps, piece, 256), F32),
        pltpu.VMEM((steps, piece, 256), F32),
        pltpu.SemaphoreType.DMA((steps, 2, slabs)),
        pltpu.SemaphoreType.DMA((4 + 3 * (toks // 256),)),
    ]
    if rest is None:
        rest = ()
        out_specs += [ANYWHERE] * 2
        out_shape += [f32(toks, width)] * 2
    else:
        low = jax.ShapeDtypeStruct((toks, width), BF16)
        whole = lambda s: pl.BlockSpec(s.shape, lambda *_: (0,) * len(s.shape), pipeline_mode=pl.Buffered(1))
        gwo, ggain = f32(width, width), f32(1, width)
        out_specs += [ANYWHERE] * 3 + [whole(gwo), whole(ggain)]
        out_shape += [low, f32(toks, width), low, gwo, ggain]
        scratch += [pltpu.VMEM((toks, width), BF16), pltpu.VMEM((toks, width), F32), pltpu.VMEM((toks, width), BF16)]
    return pl.pallas_call(
        functools.partial(ffn_kernel, steps, slabs, not acc, bool(rest)),
        grid_spec=pltpu.PrefetchScalarGridSpec(
            num_scalar_prefetch=2,
            grid=(steps,),
            in_specs=[
                full(h2),
                full(dy),
                pl.BlockSpec((width, sub), lambda s, *_: (0, base + s)),
                pl.BlockSpec((sub, width), lambda s, *_: (base + s, 0)),
            ]
            + [ANYWHERE] * len(acc)
            + [full(a) for a in rest]
            + [ANYWHERE] * len(after),
            out_specs=out_specs,
            scratch_shapes=scratch,
        ),
        out_shape=out_shape,
        cost_estimate=COST,
        compiler_params=params(),
        name="ffn",
    )(info, lengths, h2, dy, w_in, w_out, *acc, *rest, *after)


def diagonal_sums(x):
    depth, lanes = x.shape
    total = x[0:8]
    for g in range(8, depth, 8):
        total = total + pltpu.roll(x[g : g + 8], lanes - g, 1)
    at = lax.broadcasted_iota(jnp.int32, (8, lanes), 0)
    for bit in (1, 2, 4):
        total = jnp.where((at & bit) != 0, pltpu.roll(total, lanes - bit, 1), total)
    return jnp.sum(total, axis=0, keepdims=True)


def attn_bwd_kernel(slabs, first, n_more, info_ref, len_ref, q_ref, k_ref, v_ref, do_ref, lse_ref, band_ref, h1T_ref, *refs):
    more = refs[:n_more]
    dq_ref, dk_ref, dv_ref, diag_ref, keep_ref, send_ref = refs[-14:-8]
    mask_ref, p_ref, low_ref, dp_ref, ds_ref, d_ref, g_ref, sems = refs[-8:]
    pair, pairs = pl.program_id(0), pl.num_programs(0)
    rows, seq = q_ref.shape[:2]
    head = TILE // 2
    count = seq // TILE
    width, cols = h1T_ref.shape[1], g_ref.shape[2]
    stripes = keep_ref.shape[0] * 2 // width
    share = width // 2 // slabs

    def put(j, block):
        for c in range(2):
            for s in range(slabs):
                at, begin = (s * stripes + j) * share, (c * slabs + s) * share
                g_ref[c, at : at + share, :] = block[begin : begin + share]

    @pl.when(pair == 0)
    def _():
        for row in range(rows):
            fill_mask(len_ref, row, mask_ref.at[row], len_ref.shape[1] - 1)

    low_half = lax.broadcasted_iota(jnp.int32, (1, TILE), 1) < head
    bands = []
    for a in range(2):
        vector = band_ref[pl.ds(2 * (first + pair) + a, 1), :]
        bands.append((vector, band_of(vector)))
    sides = []
    for n in range(2 * rows):
        row, a = n // 2, n % 2
        qp, kp, vp, dop = q_ref[row], k_ref[row], v_ref[row], do_ref[row]
        own = low_half if a == 0 else ~low_half
        qm = jnp.where(own, qp, jnp.zeros_like(qp))
        dom = jnp.where(own, dop, jnp.zeros_like(dop))
        vector, band = bands[a]
        lse = lse_ref[row, pl.ds(2 * (first + pair) + a, 1), :]
        delta = jnp.zeros((1, seq), F32)
        for ki in range(count):
            some = slice(ki * TILE, (ki + 1) * TILE)
            s = dot(kp[some], qm, NT) + bias_row(band, vector, ki, count) + mask_ref[row, some, :]
            prob = jnp.exp(s - lse)
            dp = dot(vp[some], dom, NT)
            delta = delta + jnp.sum(prob * dp, axis=0, keepdims=True)
            p_ref[n, some, :] = prob
            low_ref[n, some, :] = prob.astype(BF16)
            dp_ref[n, some, :] = dp
        sides.append((qm, dom, delta))
    sums = [{}, {}]
    for n, (_, _, delta) in enumerate(sides):
        near = sums[n % 2]
        for ki in range(count):
            some = slice(ki * TILE, (ki + 1) * TILE)
            ds = p_ref[n, some, :] * (dp_ref[n, some, :] - delta)
            ds_ref[n, some, :] = ds.astype(BF16)
            for qi in range(count):
                step = max(-2, min(2, ki - qi))
                tile = ds[:, qi * TILE : (qi + 1) * TILE]
                near[step] = tile if step not in near else near[step] + tile
    for a, near in enumerate(sums):
        zero = jnp.zeros((TILE, TILE), F32)
        band = jnp.concatenate([near[0], near[-1], zero, near[1]], axis=1)
        diag_ref[0, a : a + 1, : 4 * TILE] = diagonal_sums(band)
        ends = jnp.concatenate([near[-2], near[2]], axis=1)
        diag_ref[0, a : a + 1, 4 * TILE :] = jnp.sum(ends, axis=0, keepdims=True)
    lanes = pl.ds(pl.multiple_of(pair * TILE, TILE), TILE)
    for row in range(rows):
        kT = k_ref[row].T
        dqT, dk, dv = [], None, None
        for a in range(2):
            n = 2 * row + a
            qm, dom, _ = sides[n]
            dva = dot(low_ref[n], dom)
            dka = dot(ds_ref[n], qm)
            dv = dva if dv is None else dv + dva
            dk = dka if dk is None else dk + dka
            dqT.append(dot(kT[a * head : (a + 1) * head], ds_ref[n]))
        dq = jnp.concatenate(dqT, axis=0).T.astype(BF16)
        dk, dv = dk.astype(BF16), dv.astype(BF16)
        dq_ref[row], dk_ref[row], dv_ref[row] = dq, dk, dv
        for j, d in enumerate((dq, dk, dv)):
            d_ref[j, row, :, lanes] = d

    @pl.when(pair == pairs - 1)
    def _():
        for j in range(3):
            g = None
            for r in range(h1T_ref.shape[0]):
                part = dot(h1T_ref[r], d_ref[j, r])
                g = part if g is None else g + part
            put(j, g)
        for j in range(stripes - 3):
            put(3 + j, more[0][:, j * cols : (j + 1) * cols])
        moves = place(
            info_ref[0], lambda ref: [(g_ref.at[0], ref)], lambda ref: [(g_ref.at[1], ref)], keep_ref, send_ref, sems
        )
        run_all(moves, "start")
        run_all(moves, "wait")


def attn_bwd(info, lengths, slabs, q, k, v, do, lse, band, h1T, first, pairs, more, after):
    rows, seq, width = q.shape
    cols = pairs * TILE
    half = width // 2 * (3 + sum(m.shape[1] // cols for m in more))
    tall = pl.BlockSpec((rows, seq, TILE), lambda p, *_: (0, 0, first + p))
    tall_out = pl.BlockSpec((rows, seq, TILE), lambda p, *_: (0, 0, p))
    full = lambda a: pl.BlockSpec(a.shape, lambda *_: (0,) * a.ndim, pipeline_mode=pl.Buffered(1))
    out = jax.ShapeDtypeStruct((rows, seq, cols), BF16)
    square = lambda dtype: pltpu.VMEM((2 * rows, seq, seq), dtype)
    return pl.pallas_call(
        functools.partial(attn_bwd_kernel, slabs, first, len(more)),
        grid_spec=pltpu.PrefetchScalarGridSpec(
            num_scalar_prefetch=2,
            grid=(pairs,),
            in_specs=[tall] * 4
            + [full(lse), full(band), full(h1T)]
            + [full(m) for m in more]
            + [ANYWHERE] * len(after),
            out_specs=[tall_out] * 3 + [pl.BlockSpec((1, 2, 6 * TILE), lambda p, *_: (p, 0, 0))] + [ANYWHERE] * 2,
            scratch_shapes=[
                pltpu.VMEM((rows, seq, seq), F32),
                square(F32),
                square(BF16),
                square(F32),
                square(BF16),
                pltpu.VMEM((3, rows, seq, cols), BF16),
                pltpu.VMEM((2, half, cols), F32),
                pltpu.SemaphoreType.DMA((2, 1)),
            ],
        ),
        out_shape=[out] * 3
        + [jax.ShapeDtypeStruct((pairs, 2, 6 * TILE), F32)]
        + [jax.ShapeDtypeStruct((half, cols), F32)] * 2,
        cost_estimate=COST,
        compiler_params=params(),
        name="attn_bwd",
    )(info, lengths, q, k, v, do, lse, band, h1T, *more, *after)


def tokgrad_kernel(halves, tok_ref, dres_ref, gain_ref, wq_ref, wk_ref, wv_ref, *refs):
    out_ref, ggain_ref = refs[-2:]
    step = pl.program_id(0)
    done = None
    for i, w in enumerate((wq_ref, wk_ref, wv_ref)):
        d = jnp.concatenate([refs[h * 3 + i][...] for h in range(halves)], axis=1)
        term = dot(d, w[...], NT)
        done = term if done is None else done + term
    tok = tok_ref[...].astype(F32)
    s = norm_scale(tok)
    g = row_of(gain_ref) * done
    out_ref[...] = (dres_ref[...] + s * g - tok * (s * s * s * jnp.mean(tok * g, axis=-1, keepdims=True))).astype(BF16)
    ggain = jnp.sum(done * tok * s, axis=0, keepdims=True)

    @pl.when(step == 0)
    def _():
        ggain_ref[...] = ggain

    @pl.when(step > 0)
    def _():
        ggain_ref[...] += ggain


def tokgrad(tok, dres, gain, ds, wq, wk, wv, after, block=256):
    toks, width = tok.shape
    full = lambda a: pl.BlockSpec(a.shape, lambda s: (0,) * a.ndim, pipeline_mode=pl.Buffered(1))
    tall = pl.BlockSpec((block, width), lambda s: (s, 0))
    return pl.pallas_call(
        functools.partial(tokgrad_kernel, len(ds) // 3),
        grid=(toks // block,),
        in_specs=[tall, tall, full(gain), full(wq), full(wk), full(wv)]
        + [pl.BlockSpec((block, d.shape[1]), lambda s: (s, 0)) for d in ds]
        + [ANYWHERE] * len(after),
        out_specs=[tall, pl.BlockSpec((1, width), lambda s: (0, 0))],
        out_shape=[jax.ShapeDtypeStruct((toks, width), BF16), jax.ShapeDtypeStruct((1, width), F32)],
        cost_estimate=COST,
        compiler_params=params(),
        name="tokgrad",
    )(tok, dres, gain, wq, wk, wv, *ds, *after)


SMALL = 16 * 2**20


class Route:
    def __init__(self, size, even, odd):
        self.size, self.even, self.odd = size, even, odd
        self.count = len(even)
        self.ways = [1 << len(group) for group in even]
        self.columns = {}
        table = [self.line(r, c) for r in range(size) for c in range(2)]
        device = lax.axis_index("rows") * 2 + lax.axis_index("blk")
        self.info = lax.dynamic_index_in_dim(jnp.asarray(np.array(table, np.int32)), device, 0, keepdims=False)

    def places(self, r, c):
        groups = (self.even, self.odd)[c]
        return [sum(((r >> b) & 1) << (len(group) - 1 - i) for i, b in enumerate(group)) for group in groups]

    def line(self, r, c):
        places, far = self.places(r, c), self.places(r, 1 - c)[0]
        line = [c, r, 2 * c + places[0], 2 * c + 1 - places[0], 2 * (1 - c) + far, 2 * (1 - c) + 1 - far, *places]
        self.place_column = 6
        for end in range(1, self.count + 1):
            for begin in range(end):
                for step in range(self.ways[end - 1]):
                    at = 0
                    for phase in range(begin, end):
                        at = at * self.ways[phase] + (places[phase] ^ (step if phase == end - 1 else 0))
                    self.columns[begin, end, step] = len(line)
                    line.append(at)
        return line

    def exchange(self, x, phase, step):
        def other(r, group):
            for i, b in enumerate(group):
                r ^= ((step >> (len(group) - 1 - i)) & 1) << b
            return r

        moves = [
            (r * 2 + c, other(r, (self.even, self.odd)[c][phase]) * 2 + c) for r in range(self.size) for c in range(2)
        ]
        return lax.ppermute(x, ("rows", "blk"), moves)


def swap_cores(x):
    return lax.ppermute(x, "blk", [(0, 1), (1, 0)])


def add_kernel(count, outs, info_ref, *refs):
    for n in range(outs):
        total = None
        for ref in refs[n * count : (n + 1) * count]:
            total = ref[...] if total is None else total + ref[...]
        refs[-outs + n][...] = total


def add_shares(info, sources, columns, rows, after, limit):
    cols = sources[0].shape[1]
    parts = 1
    while rows // parts * cols > 300000 and rows % (16 * parts) == 0:
        parts *= 2
    block = (rows // parts, cols)

    def spec(source, column):
        if column is None:
            return pl.BlockSpec(block, lambda g, i: (g, 0))
        return pl.BlockSpec(block, lambda g, i: (i[column] * parts + g, 0))

    outs = len(columns)
    return pl.pallas_call(
        functools.partial(add_kernel, len(sources), outs),
        grid_spec=pltpu.PrefetchScalarGridSpec(
            num_scalar_prefetch=1,
            grid=(parts,),
            in_specs=[spec(*pair) for line in columns for pair in zip(sources, line)] + [ANYWHERE] * len(after),
            out_specs=[pl.BlockSpec(block, lambda g, i: (g, 0))] * outs,
        ),
        out_shape=[jax.ShapeDtypeStruct((rows, cols), F32)] * outs,
        cost_estimate=LITTLE,
        compiler_params=params(limit),
        name="add_shares",
    )(info, *sources * outs, *after)


def join_kernel(column, ways, info_ref, *refs):
    pieces, out_ref, sems = refs[:ways], refs[-2], refs[-1]
    rows = pieces[0].shape[0]
    copies = []
    for step, piece in enumerate(pieces):
        at = pl.multiple_of((info_ref[column] ^ step) * rows, 8)
        copies.append(pltpu.make_async_copy(piece, out_ref.at[pl.ds(at, rows), :], sems.at[step]))
        copies[-1].start()
    for copy in copies:
        copy.wait()


def join(info, column, pieces, after):
    rows, cols = pieces[0].shape
    ways = len(pieces)
    return pl.pallas_call(
        functools.partial(join_kernel, column, ways),
        in_specs=[pl.BlockSpec(memory_space=pltpu.SMEM)] + [ANYWHERE] * (ways + len(after)),
        out_specs=pl.BlockSpec(memory_space=pltpu.VMEM),
        out_shape=jax.ShapeDtypeStruct((ways * rows, cols), F32),
        scratch_shapes=[pltpu.SemaphoreType.DMA((ways,))],
        cost_estimate=LITTLE,
        compiler_params=params(SMALL),
        name="join",
    )(info, *pieces, *after)


class Sum:
    def __init__(self, route, keep, send):
        self.route = route
        self.parts = [keep, swap_cores(send)]
        self.begins = [0, 0]
        self.shares = [keep.shape[0]]
        for ways in route.ways:
            if self.shares[-1] % (8 * ways):
                break
            self.shares.append(self.shares[-1] // ways)
        self.divided = len(self.shares) - 1
        self.phase = 0
        self.steps = (
            [self.send] * self.divided
            + [self.finish]
            + [self.add] * (route.count - self.divided)
            + [self.join] * (self.divided - 1)
            + [self.swap]
        )

    def advance(self, after):
        return self.steps.pop(0)(after) if self.steps else after

    def send(self, after):
        phase = self.phase
        flips = (1,) if phase == 0 else (1, 0)
        columns = [[self.route.columns[begin, phase + 1, flip] for begin in self.begins] for flip in flips]
        limit = VMEM if phase < 2 else SMALL
        outs = add_shares(self.route.info, self.parts, columns, self.shares[phase + 1], after, limit)
        got = self.route.exchange(outs[0], phase, 1)
        if phase == 0:
            self.parts.append(got)
            self.begins.append(1)
        else:
            self.parts = [outs[1], got]
            self.begins = [phase + 1] * 2
        self.phase += 1
        return (outs[0],)

    def finish(self, after):
        columns = [[self.route.columns.get((begin, self.phase, 0)) for begin in self.begins]]
        (self.piece,) = add_shares(self.route.info, self.parts, columns, self.shares[self.phase], after, SMALL)
        return self.gather()

    def gather(self):
        if self.divided <= self.phase < self.route.count:
            phase = self.phase
        else:
            phase = self.phase = min(self.phase, self.divided) - 1
        self.got = self.route.exchange(self.piece, phase, 1)
        if self.phase == 0:
            self.far_piece = swap_cores(self.piece)
            return (self.piece, (self.far_piece,))
        return (self.piece,)

    def add(self, after):
        parts = [self.piece, self.got]
        (self.piece,) = add_shares(self.route.info, parts, [[None] * 2], self.piece.shape[0], after, SMALL)
        self.phase += 1
        return self.gather()

    def join(self, after):
        self.piece = join(self.route.info, self.route.place_column + self.phase, [self.piece, self.got], after)
        return self.gather()

    def swap(self, after):
        self.sources = (self.piece, self.got, self.far_piece, swap_cores(self.got))
        return (self.got,)


SPACE = 10**11


def spacer_kernel(*refs):
    refs[-1][...] = jnp.zeros_like(refs[-1])


def spacer(after):
    return pl.pallas_call(
        spacer_kernel,
        in_specs=[ANYWHERE] * len(after),
        out_specs=pl.BlockSpec(memory_space=pltpu.VMEM),
        out_shape=jax.ShapeDtypeStruct((8, 128), F32),
        cost_estimate=pl.CostEstimate(flops=SPACE, transcendentals=0, bytes_accessed=1),
        name="spacer",
    )(*after)


class SmallSum:
    def __init__(self, route, values):
        self.route = route
        self.shapes = [v.shape for v in values]
        flat = jnp.concatenate([v.reshape(-1) for v in values])
        self.sum = jnp.pad(flat, (0, -flat.shape[0] % 2048)).reshape(-1, 256)
        self.steps = [functools.partial(route.exchange, phase=p, step=1) for p in range(route.count)] + [swap_cores]
        self.got = self.steps.pop(0)(self.sum)

    def advance(self, after):
        if self.got is None:
            return after
        (self.sum,) = add_shares(self.route.info, [self.sum, self.got], [[None, None]], self.sum.shape[0], after, SMALL)
        self.got = self.steps.pop(0)(self.sum) if self.steps else None
        return (self.sum,)

    def values(self):
        while self.got is not None:
            self.advance(())
        flat, at, out = self.sum.reshape(-1), 0, []
        for shape in self.shapes:
            size = int(np.prod(shape))
            out.append(flat[at : at + size].reshape(shape))
            at += size
        return out


def assemble_kernel(spread, n_outs, info_ref, *refs):
    sources, outs = refs[:4], refs[-n_outs:]
    target, half = pl.program_id(0), pl.program_id(1)
    for n in range(4):
        for t in range(2):

            @pl.when((info_ref[2 + n] == 2 * target + half) & (target == t))
            def _():
                spread(t, sources[n], outs)


def assemble(info, slabs, spread, outs, blocks, sources, group, earlier, after):
    rows, cols = sources[0].shape
    count = slabs // 2 // group

    def source_spec(n):
        def index(t, h, j, i):
            stage, now = i[2 + n], 2 * t + h
            return jnp.where(now < stage, 0, jnp.where(now == stage, j, count - 1)), 0

        return pl.BlockSpec((rows // count, cols), index)

    def out_spec(target, block, row, column):
        def index(t, h, j, i):
            if target is None:
                return row + (2 * t + h) * count + j, column
            return row + jnp.where(t == target, h * count + j, 0 if target else 2 * count - 1), column

        return pl.BlockSpec(block, index)

    return pl.pallas_call(
        functools.partial(assemble_kernel, spread, len(outs)),
        grid_spec=pltpu.PrefetchScalarGridSpec(
            num_scalar_prefetch=1,
            grid=(2, 2, count),
            in_specs=[source_spec(n) for n in range(4)] + [ANYWHERE] * (len(earlier) + len(after)),
            out_specs=[out_spec(*b) for b in blocks],
        ),
        out_shape=[jax.ShapeDtypeStruct(s, F32) for s in outs],
        cost_estimate=COST,
        input_output_aliases={5 + i: i for i in range(len(earlier))},
        compiler_params=params(),
        name="assemble",
    )(info, *sources, *earlier, *after)


def ffn_spread(width, size, slabs, group, target, source, outs):
    n, total = (size // 256, width) if target == 0 else (width // 256, size)
    rows = total // slabs
    for s in range(group):
        for j in range(n):
            at = (s * n + j) * rows
            outs[target][s * rows : (s + 1) * rows, j * 256 : (j + 1) * 256] = source[at : at + rows, :]


def attn_spread(columns, slabs, group, target, source, outs):
    n = len(columns)
    rows = source.shape[0] // (group * n)
    for s in range(group):
        for j, (out, column) in enumerate(columns):
            at = (s * n + j) * rows
            outs[out][s * rows : (s + 1) * rows, column : column + source.shape[1]] = source[at : at + rows, :]


ORDER = ("D", "F0", "s0", "F1", "s0", "B0", "s1", "s0", "B1", "s0", "s1", "s2", "D", "s0", "s3", "s1", "s0", "T", "s3", "s1", "s0", "D", "s3", "s3", "s2", "m", "s1", "m", "s0", "D", "s3", "m", "s1", "s3", "m", "s2", "s3", "s1", "s3", "D", "m", "s2", "s2", "s3", "s0", "s1", "s0", "s2", "s2", "s2", "s3", "s1", "s1", "s2", "D", "s2")


def on_device(tokens, lengths, attn_gain, wq, wk, wv, wo, table, ffn_gain, w_in, w_out, out_grad, *, size):
    rows, seq, width = tokens.shape
    buckets, heads = table.shape
    pairs = heads // 2
    ff = w_in.shape[1]
    slabs = 16
    rest = [(bit,) for bit in range(2, size.bit_length() - 1)]
    route = Route(size, [(0,), (1,)] + rest, [(1,), (0,)] + rest)
    info = route.info
    lane_buckets = band_buckets(buckets)
    onehot = np.arange(buckets)[:, None] == lane_buckets[None, :]
    band = jnp.einsum("bh,bm->hm", table, jnp.asarray(onehot, BF16), preferred_element_type=F32)
    flat = lambda a: a.reshape(rows * seq, a.shape[2])
    tall = lambda a: a.reshape(rows, seq, width)
    chunks, sub = 2, 768
    part = ff // chunks
    ends = bucket_of(np.array([-2 * TILE] * TILE + [2 * TILE] * TILE), buckets)
    spread = (np.concatenate([lane_buckets, ends])[:, None] == np.arange(buckets)[None, :]).astype(np.float32)

    h1T, q, k, v, attT, lse, x1, h2 = attn_fwd(tokens, lengths, attn_gain, ffn_gain, wq, wk, wv, wo, band)
    acc, sums, after, ds, diags = (), [], (), [], []
    ffn_grads, attn_grads = (), ()
    def put(which, after):
        nonlocal ffn_grads, attn_grads
        group = 8
        sources = sums[which].sources
        if which < chunks:
            ffn_grads = assemble(
                info, slabs, functools.partial(ffn_spread, width, part, slabs, group), [w_in.shape, w_out.shape],
                [(0, (width // slabs * group, part), 0, which), (1, (part // slabs * group, width), which * (slabs // group), 0)],
                sources, group, tuple(ffn_grads), after,
            )
            return (ffn_grads[0],)
        half = which - chunks
        block = width // 2 // slabs * group
        columns = [(0, 0), (1, 0), (2, 0)] + [(3, 0), (3, width // 2)] * (half == 0)
        blocks = [(None, (block, width // 2), 0, half)] * 3 + [(None, (block, width), 0, 0)] * (half == 0)
        made = assemble(
            info, slabs, functools.partial(attn_spread, columns, slabs, group), [wq.shape] * len(blocks), blocks,
            sources, group, tuple(attn_grads[:3]), after,
        )
        attn_grads = list(made) + list(attn_grads[3:])
        return (made[0],)

    late = []
    for at, op in enumerate(ORDER):
        if late:
            after = (*after, *late.pop(0))
        which = int(op[1]) if len(op) > 1 else 0
        if op[0] == "F":
            end = (flat(x1), ffn_gain, attT, wo) if which == chunks - 1 else None
            keep, send, *acc = ffn_chunk(
                info, lengths, slabs, flat(h2), flat(out_grad), w_in, w_out, which * part, part, sub, acc, after, end
            )
            sums.append(Sum(route, keep, send))
            if end:
                mixed, dres, datt, gwo, ggain2 = acc
            after = (keep,)
        elif op[0] == "B":
            half = pairs // 2
            more = [] if which else [gwo]
            dq, dk, dv, diag, keep, send = attn_bwd(
                info, lengths, slabs, q, k, v, tall(datt), lse, band, h1T, which * half, half, more, after
            )
            ds += [flat(dq), flat(dk), flat(dv)]
            diags.append(diag)
            sums.append(Sum(route, keep, send))
            after = (keep,)
        elif op == "T":
            tgrad, ggain1 = tokgrad(flat(tokens), dres, attn_gain, ds, wq, wk, wv, after)
            diag = jnp.concatenate(diags).reshape(heads, 6 * TILE)
            gtable = jnp.einsum("hm,mb->bh", diag, jnp.asarray(spread), precision=lax.Precision.HIGHEST)
            small = SmallSum(route, (ggain1, ggain2, gtable))
            after = (ggain1,)
        elif op == "D":
            after = (spacer(after),)
        elif op == "m":
            after = small.advance(after)
        else:
            after = sums[which].advance(after)
            if isinstance(after[-1], tuple):
                late, after = [(), after[-1]], after[:-1]
            if ORDER[at:].count(op) == 1:
                while sums[which].steps:
                    after = sums[which].advance(after)
                after = put(which, after)
    ggain1, ggain2, gtable = small.values()
    return (tall(mixed), tall(tgrad), ggain1[0], *attn_grads, gtable, ggain2[0], *ffn_grads)


def solution(mesh):
    split = P(("rows", "blk"))
    return jax.shard_map(
        functools.partial(on_device, size=mesh.shape["rows"]),
        mesh=mesh,
        in_specs=(split, split) + (P(),) * 9 + (split,),
        out_specs=(split, split) + (P(),) * 9,
        check_vma=False,
    )
```

time: 430 us -> 407 us (0.947)
  Pallas kernels: 173 us -> 242 us
  other arithmetic: 61.9 us -> 0.65 us
  starting transfers between devices: 76.1 us -> 48.4 us
  local copies, waits for them, and re-layouts: 51.2 us -> 26.5 us
  waiting for transfers between devices: 58.2 us -> 78.5 us
    pallas_call x7 -> x47, Pallas kernels: 110 us -> 179 us  [the longest x2 55.9 us: ffn_chunk(): pl.pallas_call(functools.partial(ffn_kernel, steps, slabs, not acc, bool(...]
    add x21 -> x0, other arithmetic: 46.2 us -> none  [the longest x16 43.6 us: total(): out = share if out is None else out + share]
    ppermute x44 -> x36, starting transfers between devices: 74.5 us -> 46.9 us  [exchange(): return lax.ppermute(x, ('rows', 'blk'), moves)]
    unnamed x172 -> x100, local copies, waits for them, and re-layouts: 45.7 us -> 23.3 us
    ppermute x44 -> x36, waiting for transfers between devices: 44 us -> 62.1 us  [exchange(): return lax.ppermute(x, ('rows', 'blk'), moves)]
    select_n x8 -> x0, other arithmetic: 10.2 us -> none  [join(): row = jnp.where(at == slot ^ step, pieces[step], row)]
    concatenate x8 -> x0, other arithmetic: 5.35 us -> none  [join(): self.piece = jnp.concatenate(rows)]
  transfers between devices with their start and end apart: 57 -> 49, of which waited for: 16 -> 18; matrix products, arithmetic and copies ran while one was open for 15% -> 1% of each run, Pallas kernels for 27% -> 46%
where the time goes in v3:
time: 407 us; the launch traced here: 399 us
  Pallas kernels  242 us (59%)
  waiting for transfers between devices  78.5 us (19%)
  starting transfers between devices  48.4 us (12%)
  local copies, waits for them, and re-layouts  26.5 us (7%)
    ppermute x36, waiting for transfers between devices, exchange(): return lax.ppermute(x, ('rows', 'blk'), moves)  62.1 us
    pallas_call x2, Pallas kernels, ffn_chunk(): pl.pallas_call(functools.partial(ffn_kernel, steps, slabs, not acc, bool(...  55.9 us
    pallas_call x25, Pallas kernels, add_shares(): pl.pallas_call(functools.partial(add_kernel, len(sources), outs), grid_sp...  54.1 us
    ppermute x36, starting transfers between devices, exchange(): return lax.ppermute(x, ('rows', 'blk'), moves)  46.9 us
    pallas_call x2, Pallas kernels, attn_bwd(): pl.pallas_call(functools.partial(attn_bwd_kernel, slabs, first, len(more)...  42.2 us
    pallas_call x4, Pallas kernels, assemble(): pl.pallas_call(functools.partial(assemble_kernel, spread, len(outs)), gri...  29.8 us
    pallas_call x12, Pallas kernels, join(): pl.pallas_call(functools.partial(join_kernel, column, ways), in_specs=[pl...  23.6 us
    unnamed x100, local copies, waits for them, and re-layouts  23.3 us
  transfers between devices with their start and end apart: 49, of which 18 were waited for; matrix products, arithmetic and copies ran while one was open for 1% of the time, Pallas kernels for 46%

profile of v3, /device:TPU:0, one launch (start us, length us, event | category | flops | bytes accessed | tf_op | source)
XLA Modules:
  0.0 399.0 jit_solution(11797713404988718112)
XLA Ops:
  3.2 23.1 %attn_fwd.1 = (bf16[2,768,512]{2,1,0:T(8,128)(2,1)}, bf16[2,512,768]{2,1,0:T(8,128)(2,1)}, bf16[2,512,768]{2,1,0:T(8,128)(2,1)}, bf16[2,512,768]{2,1,0:T(8,128)(...) custom-call(s32[2,8]{1,0:T(2,128)} %len_ref.9, ...), custom_call_target="tpu_custom_call" | custom-call | flops 99999997952 | bytes 1 | tf_op jit(solution)/shard_map/attn_fwd/pallas_call | solution.py:169
  26.3 25.1 %ffn.2 = (f32[4608,256]{1,0:T(8,128)}, f32[4608,256]{1,0:T(8,128)}, f32[1024,768]{1,0:T(8,128)}, f32[1024,768]{1,0:T(8,128)}) custom-call(s32[30]{0:T(128)} %dynamic-slice_bitcast_fusion.info_ref, s32[2,8]{1,0:T(2,128)} %len_ref.9, bf16[1024,768]{1,0:T(8,128)(2,1)} %bitcast.33, bf16[1024,768]{1,0:T(8,128)(2,1)} %bitcast.25, bf16[768,3072]{1,0:T(8,128)(2,1)} %win_ref.3, ...), custom_call_target="tpu_custom_call" | custom-call | flops 99999997952 | bytes 1 | tf_op jit(solution)/shard_map/ffn/pallas_call | solution.py:376
  51.9 7.9 %collective-permute-done.refs_1_.refs_4_ = f32[4608,256]{1,0:T(8,128)} collective-permute-done((f32[4608,256]{1,0:T(8,128)}, f32[4608,256]{1,0:T(8,128)}, u32[]{:S(2)}, u32[]{:S(2)}) %collective-permute-start) | collective-permute-done | bytes 4718624 | tf_op jit(solution)/shard_map/ppermute | solution.py:635
  59.8 4.2 %add_shares.25.refs_6_ = f32[2304,256]{1,0:T(8,128)} custom-call(s32[30]{0:T(128)} %dynamic-slice_bitcast_fusion.info_ref, f32[4608,256]{1,0:T(8,128)} %get-tuple-element.84.refs_0_.refs_2_.refs_3_, f32[4608,256]{1,0:T(8,128)} %collective-permute-done.refs_1_.refs_4_, f32[4608,256]{1,0:T(8,128)} %get-tuple-element.84.refs_0_.refs_2_.refs_3_), custom_call_target="tpu_custom_call" | custom-call | flops 1 | bytes 1 | tf_op jit(solution)/shard_map/add_shares/pallas_call | solution.py:659
  66.8 30.8 %ffn.3 = (f32[4608,256]{1,0:T(8,128)}, f32[4608,256]{1,0:T(8,128)}, bf16[1024,768]{1,0:T(8,128)(2,1)}, f32[1024,768]{1,0:T(8,128)}, bf16[1024,768]{1,0:T(8,128)(...) custom-call(s32[30]{0:T(128)} %dynamic-slice_bitcast_fusion.info_ref, s32[2,8]{1,0:T(2,128)} %len_ref.9, ...), custom_call_target="tpu_custom_call" | custom-call | flops 99999997952 | bytes 1 | tf_op jit(solution)/shard_map/ffn/pallas_call | solution.py:376
  97.7 5.3 %add_shares.26 = (f32[1152,256]{1,0:T(8,128)}, f32[1152,256]{1,0:T(8,128)}) custom-call(s32[30]{0:T(128)} %dynamic-slice_bitcast_fusion.info_ref, f32[4608,256]{1,0:T(8,128)} %get-tuple-element.84.refs_0_.refs_2_.refs_3_, f32[4608,256]{1,0:T(8,128)} %collective-permute-done.refs_1_.refs_4_, f32[2304,256]{1,0:T(8,128)} %collective-permute-done.1.refs_2_.refs_5_, ...), custom_call_target="tpu_custom_call" | custom-call | flops 1 | bytes 1 | tf_op jit(solution)/shard_map/add_shares/pallas_call | solution.py:659
  104.6 21.7 %attn_bwd.2 = (bf16[2,512,384]{2,1,0:T(8,128)(2,1)}, bf16[2,512,384]{2,1,0:T(8,128)(2,1)}, bf16[2,512,384]{2,1,0:T(8,128)(2,1)}, f32[3,2,768]{2,1,0:T(2,128)}, f32[1920,384]{1,0:T(8,128)}, /*index=5*/f32[1920,384]{1,0:T(8,128)}) custom-call(s32[30]{0:T(128)} %dynamic-slice_bitcast_fusion.info_ref, s32[2,8]{1,0:T(2,128)} %len_ref.9, ...), custom_call_target="tpu_custom_call" | custom-call | flops 99999997952 | bytes 1 | tf_op jit(solution)/shard_map/attn_bwd/pallas_call | solution.py:520
  126.4 4.2 %add_shares.27.refs_4_ = f32[2304,256]{1,0:T(8,128)} custom-call(s32[30]{0:T(128)} %dynamic-slice_bitcast_fusion.info_ref, f32[4608,256]{1,0:T(8,128)} %get-tuple-element.95.refs_6_.refs_0_.refs_3_, f32[4608,256]{1,0:T(8,128)} %collective-permute-done.3.refs_1_.refs_4_, f32[1920,384]{1,0:T(8,128)} %get-tuple-element.102.refs_2_.refs_0_.refs_3_), custom_call_target="tpu_custom_call" | custom-call | flops 1 | bytes 1 | tf_op jit(solution)/shard_map/add_shares/pallas_call | solution.py:659
  138.7 20.4 %attn_bwd.3 = (bf16[2,512,384]{2,1,0:T(8,128)(2,1)}, bf16[2,512,384]{2,1,0:T(8,128)(2,1)}, bf16[2,512,384]{2,1,0:T(8,128)(2,1)}, f32[3,2,768]{2,1,0:T(2,128)}, f32[1152,384]{1,0:T(8,128)}, /*index=5*/f32[1152,384]{1,0:T(8,128)}) custom-call(s32[30]{0:T(128)} %dynamic-slice_bitcast_fusion.info_ref, s32[2,8]{1,0:T(2,128)} %len_ref.9, ...), custom_call_target="tpu_custom_call" | custom-call | flops 99999997952 | bytes 1 | tf_op jit(solution)/shard_map/attn_bwd/pallas_call | solution.py:520
  165.7 5.3 %add_shares.30 = (f32[1152,256]{1,0:T(8,128)}, f32[1152,256]{1,0:T(8,128)}) custom-call(s32[30]{0:T(128)} %dynamic-slice_bitcast_fusion.info_ref, f32[4608,256]{1,0:T(8,128)} %get-tuple-element.95.refs_6_.refs_0_.refs_3_, f32[4608,256]{1,0:T(8,128)} %collective-permute-done.3.refs_1_.refs_4_, f32[2304,256]{1,0:T(8,128)} %collective-permute-done.7.refs_2_.refs_5_, ...), custom_call_target="tpu_custom_call" | custom-call | flops 1 | bytes 1 | tf_op jit(solution)/shard_map/add_shares/pallas_call | solution.py:659
  199.4 9.7 %tokgrad.1 = (bf16[1024,768]{1,0:T(8,128)(2,1)}, f32[1,768]{1,0:T(1,128)}) custom-call(bf16[1024,768]{1,0:T(8,128)(2,1)} %bitcast.27, f32[1024,768]{1,0:T(8,128)} %get-tuple-element.87.dres_ref, bf16[768]{0:T(1024)(128)(2,1)} %gain_ref.1, bf16[768,768]{1,0:T(8,128)(2,1)} %wq_ref.3, bf16[768,768]{1,0:T(8,128)(2,1)} %wk_ref.3, bf16[768,768]{1,0:T(8,128)(2,1)} %wv_ref.3, ...), custom_call_target="tpu_custom_call" | custom-call | flops 99999997952 | bytes 1 | tf_op jit(solution)/shard_map/tokgrad/pallas_call | solution.py:577
  232.2 5.0 %collective-permute-done.17.refs_1_.refs_3_ = f32[144,384]{1,0:T(8,128)S(1)} collective-permute-done((f32[144,384]{1,0:T(8,128)S(1)}, f32[144,384]{1,0:T(8,128)S(1)}, u32[]{:S(2)}, u32[]{:S(2)}) %collective-permute-start.17) | collective-permute-done | bytes 221216 | tf_op jit(solution)/shard_map/ppermute | solution.py:631
  239.1 4.2 %add_shares.39 = (f32[480,384]{1,0:T(8,128)}, f32[480,384]{1,0:T(8,128)}) custom-call(s32[30]{0:T(128)} %dynamic-slice_bitcast_fusion.info_ref, f32[1920,384]{1,0:T(8,128)} %get-tuple-element.102.refs_2_.refs_0_.refs_3_, f32[1920,384]{1,0:T(8,128)} %collective-permute-done.6.refs_1_.refs_4_, f32[960,384]{1,0:T(8,128)} %collective-permute-done.12.refs_2_.refs_5_, ...), custom_call_target="tpu_custom_call" | custom-call | flops 1 | bytes 1 | tf_op jit(solution)/shard_map/add_shares/pallas_call | solution.py:659
  253.1 3.6 join.14.refs_0_
  267.6 3.6 collective-permute-done.20.refs_1_
  278.2 14.8 %collective-permute-done.24.refs_1_ = f32[8,256]{1,0:T(8,128)S(1)} collective-permute-done((f32[8,256]{1,0:T(8,128)S(1)}, f32[8,256]{1,0:T(8,128)S(1)}, u32[]{:S(2)}, u32[]{:S(2)}) %collective-permute-start.24) | collective-permute-done | bytes 8224 | tf_op jit(solution)/shard_map/ppermute | solution.py:631
  328.3 9.3 %assemble.4 = (f32[768,3072]{1,0:T(8,128)}, f32[3072,768]{1,0:T(8,128)}) custom-call(s32[30]{0:T(128)} %dynamic-slice_bitcast_fusion.info_ref, f32[2304,256]{1,0:T(8,128)} %join.14.refs_0_, f32[2304,256]{1,0:T(8,128)} %copy-done.11, f32[2304,256]{1,0:T(8,128)} %collective-permute-done.23.refs_3_.refs_2_, f32[2304,256]{1,0:T(8,128)} %collective-permute-done.37.refs_3_, ...), custom_call_target="tpu_custom_call" | custom-call | flops 99999997952 | bytes 1 | tf_op jit(solution)/shard_map/assemble/pallas_call | solution.py:846
  338.5 3.7 copy-done.3
  344.9 9.3 %collective-permute-done.40.refs_1_ = f32[240,384]{1,0:T(8,128)S(1)} collective-permute-done((f32[240,384]{1,0:T(8,128)S(1)}, f32[240,384]{1,0:T(8,128)S(1)}, u32[]{:S(2)}, u32[]{:S(2)}) %collective-permute-start.40) | collective-permute-done | bytes 368672 | tf_op jit(solution)/shard_map/ppermute | solution.py:631
  358.5 8.2 %collective-permute-done.41.refs_1_ = f32[480,384]{1,0:T(8,128)S(1)} collective-permute-done((f32[480,384]{1,0:T(8,128)S(1)}, f32[480,384]{1,0:T(8,128)S(1)}, u32[]{:S(2)}, u32[]{:S(2)}) %collective-permute-start.41) | collective-permute-done | bytes 737312 | tf_op jit(solution)/shard_map/ppermute | solution.py:631
  371.0 4.9 %assemble.5 = (f32[768,768]{1,0:T(8,128)}, f32[768,768]{1,0:T(8,128)}, f32[768,768]{1,0:T(8,128)}) custom-call(s32[30]{0:T(128)} %dynamic-slice_bitcast_fusion.info_ref, f32[576,384]{1,0:T(8,128)} %join.19.refs_0_, f32[576,384]{1,0:T(8,128)} %collective-permute-done.45.refs_1_, f32[576,384]{1,0:T(8,128)} %collective-permute-done.32.refs_3_.refs_2_, ...), custom_call_target="tpu_custom_call" | custom-call | flops 99999997952 | bytes 1 | tf_op jit(solution)/shard_map/assemble/pallas_call | solution.py:846
  376.0 9.2 %assemble.7 = (f32[768,3072]{1,0:T(8,128)}, f32[3072,768]{1,0:T(8,128)}) custom-call(s32[30]{0:T(128)} %dynamic-slice_bitcast_fusion.info_ref, f32[2304,256]{1,0:T(8,128)} %join.20.refs_4_.refs_0_, f32[2304,256]{1,0:T(8,128)} %collective-permute-done.47.refs_1_.refs_6_, ...), custom_call_target="tpu_custom_call", output_to_operand_aliasing={{0}: (5, {}), {1}: (6, {})} | custom-call | flops 99999997952 | bytes 1 | tf_op jit(solution)/shard_map/assemble/pallas_call | solution.py:846
  385.2 3.6 collective-permute-done.42.refs_0_.refs_1_
  392.4 6.5 %assemble.6 = (f32[768,768]{1,0:T(8,128)}, f32[768,768]{1,0:T(8,128)}, f32[768,768]{1,0:T(8,128)}, f32[768,768]{1,0:T(8,128)}) custom-call(s32[30]{0:T(128)} %dynamic-slice_bitcast_fusion.info_ref, f32[960,384]{1,0:T(8,128)} %join.23.refs_4_.refs_0_, ...), custom_call_target="tpu_custom_call", output_to_operand_aliasing={{0}: (5, {}), {1}: (6, {}), {2}: (7, {})} | custom-call | flops 99999997952 | bytes 1 | tf_op jit(solution)/shard_map/assemble/pallas_call | solution.py:846
  (242 shorter events, 153.9 us)
Async XLA Ops:
  64.0 33.8 %collective-permute-start.1 = (f32[2304,256]{1,0:T(8,128)}, f32[2304,256]{1,0:T(8,128)}, u32[]{:S(2)}, u32[]{:S(2)}) collective-permute-start(f32[2304,256]{1,0:T(8,128)} %add_shares.25.refs_6_), channel_id=1, source_target_pairs={{0,2},{1,5},{2,0},{3,7},{4,6},{5,1},{6,4},{7,3},{8,10},{9,13},{10,... | collective-permute-start | bytes 7077896 | tf_op jit(solution)/shard_map/ppermute | solution.py:631
  97.6 28.7 %collective-permute-start.3 = (f32[4608,256]{1,0:T(8,128)}, f32[4608,256]{1,0:T(8,128)}, u32[]{:S(2)}, u32[]{:S(2)}) collective-permute-start(f32[4608,256]{1,0:T(8,128)} %get-tuple-element.101), channel_id=1, source_target_pairs={{0,1},{1,0},{2,3},{3,2},{4,5},{5,4},{6,7},{7,6},{8,9},{9,8},{10,11... | collective-permute-start | bytes 14155784 | tf_op jit(solution)/shard_map/ppermute | solution.py:635
  103.0 28.3 %collective-permute-start.2 = (f32[1152,256]{1,0:T(8,128)}, f32[1152,256]{1,0:T(8,128)}, u32[]{:S(2)}, u32[]{:S(2)}) collective-permute-start(f32[1152,256]{1,0:T(8,128)} %get-tuple-element.96.refs_1_), channel_id=1, source_target_pairs={{0,4},{1,3},{2,6},{3,1},{4,0},{5,7},{6,2},{7,5},{8,12},{9,11},{10,... | collective-permute-start | bytes 3538952 | tf_op jit(solution)/shard_map/ppermute | solution.py:631
  126.3 46.2 %collective-permute-start.6 = (f32[1920,384]{1,0:T(8,128)}, f32[1920,384]{1,0:T(8,128)}, u32[]{:S(2)}, u32[]{:S(2)}) collective-permute-start(f32[1920,384]{1,0:T(8,128)} %get-tuple-element.111), channel_id=1, source_target_pairs={{0,1},{1,0},{2,3},{3,2},{4,5},{5,4},{6,7},{7,6},{8,9},{9,8},{10,11... | collective-permute-start | bytes 8847368 | tf_op jit(solution)/shard_map/ppermute | solution.py:635
  130.6 35.1 %collective-permute-start.7 = (f32[2304,256]{1,0:T(8,128)}, f32[2304,256]{1,0:T(8,128)}, u32[]{:S(2)}, u32[]{:S(2)}) collective-permute-start(f32[2304,256]{1,0:T(8,128)} %add_shares.27.refs_4_), channel_id=1, source_target_pairs={{0,2},{1,5},{2,0},{3,7},{4,6},{5,1},{6,4},{7,3},{8,10},{9,13},{10,... | collective-permute-start | bytes 7077896 | tf_op jit(solution)/shard_map/ppermute | solution.py:631
  137.1 22.1 %collective-permute-start.4 = (f32[576,256]{1,0:T(8,128)}, f32[576,256]{1,0:T(8,128)}, u32[]{:S(2)}, u32[]{:S(2)}) collective-permute-start(f32[576,256]{1,0:T(8,128)} %get-tuple-element.103.refs_0_), channel_id=1, source_target_pairs={{0,8},{1,9},{2,10},{3,11},{4,12},{5,13},{6,14},{7,15},{8,0},{9,1},... | collective-permute-start | bytes 1769480 | tf_op jit(solution)/shard_map/ppermute | solution.py:631
  159.1 24.4 %collective-permute-start.10 = (f32[1152,384]{1,0:T(8,128)}, f32[1152,384]{1,0:T(8,128)}, u32[]{:S(2)}, u32[]{:S(2)}) collective-permute-start(f32[1152,384]{1,0:T(8,128)} %get-tuple-element.114), channel_id=1, source_target_pairs={{0,1},{1,0},{2,3},{3,2},{4,5},{5,4},{6,7},{7,6},{8,9},{9,8},{10,11... | collective-permute-start | bytes 5308424 | tf_op jit(solution)/shard_map/ppermute | solution.py:635
  182.2 56.9 %collective-permute-start.12 = (f32[960,384]{1,0:T(8,128)}, f32[960,384]{1,0:T(8,128)}, u32[]{:S(2)}, u32[]{:S(2)}) collective-permute-start(f32[960,384]{1,0:T(8,128)} %add_shares.31.refs_0_), channel_id=1, source_target_pairs={{0,2},{1,5},{2,0},{3,7},{4,6},{5,1},{6,4},{7,3},{8,10},{9,13},{10,... | collective-permute-start | bytes 4423688 | tf_op jit(solution)/shard_map/ppermute | solution.py:631
  186.6 25.3 %collective-permute-start.13 = (f32[576,384]{1,0:T(8,128)}, f32[576,384]{1,0:T(8,128)}, u32[]{:S(2)}, u32[]{:S(2)}) collective-permute-start(f32[576,384]{1,0:T(8,128)} %add_shares.33.refs_4_), channel_id=1, source_target_pairs={{0,2},{1,5},{2,0},{3,7},{4,6},{5,1},{6,4},{7,3},{8,10},{9,13},{10,... | collective-permute-start | bytes 2654216 | tf_op jit(solution)/shard_map/ppermute | solution.py:631
  194.9 22.1 %collective-permute-start.16 = (f32[576,256]{1,0:T(8,128)}, f32[576,256]{1,0:T(8,128)}, u32[]{:S(2)}, u32[]{:S(2)}) collective-permute-start(f32[576,256]{1,0:T(8,128)} %get-tuple-element.115.refs_2_), channel_id=1, source_target_pairs={{0,8},{1,9},{2,10},{3,11},{4,12},{5,13},{6,14},{7,15},{8,0},{9,1},... | collective-permute-start | bytes 1769480 | tf_op jit(solution)/shard_map/ppermute | solution.py:631
  199.3 22.8 %collective-permute-start.15 = (f32[576,256]{1,0:T(8,128)}, f32[576,256]{1,0:T(8,128)}, u32[]{:S(2)}, u32[]{:S(2)}) collective-permute-start(f32[576,256]{1,0:T(8,128)} %join.12.refs_6_.refs_0_), channel_id=1, source_target_pairs={{0,8},{1,9},{2,10},{3,11},{4,12},{5,13},{6,14},{7,15},{8,0},{9,1},... | collective-permute-start | bytes 1769480 | tf_op jit(solution)/shard_map/ppermute | solution.py:631
  225.0 28.1 %collective-permute-start.22 = (f32[1152,256]{1,0:T(8,128)}, f32[1152,256]{1,0:T(8,128)}, u32[]{:S(2)}, u32[]{:S(2)}) collective-permute-start(f32[1152,256]{1,0:T(8,128)} %join.13.refs_0_), channel_id=1, source_target_pairs={{0,4},{1,3},{2,6},{3,1},{4,0},{5,7},{6,2},{7,5},{8,12},{9,11},{10,... | collective-permute-start | bytes 3538952 | tf_op jit(solution)/shard_map/ppermute | solution.py:631
  227.2 22.0 %collective-permute-start.19 = (f32[288,256]{1,0:T(8,128)}, f32[288,256]{1,0:T(8,128)S(1)}, u32[]{:S(2)}, u32[]{:S(2)}) collective-permute-start(f32[288,256]{1,0:T(8,128)} %get-tuple-element.124.refs_2_), channel_id=1, source_target_pairs={{0,16},{1,17},{2,18},{3,19},{4,20},{5,21},{6,22},{7,23},{8,24},{9,... | collective-permute-start | bytes 884744 | tf_op jit(solution)/shard_map/ppermute | solution.py:631
  248.3 45.3 %collective-permute-start.29 = (f32[480,384]{1,0:T(8,128)}, f32[480,384]{1,0:T(8,128)S(1)}, u32[]{:S(2)}, u32[]{:S(2)}) collective-permute-start(f32[480,384]{1,0:T(8,128)} %get-tuple-element.128.refs_2_), channel_id=1, source_target_pairs={{0,4},{1,3},{2,6},{3,1},{4,0},{5,7},{6,2},{7,5},{8,12},{9,11},{10,... | collective-permute-start | bytes 2211848 | tf_op jit(solution)/shard_map/ppermute | solution.py:631
  252.4 19.4 %collective-permute-start.26 = (f32[288,256]{1,0:T(8,128)S(1)}, f32[288,256]{1,0:T(8,128)}, u32[]{:S(2)}, u32[]{:S(2)}) collective-permute-start(f32[288,256]{1,0:T(8,128)S(1)} %add_shares.41.refs_2_.refs_0_), channel_id=1, source_target_pairs={{0,16},{1,17},{2,18},{3,19},{4,20},{5,21},{6,22},{7,23},{8,24},{9,... | collective-permute-start | bytes 884744 | tf_op jit(solution)/shard_map/ppermute | solution.py:631
  256.7 40.7 %collective-permute-start.36 = (f32[2304,256]{1,0:T(8,128)}, f32[2304,256]{1,0:T(8,128)S(1)}, u32[]{:S(2)}, u32[]{:S(2)}) collective-permute-start(f32[2304,256]{1,0:T(8,128)} %join.14.refs_0_), channel_id=1, source_target_pairs={{0,2},{1,5},{2,0},{3,7},{4,6},{5,1},{6,4},{7,3},{8,10},{9,13},{10,... | collective-permute-start | bytes 7077896 | tf_op jit(solution)/shard_map/ppermute | solution.py:631
  274.3 20.7 %collective-permute-start.28 = (f32[144,384]{1,0:T(8,128)S(1)}, f32[144,384]{1,0:T(8,128)S(1)}, u32[]{:S(2)}, u32[]{:S(2)}) collective-permute-start(f32[144,384]{1,0:T(8,128)S(1)} %join.16.refs_2_.refs_0_), channel_id=1, source_target_pairs={{0,8},{1,9},{2,10},{3,11},{4,12},{5,13},{6,14},{7,15},{8,0},{9,1},... | collective-permute-start | bytes 663560 | tf_op jit(solution)/shard_map/ppermute | solution.py:631
  276.0 24.7 %collective-permute-start.31 = (f32[576,256]{1,0:T(8,128)S(1)}, f32[576,256]{1,0:T(8,128)S(1)}, u32[]{:S(2)}, u32[]{:S(2)}) collective-permute-start(f32[576,256]{1,0:T(8,128)S(1)} %join.15.refs_2_.refs_0_), channel_id=1, source_target_pairs={{0,8},{1,9},{2,10},{3,11},{4,12},{5,13},{6,14},{7,15},{8,0},{9,1},... | collective-permute-start | bytes 1769480 | tf_op jit(solution)/shard_map/ppermute | solution.py:631
  297.5 30.8 %collective-permute-start.37 = (f32[2304,256]{1,0:T(8,128)S(1)}, f32[2304,256]{1,0:T(8,128)}, u32[]{:S(2)}, u32[]{:S(2)}) collective-permute-start(f32[2304,256]{1,0:T(8,128)S(1)} %collective-permute-done.36.refs_2_.refs_1_), channel_id=1, source_target_pairs={{0,1},{1,0},{2,3},{3,2},{4,5},{5,4},{6,7},{7,6},{8,9},{9,8},{10,11... | collective-permute-start | bytes 7077896 | tf_op jit(solution)/shard_map/ppermute | solution.py:635
  318.2 26.8 %collective-permute-start.45 = (f32[576,384]{1,0:T(8,128)}, f32[576,384]{1,0:T(8,128)}, u32[]{:S(2)}, u32[]{:S(2)}) collective-permute-start(f32[576,384]{1,0:T(8,128)} %join.19.refs_0_), channel_id=1, source_target_pairs={{0,2},{1,5},{2,0},{3,7},{4,6},{5,1},{6,4},{7,3},{8,10},{9,13},{10,... | collective-permute-start | bytes 2654216 | tf_op jit(solution)/shard_map/ppermute | solution.py:631
  322.7 35.8 %collective-permute-start.47 = (f32[2304,256]{1,0:T(8,128)}, f32[2304,256]{1,0:T(8,128)}, u32[]{:S(2)}, u32[]{:S(2)}) collective-permute-start(f32[2304,256]{1,0:T(8,128)} %join.20.refs_4_.refs_0_), channel_id=1, source_target_pairs={{0,2},{1,5},{2,0},{3,7},{4,6},{5,1},{6,4},{7,3},{8,10},{9,13},{10,... | collective-permute-start | bytes 7077896 | tf_op jit(solution)/shard_map/ppermute | solution.py:631
  344.9 25.2 %collective-permute-start.46 = (f32[576,384]{1,0:T(8,128)}, f32[576,384]{1,0:T(8,128)S(1)}, u32[]{:S(2)}, u32[]{:S(2)}) collective-permute-start(f32[576,384]{1,0:T(8,128)} %collective-permute-done.45.refs_1_), channel_id=1, source_target_pairs={{0,1},{1,0},{2,3},{3,2},{4,5},{5,4},{6,7},{7,6},{8,9},{9,8},{10,11... | collective-permute-start | bytes 2654216 | tf_op jit(solution)/shard_map/ppermute | solution.py:635
  369.0 19.7 %collective-permute-start.42 = (f32[960,384]{1,0:T(8,128)}, f32[960,384]{1,0:T(8,128)}, u32[]{:S(2)}, u32[]{:S(2)}) collective-permute-start(f32[960,384]{1,0:T(8,128)} %join.23.refs_4_.refs_0_), channel_id=1, source_target_pairs={{0,2},{1,5},{2,0},{3,7},{4,6},{5,1},{6,4},{7,3},{8,10},{9,13},{10,... | collective-permute-start | bytes 4423688 | tf_op jit(solution)/shard_map/ppermute | solution.py:631
  370.1 19.2 %collective-permute-start.43 = (f32[960,384]{1,0:T(8,128)}, f32[960,384]{1,0:T(8,128)}, u32[]{:S(2)}, u32[]{:S(2)}) collective-permute-start(f32[960,384]{1,0:T(8,128)} %join.23.refs_4_.refs_0_), channel_id=1, source_target_pairs={{0,1},{1,0},{2,3},{3,2},{4,5},{5,4},{6,7},{7,6},{8,9},{9,8},{10,11... | collective-permute-start | bytes 4423688 | tf_op jit(solution)/shard_map/ppermute | solution.py:635
  (74 other events, 514.6 us)

commit v4 on v3

--- a/solution.py
+++ b/solution.py
@@ -89,9 +89,14 @@
 
 VMEM = 63 * 2**20
 ANYWHERE = pl.BlockSpec(memory_space=pl.ANY)
+OUTSIDE = pl.BlockSpec(memory_space=pltpu.HBM)
 FLOPS = 10**11
 LITTLE = pl.CostEstimate(flops=1, transcendentals=0, bytes_accessed=1)
 COST = pl.CostEstimate(flops=FLOPS, transcendentals=0, bytes_accessed=1)
+
+
+def unused(arrays):
+    return [OUTSIDE if a.size >= 2**18 else ANYWHERE for a in arrays]
 
 
 def params(limit=VMEM):
@@ -219,9 +224,12 @@
     refs = list(refs)
     acc_in = [] if first else [refs.pop(0), refs.pop(0)]
     if last:
-        x1_ref, gain_ref, attT_ref, wo_ref = refs[:4]
-        keep_ref, send_ref, mixed_out, dres_out, datt_out, gwo_ref, ggain_ref = refs[-19:-12]
-        mix_ref, dtwo_ref, h2T_ref, act_ref, dpre_ref, gin_ref, gout_ref, sems, acc_sems, mixed_ref, dres_ref, datt_ref = refs[-12:]
+        gain_ref, late = refs[0], refs[1:4]
+        keep_ref, send_ref, mixed_out, dres_out, datt_out, gwo_ref, ggain_ref = refs[-22:-15]
+        mix_ref, dtwo_ref, h2T_ref, act_ref, dpre_ref, gin_ref, gout_ref, sems, acc_sems, mixed_ref, dres_ref, datt_ref = refs[-15:-3]
+        x1_ref, attT_ref, wo_ref = refs[-3:]
+        first_late = acc_sems.shape[0] - 3
+        late = [pltpu.make_async_copy(a, b, acc_sems.at[first_late + i]) for i, (a, b) in enumerate(zip(late, refs[-3:]))]
     else:
         keep_ref, send_ref = refs[-13:-11]
         acc_out = refs[-11:-9]
@@ -254,15 +262,16 @@
     def _():
         for i, ref in enumerate(acc_in):
             pltpu.make_async_copy(ref, totals[i], acc_sems.at[i]).start()
+        if last:
+            for copy in late:
+                copy.start()
         h2T_ref[...] = h2_ref[...].T
 
-    for c in range(0, sub, 256):
-        cols = slice(c, c + 256)
-        pre = dot(h2_ref[...], win_ref[:, cols])
-        dact = dot(dy_ref[...], wout_ref[cols, :], NT)
-        act, slope = gelu_pair(pre)
-        act_ref[:, cols] = act.astype(BF16)
-        dpre_ref[:, cols] = (dact * slope).astype(BF16)
+    pre = dot(h2_ref[...], win_ref[...])
+    dact = dot(dy_ref[...], wout_ref[...], NT)
+    act, slope = gelu_pair(pre)
+    act_ref[...] = act.astype(BF16)
+    dpre_ref[...] = (dact * slope).astype(BF16)
     mix = dot(act_ref[...], wout_ref[...])
     dtwo = dot(dpre_ref[...], win_ref[...], NT)
 
@@ -304,6 +313,8 @@
     @pl.when(step == steps - 1)
     def _():
         if last:
+            for copy in late:
+                copy.wait()
             rows = len_ref.shape[0]
             seq = toks // rows
             block = 256
@@ -360,19 +371,22 @@
         pltpu.VMEM((steps, piece, 256), F32),
         pltpu.VMEM((steps, piece, 256), F32),
         pltpu.SemaphoreType.DMA((steps, 2, slabs)),
-        pltpu.SemaphoreType.DMA((4 + 3 * (toks // 256),)),
+        pltpu.SemaphoreType.DMA((7 + 3 * (toks // 256),)),
     ]
     if rest is None:
-        rest = ()
+        rest, gain = (), ()
         out_specs += [ANYWHERE] * 2
         out_shape += [f32(toks, width)] * 2
     else:
+        gain, *rest = rest
+        gain = (gain,)
         low = jax.ShapeDtypeStruct((toks, width), BF16)
         whole = lambda s: pl.BlockSpec(s.shape, lambda *_: (0,) * len(s.shape), pipeline_mode=pl.Buffered(1))
         gwo, ggain = f32(width, width), f32(1, width)
         out_specs += [ANYWHERE] * 3 + [whole(gwo), whole(ggain)]
         out_shape += [low, f32(toks, width), low, gwo, ggain]
         scratch += [pltpu.VMEM((toks, width), BF16), pltpu.VMEM((toks, width), F32), pltpu.VMEM((toks, width), BF16)]
+        scratch += [pltpu.VMEM(a.shape, a.dtype) for a in rest]
     return pl.pallas_call(
         functools.partial(ffn_kernel, steps, slabs, not acc, bool(rest)),
         grid_spec=pltpu.PrefetchScalarGridSpec(
@@ -385,8 +399,9 @@
                 pl.BlockSpec((sub, width), lambda s, *_: (base + s, 0)),
             ]
             + [ANYWHERE] * len(acc)
-            + [full(a) for a in rest]
-            + [ANYWHERE] * len(after),
+            + [full(a) for a in gain]
+            + [ANYWHERE] * len(rest)
+            + unused(after),
             out_specs=out_specs,
             scratch_shapes=scratch,
         ),
@@ -394,7 +409,7 @@
         cost_estimate=COST,
         compiler_params=params(),
         name="ffn",
-    )(info, lengths, h2, dy, w_in, w_out, *acc, *rest, *after)
+    )(info, lengths, h2, dy, w_in, w_out, *acc, *gain, *rest, *after)
 
 
 def diagonal_sums(x):
@@ -525,7 +540,7 @@
             in_specs=[tall] * 4
             + [full(lse), full(band), full(h1T)]
             + [full(m) for m in more]
-            + [ANYWHERE] * len(after),
+            + unused(after),
             out_specs=[tall_out] * 3 + [pl.BlockSpec((1, 2, 6 * TILE), lambda p, *_: (p, 0, 0))] + [ANYWHERE] * 2,
             scratch_shapes=[
                 pltpu.VMEM((rows, seq, seq), F32),
@@ -579,7 +594,7 @@
         grid=(toks // block,),
         in_specs=[tall, tall, full(gain), full(wq), full(wk), full(wv)]
         + [pl.BlockSpec((block, d.shape[1]), lambda s: (s, 0)) for d in ds]
-        + [ANYWHERE] * len(after),
+        + unused(after),
         out_specs=[tall, pl.BlockSpec((1, width), lambda s: (0, 0))],
         out_shape=[jax.ShapeDtypeStruct((toks, width), BF16), jax.ShapeDtypeStruct((1, width), F32)],
         cost_estimate=COST,
@@ -661,7 +676,7 @@
         grid_spec=pltpu.PrefetchScalarGridSpec(
             num_scalar_prefetch=1,
             grid=(parts,),
-            in_specs=[spec(*pair) for line in columns for pair in zip(sources, line)] + [ANYWHERE] * len(after),
+            in_specs=[spec(*pair) for line in columns for pair in zip(sources, line)] + unused(after),
             out_specs=[pl.BlockSpec(block, lambda g, i: (g, 0))] * outs,
         ),
         out_shape=[jax.ShapeDtypeStruct((rows, cols), F32)] * outs,
@@ -688,7 +703,7 @@
     ways = len(pieces)
     return pl.pallas_call(
         functools.partial(join_kernel, column, ways),
-        in_specs=[pl.BlockSpec(memory_space=pltpu.SMEM)] + [ANYWHERE] * (ways + len(after)),
+        in_specs=[pl.BlockSpec(memory_space=pltpu.SMEM)] + [ANYWHERE] * ways + unused(after),
         out_specs=pl.BlockSpec(memory_space=pltpu.VMEM),
         out_shape=jax.ShapeDtypeStruct((ways * rows, cols), F32),
         scratch_shapes=[pltpu.SemaphoreType.DMA((ways,))],
@@ -723,14 +738,14 @@
 
     def send(self, after):
         phase = self.phase
-        flips = (1,) if phase == 0 else (1, 0)
+        flips = (1,) if phase < 2 else (1, 0)
         columns = [[self.route.columns[begin, phase + 1, flip] for begin in self.begins] for flip in flips]
-        limit = VMEM if phase < 2 else SMALL
+        limit = VMEM if phase < 3 else SMALL
         outs = add_shares(self.route.info, self.parts, columns, self.shares[phase + 1], after, limit)
         got = self.route.exchange(outs[0], phase, 1)
-        if phase == 0:
+        if phase < 2:
             self.parts.append(got)
-            self.begins.append(1)
+            self.begins.append(phase + 1)
         else:
             self.parts = [outs[1], got]
             self.begins = [phase + 1] * 2
@@ -778,7 +793,7 @@
 def spacer(after):
     return pl.pallas_call(
         spacer_kernel,
-        in_specs=[ANYWHERE] * len(after),
+        in_specs=unused(after),
         out_specs=pl.BlockSpec(memory_space=pltpu.VMEM),
         out_shape=jax.ShapeDtypeStruct((8, 128), F32),
         cost_estimate=pl.CostEstimate(flops=SPACE, transcendentals=0, bytes_accessed=1),
@@ -848,7 +863,7 @@
         grid_spec=pltpu.PrefetchScalarGridSpec(
             num_scalar_prefetch=1,
             grid=(2, 2, count),
-            in_specs=[source_spec(n) for n in range(4)] + [ANYWHERE] * (len(earlier) + len(after)),
+            in_specs=[source_spec(n) for n in range(4)] + [OUTSIDE] * len(earlier) + unused(after),
             out_specs=[out_spec(*b) for b in blocks],
         ),
         out_shape=[jax.ShapeDtypeStruct(s, F32) for s in outs],
@@ -877,7 +892,7 @@
             outs[out][s * rows : (s + 1) * rows, column : column + source.shape[1]] = source[at : at + rows, :]
 
 
-ORDER = ("D", "F0", "s0", "F1", "s0", "B0", "s1", "s0", "B1", "s0", "s1", "s2", "D", "s0", "s3", "s1", "s0", "T", "s3", "s1", "s0", "D", "s3", "s3", "s2", "m", "s1", "m", "s0", "D", "s3", "m", "s1", "s3", "m", "s2", "s3", "s1", "s3", "D", "m", "s2", "s2", "s3", "s0", "s1", "s0", "s2", "s2", "s2", "s3", "s1", "s1", "s2", "D", "s2")
+ORDER = ("F0", "s0", "F1", "s0", "B0", "s1", "s0", "B1", "s0", "s1", "s2", "D", "s3", "D", "s0", "s1", "s0", "T", "s3", "s1", "s0", "D", "m", "s3", "s2", "s3", "s1", "m", "s0", "D", "s3", "s1", "m", "s3", "s2", "s3", "s1", "m", "s3", "D", "m", "s2", "s2", "s3", "s0", "s1", "s0", "s2", "s2", "s2", "s3", "s1", "s1", "s2", "D", "s2")
 
 
 def on_device(tokens, lengths, attn_gain, wq, wk, wv, wo, table, ffn_gain, w_in, w_out, out_grad, *, size):
@@ -886,9 +901,9 @@
     pairs = heads // 2
     ff = w_in.shape[1]
     slabs = 16
-    rest = [(bit,) for bit in range(2, size.bit_length() - 1)]
-    route = Route(size, [(0,), (1,)] + rest, [(1,), (0,)] + rest)
-    info = route.info
+    bits = range(size.bit_length() - 1)
+    straight = Route(size, [(b,) for b in bits], [(b,) for b in (1, 0, *bits[2:])])
+    info = straight.info
     lane_buckets = band_buckets(buckets)
     onehot = np.arange(buckets)[:, None] == lane_buckets[None, :]
     band = jnp.einsum("bh,bm->hm", table, jnp.asarray(onehot, BF16), preferred_element_type=F32)
@@ -905,7 +920,7 @@
     def put(which, after):
         nonlocal ffn_grads, attn_grads
         group = 8
-        sources = sums[which].sources
+        sources, info = sums[which].sources, sums[which].route.info
         if which < chunks:
             ffn_grads = assemble(
                 info, slabs, functools.partial(ffn_spread, width, part, slabs, group), [w_in.shape, w_out.shape],
@@ -930,11 +945,11 @@
             after = (*after, *late.pop(0))
         which = int(op[1]) if len(op) > 1 else 0
         if op[0] == "F":
-            end = (flat(x1), ffn_gain, attT, wo) if which == chunks - 1 else None
+            end = (ffn_gain, flat(x1), attT, wo) if which == chunks - 1 else None
             keep, send, *acc = ffn_chunk(
                 info, lengths, slabs, flat(h2), flat(out_grad), w_in, w_out, which * part, part, sub, acc, after, end
             )
-            sums.append(Sum(route, keep, send))
+            sums.append(Sum(straight, keep, send))
             if end:
                 mixed, dres, datt, gwo, ggain2 = acc
             after = (keep,)
@@ -946,13 +961,13 @@
             )
             ds += [flat(dq), flat(dk), flat(dv)]
             diags.append(diag)
-            sums.append(Sum(route, keep, send))
+            sums.append(Sum(straight, keep, send))
             after = (keep,)
         elif op == "T":
             tgrad, ggain1 = tokgrad(flat(tokens), dres, attn_gain, ds, wq, wk, wv, after)
             diag = jnp.concatenate(diags).reshape(heads, 6 * TILE)
             gtable = jnp.einsum("hm,mb->bh", diag, jnp.asarray(spread), precision=lax.Precision.HIGHEST)
-            small = SmallSum(route, (ggain1, ggain2, gtable))
+            small = SmallSum(straight, (ggain1, ggain2, gtable))
             after = (ggain1,)
         elif op == "D":
             after = (spacer(after),)

time: 407 us -> 390 us (0.958)
  local copies, waits for them, and re-layouts: 26.5 us -> 17.1 us
  Pallas kernels: 242 us -> 237 us
    unnamed x100 -> x72, local copies, waits for them, and re-layouts: 23.3 us -> 14.4 us
    pallas_call x2, Pallas kernels: 55.9 us -> 51.3 us  [ffn_chunk(): pl.pallas_call(functools.partial(ffn_kernel, steps, slabs, not acc, bool(...]
  transfers between devices with their start and end apart: 49 -> 49, of which waited for: 18 -> 18; matrix products, arithmetic and copies ran while one was open for 1% -> 1% of each run, Pallas kernels for 46% -> 47%
where the time goes in v4:
time: 390 us; the launch traced here: 382 us
  Pallas kernels  237 us (61%)
  waiting for transfers between devices  75.5 us (19%)
  starting transfers between devices  46.4 us (12%)
  local copies, waits for them, and re-layouts  17.1 us (4%)
    ppermute x36, waiting for transfers between devices, exchange(): return lax.ppermute(x, ('rows', 'blk'), moves)  62.8 us
    pallas_call x25, Pallas kernels, add_shares(): pl.pallas_call(functools.partial(add_kernel, len(sources), outs), grid_sp...  56 us
    pallas_call x2, Pallas kernels, ffn_chunk(): pl.pallas_call(functools.partial(ffn_kernel, steps, slabs, not acc, bool(...  51.3 us
    ppermute x36, starting transfers between devices, exchange(): return lax.ppermute(x, ('rows', 'blk'), moves)  44.9 us
    pallas_call x2, Pallas kernels, attn_bwd(): pl.pallas_call(functools.partial(attn_bwd_kernel, slabs, first, len(more)...  42 us
    pallas_call x4, Pallas kernels, assemble(): pl.pallas_call(functools.partial(assemble_kernel, spread, len(outs)), gri...  29.8 us
    pallas_call x1, Pallas kernels, attn_fwd(): pl.pallas_call(attn_fwd_kernel, grid_spec=pltpu.PrefetchScalarGridSpec(nu...  23.1 us
    pallas_call x12, Pallas kernels, join(): pl.pallas_call(functools.partial(join_kernel, column, ways), in_specs=[pl...  21.9 us
  transfers between devices with their start and end apart: 49, of which 18 were waited for; matrix products, arithmetic and copies ran while one was open for 1% of the time, Pallas kernels for 47%

profile of v4, /device:TPU:0, one launch (start us, length us, event | category | flops | bytes accessed | tf_op | source)
XLA Modules:
  0.0 382.2 jit_solution(2951459232756760322)
XLA Ops:
  3.4 23.1 %attn_fwd.1 = (bf16[2,768,512]{2,1,0:T(8,128)(2,1)}, bf16[2,512,768]{2,1,0:T(8,128)(2,1)}, bf16[2,512,768]{2,1,0:T(8,128)(2,1)}, bf16[2,512,768]{2,1,0:T(8,128)(...) custom-call(s32[2,8]{1,0:T(2,128)} %len_ref.9, ...), custom_call_target="tpu_custom_call" | custom-call | flops 99999997952 | bytes 1 | tf_op jit(solution)/shard_map/attn_fwd/pallas_call | solution.py:174
  26.5 23.4 %ffn.2 = (f32[4608,256]{1,0:T(8,128)}, f32[4608,256]{1,0:T(8,128)}, f32[1024,768]{1,0:T(8,128)}, f32[1024,768]{1,0:T(8,128)}) custom-call(s32[30]{0:T(128)} %dynamic-slice_bitcast_fusion.info_ref, s32[2,8]{1,0:T(2,128)} %len_ref.9, bf16[1024,768]{1,0:T(8,128)(2,1)} %bitcast.33, bf16[1024,768]{1,0:T(8,128)(2,1)} %bitcast.25, bf16[768,3072]{1,0:T(8,128)(2,1)} %win_ref.3, ...), custom_call_target="tpu_custom_call" | custom-call | flops 99999997952 | bytes 1 | tf_op jit(solution)/shard_map/ffn/pallas_call | solution.py:390
  50.4 7.9 %collective-permute-done.refs_1_.refs_5_ = f32[4608,256]{1,0:T(8,128)} collective-permute-done((f32[4608,256]{1,0:T(8,128)}, f32[4608,256]{1,0:T(8,128)}, u32[]{:S(2)}, u32[]{:S(2)}) %collective-permute-start) | collective-permute-done | bytes 4718624 | tf_op jit(solution)/shard_map/ppermute | solution.py:650
  58.3 4.2 %add_shares.25.refs_6_ = f32[2304,256]{1,0:T(8,128)} custom-call(s32[30]{0:T(128)} %dynamic-slice_bitcast_fusion.info_ref, f32[4608,256]{1,0:T(8,128)} %get-tuple-element.76.refs_0_.refs_2_.refs_4_, f32[4608,256]{1,0:T(8,128)} %collective-permute-done.refs_1_.refs_5_, f32[4608,256]{1,0:T(8,128)} %get-tuple-element.76.refs_0_.refs_2_.refs_4_), custom_call_target="tpu_custom_call" | custom-call | flops 1 | bytes 1 | tf_op jit(solution)/shard_map/add_shares/pallas_call | solution.py:674
  65.3 28.0 %ffn.3 = (f32[4608,256]{1,0:T(8,128)}, f32[4608,256]{1,0:T(8,128)}, bf16[1024,768]{1,0:T(8,128)(2,1)}, f32[1024,768]{1,0:T(8,128)}, bf16[1024,768]{1,0:T(8,128)(...) custom-call(s32[30]{0:T(128)} %dynamic-slice_bitcast_fusion.info_ref, s32[2,8]{1,0:T(2,128)} %len_ref.9, ...), custom_call_target="tpu_custom_call" | custom-call | flops 99999997952 | bytes 1 | tf_op jit(solution)/shard_map/ffn/pallas_call | solution.py:390
  94.7 3.8 %add_shares.26.refs_1_ = f32[1152,256]{1,0:T(8,128)} custom-call(s32[30]{0:T(128)} %dynamic-slice_bitcast_fusion.info_ref, f32[4608,256]{1,0:T(8,128)} %get-tuple-element.76.refs_0_.refs_2_.refs_4_, f32[4608,256]{1,0:T(8,128)} %collective-permute-done.refs_1_.refs_5_, f32[2304,256]{1,0:T(8,128)} %collective-permute-done.1.refs_2_.refs_6_, ...), custom_call_target="tpu_custom_call" | custom-call | flops 1 | bytes 1 | tf_op jit(solution)/shard_map/add_shares/pallas_call | solution.py:674
  100.0 21.7 %attn_bwd.2 = (bf16[2,512,384]{2,1,0:T(8,128)(2,1)}, bf16[2,512,384]{2,1,0:T(8,128)(2,1)}, bf16[2,512,384]{2,1,0:T(8,128)(2,1)}, f32[3,2,768]{2,1,0:T(2,128)}, f32[1920,384]{1,0:T(8,128)}, /*index=5*/f32[1920,384]{1,0:T(8,128)}) custom-call(s32[30]{0:T(128)} %dynamic-slice_bitcast_fusion.info_ref, s32[2,8]{1,0:T(2,128)} %len_ref.9, ...), custom_call_target="tpu_custom_call" | custom-call | flops 99999997952 | bytes 1 | tf_op jit(solution)/shard_map/attn_bwd/pallas_call | solution.py:535
  121.8 4.2 %add_shares.27.refs_8_ = f32[2304,256]{1,0:T(8,128)} custom-call(s32[30]{0:T(128)} %dynamic-slice_bitcast_fusion.info_ref, f32[4608,256]{1,0:T(8,128)} %get-tuple-element.87.refs_3_.refs_0_.refs_4_, f32[4608,256]{1,0:T(8,128)} %collective-permute-done.3.refs_1_.refs_5_, f32[1920,384]{1,0:T(8,128)} %get-tuple-element.92.refs_2_.refs_0_.refs_4_), custom_call_target="tpu_custom_call" | custom-call | flops 1 | bytes 1 | tf_op jit(solution)/shard_map/add_shares/pallas_call | solution.py:674
  126.7 4.1 %add_shares.28 = (f32[576,256]{1,0:T(8,128)}, f32[576,256]{1,0:T(8,128)}) custom-call(s32[30]{0:T(128)} %dynamic-slice_bitcast_fusion.info_ref, f32[4608,256]{1,0:T(8,128)} %get-tuple-element.76.refs_0_.refs_2_.refs_4_, f32[4608,256]{1,0:T(8,128)} %collective-permute-done.refs_1_.refs_5_, f32[2304,256]{1,0:T(8,128)} %collective-permute-done.1.refs_2_.refs_6_, ...), custom_call_target="tpu_custom_call" | custom-call | flops 1 | bytes 1 | tf_op jit(solution)/shard_map/add_shares/pallas_call | solution.py:674
  132.4 20.2 %attn_bwd.3 = (bf16[2,512,384]{2,1,0:T(8,128)(2,1)}, bf16[2,512,384]{2,1,0:T(8,128)(2,1)}, bf16[2,512,384]{2,1,0:T(8,128)(2,1)}, f32[3,2,768]{2,1,0:T(2,128)}, f32[1152,384]{1,0:T(8,128)}, /*index=5*/f32[1152,384]{1,0:T(8,128)}) custom-call(s32[30]{0:T(128)} %dynamic-slice_bitcast_fusion.info_ref, s32[2,8]{1,0:T(2,128)} %len_ref.9, ...), custom_call_target="tpu_custom_call" | custom-call | flops 99999997952 | bytes 1 | tf_op jit(solution)/shard_map/attn_bwd/pallas_call | solution.py:535
  159.2 3.8 %add_shares.30.refs_2_ = f32[1152,256]{1,0:T(8,128)} custom-call(s32[30]{0:T(128)} %dynamic-slice_bitcast_fusion.info_ref, f32[4608,256]{1,0:T(8,128)} %get-tuple-element.87.refs_3_.refs_0_.refs_4_, f32[4608,256]{1,0:T(8,128)} %collective-permute-done.3.refs_1_.refs_5_, f32[2304,256]{1,0:T(8,128)} %collective-permute-done.8.refs_2_.refs_6_, ...), custom_call_target="tpu_custom_call" | custom-call | flops 1 | bytes 1 | tf_op jit(solution)/shard_map/add_shares/pallas_call | solution.py:674
  179.5 4.1 %add_shares.34 = (f32[576,256]{1,0:T(8,128)}, f32[576,256]{1,0:T(8,128)}) custom-call(s32[30]{0:T(128)} %dynamic-slice_bitcast_fusion.info_ref, f32[4608,256]{1,0:T(8,128)} %get-tuple-element.87.refs_3_.refs_0_.refs_4_, f32[4608,256]{1,0:T(8,128)} %collective-permute-done.3.refs_1_.refs_5_, f32[2304,256]{1,0:T(8,128)} %collective-permute-done.8.refs_2_.refs_6_, ...), custom_call_target="tpu_custom_call" | custom-call | flops 1 | bytes 1 | tf_op jit(solution)/shard_map/add_shares/pallas_call | solution.py:674
  186.0 5.6 %collective-permute-done.9.refs_1_ = f32[288,256]{1,0:T(8,128)S(1)} collective-permute-done((f32[288,256]{1,0:T(8,128)S(1)}, f32[288,256]{1,0:T(8,128)S(1)}, u32[]{:S(2)}, u32[]{:S(2)}) %collective-permute-start.9) | collective-permute-done | bytes 294944 | tf_op jit(solution)/shard_map/ppermute | solution.py:646
  195.2 9.7 %tokgrad.1 = (bf16[1024,768]{1,0:T(8,128)(2,1)}, f32[1,768]{1,0:T(1,128)}) custom-call(bf16[1024,768]{1,0:T(8,128)(2,1)} %bitcast.27, f32[1024,768]{1,0:T(8,128)} %get-tuple-element.79.dres_ref, bf16[768]{0:T(1024)(128)(2,1)} %gain_ref.1, bf16[768,768]{1,0:T(8,128)(2,1)} %wq_ref.3, bf16[768,768]{1,0:T(8,128)(2,1)} %wk_ref.3, bf16[768,768]{1,0:T(8,128)(2,1)} %wv_ref.3, ...), custom_call_target="tpu_custom_call" | custom-call | flops 99999997952 | bytes 1 | tf_op jit(solution)/shard_map/tokgrad/pallas_call | solution.py:592
  253.4 5.3 %collective-permute-done.21.refs_1_ = f32[288,256]{1,0:T(8,128)S(1)} collective-permute-done((f32[288,256]{1,0:T(8,128)S(1)}, f32[288,256]{1,0:T(8,128)S(1)}, u32[]{:S(2)}, u32[]{:S(2)}) %collective-permute-start.21) | collective-permute-done | bytes 294944 | tf_op jit(solution)/shard_map/ppermute | solution.py:646
  277.1 5.2 %collective-permute-done.26.refs_1_ = f32[576,256]{1,0:T(8,128)} collective-permute-done((f32[576,256]{1,0:T(8,128)S(1)}, f32[576,256]{1,0:T(8,128)}, u32[]{:S(2)}, u32[]{:S(2)}) %collective-permute-start.26) | collective-permute-done | bytes 589856 | tf_op jit(solution)/shard_map/ppermute | solution.py:646
  294.8 10.3 %collective-permute-done.38.refs_1_ = f32[1152,256]{1,0:T(8,128)S(1)} collective-permute-done((f32[1152,256]{1,0:T(8,128)S(1)}, f32[1152,256]{1,0:T(8,128)S(1)}, u32[]{:S(2)}, u32[]{:S(2)}) %collective-permute-start.38) | collective-permute-done | bytes 1179680 | tf_op jit(solution)/shard_map/ppermute | solution.py:646
  311.1 9.2 %assemble.4 = (f32[768,3072]{1,0:T(8,128)}, f32[3072,768]{1,0:T(8,128)}) custom-call(s32[30]{0:T(128)} %dynamic-slice_bitcast_fusion.info_ref, f32[2304,256]{1,0:T(8,128)} %join.14.refs_0_, f32[2304,256]{1,0:T(8,128)} %collective-permute-done.36.refs_2_.refs_1_, f32[2304,256]{1,0:T(8,128)} %copy-done.8, f32[2304,256]{1,0:T(8,128)} %collective-permute-done.37.refs_3_, ...), custom_call_target="tpu_custom_call" | custom-call | flops 99999997952 | bytes 1 | tf_op jit(solution)/shard_map/assemble/pallas_call | solution.py:861
  328.0 9.4 %collective-permute-done.40.refs_1_ = f32[240,384]{1,0:T(8,128)S(1)} collective-permute-done((f32[240,384]{1,0:T(8,128)S(1)}, f32[240,384]{1,0:T(8,128)S(1)}, u32[]{:S(2)}, u32[]{:S(2)}) %collective-permute-start.40) | collective-permute-done | bytes 368672 | tf_op jit(solution)/shard_map/ppermute | solution.py:646
  340.7 9.1 %collective-permute-done.41.refs_1_ = f32[480,384]{1,0:T(8,128)S(1)} collective-permute-done((f32[480,384]{1,0:T(8,128)S(1)}, f32[480,384]{1,0:T(8,128)S(1)}, u32[]{:S(2)}, u32[]{:S(2)}) %collective-permute-start.41) | collective-permute-done | bytes 737312 | tf_op jit(solution)/shard_map/ppermute | solution.py:646
  352.8 4.9 %assemble.5 = (f32[768,768]{1,0:T(8,128)}, f32[768,768]{1,0:T(8,128)}, f32[768,768]{1,0:T(8,128)}) custom-call(s32[30]{0:T(128)} %dynamic-slice_bitcast_fusion.info_ref, f32[576,384]{1,0:T(8,128)} %join.19.refs_0_, f32[576,384]{1,0:T(8,128)} %collective-permute-done.45.refs_1_, f32[576,384]{1,0:T(8,128)} %collective-permute-done.32.refs_3_.refs_2_, ...), custom_call_target="tpu_custom_call" | custom-call | flops 99999997952 | bytes 1 | tf_op jit(solution)/shard_map/assemble/pallas_call | solution.py:861
  357.7 9.2 %assemble.7 = (f32[768,3072]{1,0:T(8,128)}, f32[3072,768]{1,0:T(8,128)}) custom-call(s32[30]{0:T(128)} %dynamic-slice_bitcast_fusion.info_ref, f32[2304,256]{1,0:T(8,128)} %join.20.refs_4_.refs_0_, f32[2304,256]{1,0:T(8,128)} %collective-permute-done.47.refs_1_.refs_6_, ...), custom_call_target="tpu_custom_call", output_to_operand_aliasing={{0}: (5, {}), {1}: (6, {})} | custom-call | flops 99999997952 | bytes 1 | tf_op jit(solution)/shard_map/assemble/pallas_call | solution.py:861
  366.9 5.0 %collective-permute-done.42.refs_0_.refs_1_ = f32[960,384]{1,0:T(8,128)} collective-permute-done((f32[960,384]{1,0:T(8,128)}, f32[960,384]{1,0:T(8,128)}, u32[]{:S(2)}, u32[]{:S(2)}) %collective-permute-start.42) | collective-permute-done | bytes 1474592 | tf_op jit(solution)/shard_map/ppermute | solution.py:646
  375.5 6.5 %assemble.6 = (f32[768,768]{1,0:T(8,128)}, f32[768,768]{1,0:T(8,128)}, f32[768,768]{1,0:T(8,128)}, f32[768,768]{1,0:T(8,128)}) custom-call(s32[30]{0:T(128)} %dynamic-slice_bitcast_fusion.info_ref, f32[960,384]{1,0:T(8,128)} %join.23.refs_4_.refs_0_, ...), custom_call_target="tpu_custom_call", output_to_operand_aliasing={{0}: (5, {}), {1}: (6, {}), {2}: (7, {})} | custom-call | flops 99999997952 | bytes 1 | tf_op jit(solution)/shard_map/assemble/pallas_call | solution.py:861
  (214 shorter events, 142.8 us)
Async XLA Ops:
  62.5 32.2 %collective-permute-start.1 = (f32[2304,256]{1,0:T(8,128)}, f32[2304,256]{1,0:T(8,128)}, u32[]{:S(2)}, u32[]{:S(2)}) collective-permute-start(f32[2304,256]{1,0:T(8,128)} %add_shares.25.refs_6_), channel_id=1, source_target_pairs={{0,2},{1,5},{2,0},{3,7},{4,6},{5,1},{6,4},{7,3},{8,10},{9,13},{10,... | collective-permute-start | bytes 7077896 | tf_op jit(solution)/shard_map/ppermute | solution.py:646
  93.3 28.5 %collective-permute-start.3 = (f32[4608,256]{1,0:T(8,128)}, f32[4608,256]{1,0:T(8,128)}, u32[]{:S(2)}, u32[]{:S(2)}) collective-permute-start(f32[4608,256]{1,0:T(8,128)} %get-tuple-element.91), channel_id=1, source_target_pairs={{0,1},{1,0},{2,3},{3,2},{4,5},{5,4},{6,7},{7,6},{8,9},{9,8},{10,11... | collective-permute-start | bytes 14155784 | tf_op jit(solution)/shard_map/ppermute | solution.py:650
  98.5 28.2 %collective-permute-start.2 = (f32[1152,256]{1,0:T(8,128)}, f32[1152,256]{1,0:T(8,128)}, u32[]{:S(2)}, u32[]{:S(2)}) collective-permute-start(f32[1152,256]{1,0:T(8,128)} %add_shares.26.refs_1_), channel_id=1, source_target_pairs={{0,4},{1,3},{2,6},{3,1},{4,0},{5,7},{6,2},{7,5},{8,12},{9,11},{10,... | collective-permute-start | bytes 3538952 | tf_op jit(solution)/shard_map/ppermute | solution.py:646
  121.7 42.8 %collective-permute-start.7 = (f32[1920,384]{1,0:T(8,128)}, f32[1920,384]{1,0:T(8,128)}, u32[]{:S(2)}, u32[]{:S(2)}) collective-permute-start(f32[1920,384]{1,0:T(8,128)} %get-tuple-element.102), channel_id=1, source_target_pairs={{0,1},{1,0},{2,3},{3,2},{4,5},{5,4},{6,7},{7,6},{8,9},{9,8},{10,11... | collective-permute-start | bytes 8847368 | tf_op jit(solution)/shard_map/ppermute | solution.py:650
  126.0 33.2 %collective-permute-start.8 = (f32[2304,256]{1,0:T(8,128)}, f32[2304,256]{1,0:T(8,128)}, u32[]{:S(2)}, u32[]{:S(2)}) collective-permute-start(f32[2304,256]{1,0:T(8,128)} %add_shares.27.refs_8_), channel_id=1, source_target_pairs={{0,2},{1,5},{2,0},{3,7},{4,6},{5,1},{6,4},{7,3},{8,10},{9,13},{10,... | collective-permute-start | bytes 7077896 | tf_op jit(solution)/shard_map/ppermute | solution.py:646
  130.8 21.9 %collective-permute-start.4 = (f32[576,256]{1,0:T(8,128)}, f32[576,256]{1,0:T(8,128)}, u32[]{:S(2)}, u32[]{:S(2)}) collective-permute-start(f32[576,256]{1,0:T(8,128)} %get-tuple-element.93.refs_0_), channel_id=1, source_target_pairs={{0,8},{1,9},{2,10},{3,11},{4,12},{5,13},{6,14},{7,15},{8,0},{9,1},... | collective-permute-start | bytes 1769480 | tf_op jit(solution)/shard_map/ppermute | solution.py:646
  176.7 30.4 %collective-permute-start.14 = (f32[576,384]{1,0:T(8,128)}, f32[576,384]{1,0:T(8,128)}, u32[]{:S(2)}, u32[]{:S(2)}) collective-permute-start(f32[576,384]{1,0:T(8,128)} %add_shares.32.refs_0_), channel_id=1, source_target_pairs={{0,2},{1,5},{2,0},{3,7},{4,6},{5,1},{6,4},{7,3},{8,10},{9,13},{10,... | collective-permute-start | bytes 2654216 | tf_op jit(solution)/shard_map/ppermute | solution.py:646
  178.1 49.4 %collective-permute-start.19 = (f32[960,384]{1,0:T(8,128)}, f32[960,384]{1,0:T(8,128)}, u32[]{:S(2)}, u32[]{:S(2)}) collective-permute-start(f32[960,384]{1,0:T(8,128)} %add_shares.31.refs_0_), channel_id=1, source_target_pairs={{0,2},{1,5},{2,0},{3,7},{4,6},{5,1},{6,4},{7,3},{8,10},{9,13},{10,... | collective-permute-start | bytes 4423688 | tf_op jit(solution)/shard_map/ppermute | solution.py:646
  183.7 26.9 %collective-permute-start.13 = (f32[576,256]{1,0:T(8,128)}, f32[576,256]{1,0:T(8,128)}, u32[]{:S(2)}, u32[]{:S(2)}) collective-permute-start(f32[576,256]{1,0:T(8,128)} %get-tuple-element.103.refs_2_), channel_id=1, source_target_pairs={{0,8},{1,9},{2,10},{3,11},{4,12},{5,13},{6,14},{7,15},{8,0},{9,1},... | collective-permute-start | bytes 1769480 | tf_op jit(solution)/shard_map/ppermute | solution.py:646
  195.1 21.7 %collective-permute-start.12 = (f32[576,256]{1,0:T(8,128)}, f32[576,256]{1,0:T(8,128)}, u32[]{:S(2)}, u32[]{:S(2)}) collective-permute-start(f32[576,256]{1,0:T(8,128)} %join.12.refs_6_.refs_0_), channel_id=1, source_target_pairs={{0,8},{1,9},{2,10},{3,11},{4,12},{5,13},{6,14},{7,15},{8,0},{9,1},... | collective-permute-start | bytes 1769480 | tf_op jit(solution)/shard_map/ppermute | solution.py:646
  214.0 22.3 %collective-permute-start.16 = (f32[288,256]{1,0:T(8,128)}, f32[288,256]{1,0:T(8,128)}, u32[]{:S(2)}, u32[]{:S(2)}) collective-permute-start(f32[288,256]{1,0:T(8,128)} %get-tuple-element.110.refs_2_), channel_id=1, source_target_pairs={{0,16},{1,17},{2,18},{3,19},{4,20},{5,21},{6,22},{7,23},{8,24},{9,... | collective-permute-start | bytes 884744 | tf_op jit(solution)/shard_map/ppermute | solution.py:646
  219.7 21.6 %collective-permute-start.23 = (f32[1152,256]{1,0:T(8,128)}, f32[1152,256]{1,0:T(8,128)}, u32[]{:S(2)}, u32[]{:S(2)}) collective-permute-start(f32[1152,256]{1,0:T(8,128)} %join.13.refs_0_), channel_id=1, source_target_pairs={{0,4},{1,3},{2,6},{3,1},{4,0},{5,7},{6,2},{7,5},{8,12},{9,11},{10,... | collective-permute-start | bytes 3538952 | tf_op jit(solution)/shard_map/ppermute | solution.py:646
  230.7 32.5 %collective-permute-start.29 = (f32[480,384]{1,0:T(8,128)}, f32[480,384]{1,0:T(8,128)}, u32[]{:S(2)}, u32[]{:S(2)}) collective-permute-start(f32[480,384]{1,0:T(8,128)} %add_shares.39.refs_4_), channel_id=1, source_target_pairs={{0,4},{1,3},{2,6},{3,1},{4,0},{5,7},{6,2},{7,5},{8,12},{9,11},{10,... | collective-permute-start | bytes 2211848 | tf_op jit(solution)/shard_map/ppermute | solution.py:646
  237.8 20.9 %collective-permute-start.21 = (f32[288,256]{1,0:T(8,128)S(1)}, f32[288,256]{1,0:T(8,128)S(1)}, u32[]{:S(2)}, u32[]{:S(2)}) collective-permute-start(f32[288,256]{1,0:T(8,128)S(1)} %add_shares.41.refs_2_.refs_0_), channel_id=1, source_target_pairs={{0,16},{1,17},{2,18},{3,19},{4,20},{5,21},{6,22},{7,23},{8,24},{9,... | collective-permute-start | bytes 884744 | tf_op jit(solution)/shard_map/ppermute | solution.py:646
  245.0 30.0 %collective-permute-start.36 = (f32[2304,256]{1,0:T(8,128)}, f32[2304,256]{1,0:T(8,128)}, u32[]{:S(2)}, u32[]{:S(2)}) collective-permute-start(f32[2304,256]{1,0:T(8,128)} %join.14.refs_0_), channel_id=1, source_target_pairs={{0,2},{1,5},{2,0},{3,7},{4,6},{5,1},{6,4},{7,3},{8,10},{9,13},{10,... | collective-permute-start | bytes 7077896 | tf_op jit(solution)/shard_map/ppermute | solution.py:646
  261.2 21.2 %collective-permute-start.26 = (f32[576,256]{1,0:T(8,128)S(1)}, f32[576,256]{1,0:T(8,128)}, u32[]{:S(2)}, u32[]{:S(2)}) collective-permute-start(f32[576,256]{1,0:T(8,128)S(1)} %join.15.refs_2_.refs_0_), channel_id=1, source_target_pairs={{0,8},{1,9},{2,10},{3,11},{4,12},{5,13},{6,14},{7,15},{8,0},{9,1},... | collective-permute-start | bytes 1769480 | tf_op jit(solution)/shard_map/ppermute | solution.py:646
  275.1 36.0 %collective-permute-start.37 = (f32[2304,256]{1,0:T(8,128)}, f32[2304,256]{1,0:T(8,128)}, u32[]{:S(2)}, u32[]{:S(2)}) collective-permute-start(f32[2304,256]{1,0:T(8,128)} %collective-permute-done.36.refs_2_.refs_1_), channel_id=1, source_target_pairs={{0,1},{1,0},{2,3},{3,2},{4,5},{5,4},{6,7},{7,6},{8,9},{9,8},{10,11... | collective-permute-start | bytes 7077896 | tf_op jit(solution)/shard_map/ppermute | solution.py:650
  275.1 18.2 %collective-permute-start.33 = (f32[240,384]{1,0:T(8,128)}, f32[240,384]{1,0:T(8,128)S(1)}, u32[]{:S(2)}, u32[]{:S(2)}) collective-permute-start(f32[240,384]{1,0:T(8,128)} %get-tuple-element.116.refs_2_), channel_id=1, source_target_pairs={{0,8},{1,9},{2,10},{3,11},{4,12},{5,13},{6,14},{7,15},{8,0},{9,1},... | collective-permute-start | bytes 1105928 | tf_op jit(solution)/shard_map/ppermute | solution.py:646
  284.3 20.7 %collective-permute-start.38 = (f32[1152,256]{1,0:T(8,128)S(1)}, f32[1152,256]{1,0:T(8,128)S(1)}, u32[]{:S(2)}, u32[]{:S(2)}) collective-permute-start(f32[1152,256]{1,0:T(8,128)S(1)} %join.18.refs_2_.refs_0_), channel_id=1, source_target_pairs={{0,4},{1,3},{2,6},{3,1},{4,0},{5,7},{6,2},{7,5},{8,12},{9,11},{10,... | collective-permute-start | bytes 3538952 | tf_op jit(solution)/shard_map/ppermute | solution.py:646
  294.5 33.5 %collective-permute-start.45 = (f32[576,384]{1,0:T(8,128)}, f32[576,384]{1,0:T(8,128)}, u32[]{:S(2)}, u32[]{:S(2)}) collective-permute-start(f32[576,384]{1,0:T(8,128)} %join.19.refs_0_), channel_id=1, source_target_pairs={{0,2},{1,5},{2,0},{3,7},{4,6},{5,1},{6,4},{7,3},{8,10},{9,13},{10,... | collective-permute-start | bytes 2654216 | tf_op jit(solution)/shard_map/ppermute | solution.py:646
  307.6 33.1 %collective-permute-start.47 = (f32[2304,256]{1,0:T(8,128)}, f32[2304,256]{1,0:T(8,128)}, u32[]{:S(2)}, u32[]{:S(2)}) collective-permute-start(f32[2304,256]{1,0:T(8,128)} %join.20.refs_4_.refs_0_), channel_id=1, source_target_pairs={{0,2},{1,5},{2,0},{3,7},{4,6},{5,1},{6,4},{7,3},{8,10},{9,13},{10,... | collective-permute-start | bytes 7077896 | tf_op jit(solution)/shard_map/ppermute | solution.py:646
  328.0 24.8 %collective-permute-start.46 = (f32[576,384]{1,0:T(8,128)}, f32[576,384]{1,0:T(8,128)}, u32[]{:S(2)}, u32[]{:S(2)}) collective-permute-start(f32[576,384]{1,0:T(8,128)} %collective-permute-done.45.refs_1_), channel_id=1, source_target_pairs={{0,1},{1,0},{2,3},{3,2},{4,5},{5,4},{6,7},{7,6},{8,9},{9,8},{10,11... | collective-permute-start | bytes 2654216 | tf_op jit(solution)/shard_map/ppermute | solution.py:650
  352.1 19.7 %collective-permute-start.42 = (f32[960,384]{1,0:T(8,128)}, f32[960,384]{1,0:T(8,128)}, u32[]{:S(2)}, u32[]{:S(2)}) collective-permute-start(f32[960,384]{1,0:T(8,128)} %join.23.refs_4_.refs_0_), channel_id=1, source_target_pairs={{0,2},{1,5},{2,0},{3,7},{4,6},{5,1},{6,4},{7,3},{8,10},{9,13},{10,... | collective-permute-start | bytes 4423688 | tf_op jit(solution)/shard_map/ppermute | solution.py:646
  352.8 19.7 %collective-permute-start.43 = (f32[960,384]{1,0:T(8,128)}, f32[960,384]{1,0:T(8,128)}, u32[]{:S(2)}, u32[]{:S(2)}) collective-permute-start(f32[960,384]{1,0:T(8,128)} %join.23.refs_4_.refs_0_), channel_id=1, source_target_pairs={{0,1},{1,0},{2,3},{3,2},{4,5},{5,4},{6,7},{7,6},{8,9},{9,8},{10,11... | collective-permute-start | bytes 4423688 | tf_op jit(solution)/shard_map/ppermute | solution.py:650
  (60 other events, 460.3 us)

commit v5 on v4

--- a/solution.py
+++ b/solution.py
@@ -225,13 +225,13 @@
     acc_in = [] if first else [refs.pop(0), refs.pop(0)]
     if last:
         gain_ref, late = refs[0], refs[1:4]
-        keep_ref, send_ref, mixed_out, dres_out, datt_out, gwo_ref, ggain_ref = refs[-22:-15]
+        keep_ref, *send_refs, mixed_out, dres_out, datt_out, gwo_ref, ggain_ref = refs[-23:-15]
         mix_ref, dtwo_ref, h2T_ref, act_ref, dpre_ref, gin_ref, gout_ref, sems, acc_sems, mixed_ref, dres_ref, datt_ref = refs[-15:-3]
         x1_ref, attT_ref, wo_ref = refs[-3:]
         first_late = acc_sems.shape[0] - 3
         late = [pltpu.make_async_copy(a, b, acc_sems.at[first_late + i]) for i, (a, b) in enumerate(zip(late, refs[-3:]))]
     else:
-        keep_ref, send_ref = refs[-13:-11]
+        keep_ref, *send_refs = refs[-14:-11]
         acc_out = refs[-11:-9]
         mix_ref, dtwo_ref, h2T_ref, act_ref, dpre_ref, gin_ref, gout_ref, sems, acc_sems = refs[-9:]
     step = pl.program_id(0)
@@ -244,19 +244,28 @@
     totals = (mix_ref, dtwo_ref)
 
     def moves(at):
-        def of_in(ref):
-            return [
-                (
-                    gin_ref.at[at, i * in_rows * tall : (i + 1) * in_rows * tall, :],
-                    ref.at[pl.ds(pl.multiple_of(i * piece + at * (in_rows * tall), 8), in_rows * tall), :],
-                )
-                for i in range(slabs)
-            ]
-
-        def of_out(ref):
-            return [(gout_ref.at[at], ref.at[pl.ds(pl.multiple_of(at * (here * piece), 8), here * piece), :])]
-
-        return place(info_ref[0], of_in, of_out, keep_ref, send_ref, sems.at[at])
+        core, first_half = info_ref[0], 1 - info_ref[4] % 2
+        half = slabs // 2
+        block = in_rows * tall
+        cases = []
+        for c in range(2):
+            for f in range(2):
+                here_now = (core == c) & (first_half == f)
+                copies = []
+                for i in range(slabs):
+                    src = gin_ref.at[at, i * block : (i + 1) * block, :]
+                    dst, row = (keep_ref, i) if c == 0 else (send_refs[0 if i // half == f else 1], i % half)
+                    dst = dst.at[pl.ds(pl.multiple_of(row * piece + at * block, 8), block), :]
+                    copies.append((src, dst, sems.at[at, 0, i]))
+                cases.append((here_now, copies))
+                if c == 1:
+                    dst = keep_ref.at[pl.ds(pl.multiple_of(at * (here * piece), 8), here * piece), :]
+                    cases.append((here_now, [(gout_ref.at[at], dst, sems.at[at, 1, 0])]))
+                else:
+                    for now in range(2):
+                        dst = send_refs[0 if now == f else 1]
+                        cases.append((here_now & (at == now), [(gout_ref.at[at], dst, sems.at[at, 1, 0])]))
+        return cases
 
     @pl.when(step == 0)
     def _():
@@ -360,8 +369,8 @@
     piece = width * (sub // 256)
     full = lambda a: pl.BlockSpec(a.shape, lambda s, *_: (0,) * a.ndim, pipeline_mode=pl.Buffered(1))
     f32 = lambda *s: jax.ShapeDtypeStruct(s, F32)
-    out_specs = [ANYWHERE] * 2
-    out_shape = [f32(steps * piece, 256)] * 2
+    out_specs = [ANYWHERE] * 3
+    out_shape = [f32(steps * piece, 256)] + [f32(steps * piece // 2, 256)] * 2
     scratch = [
         pltpu.VMEM((toks, width), F32),
         pltpu.VMEM((toks, width), F32),
@@ -714,10 +723,12 @@
 
 
 class Sum:
-    def __init__(self, route, keep, send):
+    def __init__(self, route, keep, *send):
         self.route = route
-        self.parts = [keep, swap_cores(send)]
-        self.begins = [0, 0]
+        self.parts = [keep] + [swap_cores(s) for s in send]
+        self.begins = [0] * len(self.parts)
+        if len(send) == 2:
+            self.begins[2] = 1
         self.shares = [keep.shape[0]]
         for ways in route.ways:
             if self.shares[-1] % (8 * ways):
@@ -739,9 +750,13 @@
     def send(self, after):
         phase = self.phase
         flips = (1,) if phase < 2 else (1, 0)
-        columns = [[self.route.columns[begin, phase + 1, flip] for begin in self.begins] for flip in flips]
+        parts = self.parts
+        columns = [[self.route.columns.get((begin, phase + 1, flip)) for begin in self.begins] for flip in flips]
+        if phase == 0 and len(parts) == 3:
+            parts, columns = parts[:2], [[columns[0][0], None]]
+            self.parts, self.begins = [self.parts[0], self.parts[2]], [0, 1]
         limit = VMEM if phase < 3 else SMALL
-        outs = add_shares(self.route.info, self.parts, columns, self.shares[phase + 1], after, limit)
+        outs = add_shares(self.route.info, parts, columns, self.shares[phase + 1], after, limit)
         got = self.route.exchange(outs[0], phase, 1)
         if phase < 2:
             self.parts.append(got)
@@ -892,7 +907,7 @@
             outs[out][s * rows : (s + 1) * rows, column : column + source.shape[1]] = source[at : at + rows, :]
 
 
-ORDER = ("F0", "s0", "F1", "s0", "B0", "s1", "s0", "B1", "s0", "s1", "s2", "D", "s3", "D", "s0", "s1", "s0", "T", "s3", "s1", "s0", "D", "m", "s3", "s2", "s3", "s1", "m", "s0", "D", "s3", "s1", "m", "s3", "s2", "s3", "s1", "m", "s3", "D", "m", "s2", "s2", "s3", "s0", "s1", "s0", "s2", "s2", "s2", "s3", "s1", "s1", "s2", "D", "s2")
+ORDER = ("F0", "s0", "F1", "s0", "B0", "s1", "s0", "B1", "s0", "s1", "s2", "s0", "D", "s3", "D", "s1", "s0", "T", "s3", "s1", "s0", "D", "m", "s3", "s2", "D", "s3", "s1", "m", "s0", "D", "s3", "s1", "m", "s3", "s2", "s3", "s1", "m", "s3", "D", "m", "s2", "s2", "s3", "s0", "s1", "s0", "s2", "s2", "s2", "s3", "s1", "s1", "s2", "D", "s2")
 
 
 def on_device(tokens, lengths, attn_gain, wq, wk, wv, wo, table, ffn_gain, w_in, w_out, out_grad, *, size):
@@ -946,10 +961,10 @@
         which = int(op[1]) if len(op) > 1 else 0
         if op[0] == "F":
             end = (ffn_gain, flat(x1), attT, wo) if which == chunks - 1 else None
-            keep, send, *acc = ffn_chunk(
+            keep, send, rest, *acc = ffn_chunk(
                 info, lengths, slabs, flat(h2), flat(out_grad), w_in, w_out, which * part, part, sub, acc, after, end
             )
-            sums.append(Sum(straight, keep, send))
+            sums.append(Sum(straight, keep, send, rest))
             if end:
                 mixed, dres, datt, gwo, ggain2 = acc
             after = (keep,)

time: 390 us -> 384 us (0.985)
    ppermute x36, starting transfers between devices: 44.9 us -> 40.9 us  [exchange(): return lax.ppermute(x, ('rows', 'blk'), moves)]
    ppermute x13 -> x15, waiting for transfers between devices: 12.7 us -> 9.27 us  [swap_cores(): return lax.ppermute(x, 'blk', [(0, 1), (1, 0)])]
    unnamed x72 -> x70, local copies, waits for them, and re-layouts: 14.4 us -> 14.3 us
  transfers between devices with their start and end apart: 49 -> 51, of which waited for: 18 -> 19; matrix products, arithmetic and copies ran while one was open for 1% -> 1% of each run, Pallas kernels for 47% -> 49%
where the time goes in v5:
time: 384 us; the launch traced here: 376 us
  Pallas kernels  237 us (62%)
  waiting for transfers between devices  72.4 us (19%)
  starting transfers between devices  43.2 us (11%)
  local copies, waits for them, and re-layouts  17.6 us (5%)
    ppermute x36, waiting for transfers between devices, exchange(): return lax.ppermute(x, ('rows', 'blk'), moves)  63.1 us
    pallas_call x25, Pallas kernels, add_shares(): pl.pallas_call(functools.partial(add_kernel, len(sources), outs), grid_sp...  56.2 us
    pallas_call x2, Pallas kernels, ffn_chunk(): pl.pallas_call(functools.partial(ffn_kernel, steps, slabs, not acc, bool(...  51.5 us
    pallas_call x2, Pallas kernels, attn_bwd(): pl.pallas_call(functools.partial(attn_bwd_kernel, slabs, first, len(more)...  42 us
    ppermute x36, starting transfers between devices, exchange(): return lax.ppermute(x, ('rows', 'blk'), moves)  40.9 us
    pallas_call x4, Pallas kernels, assemble(): pl.pallas_call(functools.partial(assemble_kernel, spread, len(outs)), gri...  29.8 us
    pallas_call x1, Pallas kernels, attn_fwd(): pl.pallas_call(attn_fwd_kernel, grid_spec=pltpu.PrefetchScalarGridSpec(nu...  23.1 us
    pallas_call x12, Pallas kernels, join(): pl.pallas_call(functools.partial(join_kernel, column, ways), in_specs=[pl...  20.8 us
  transfers between devices with their start and end apart: 51, of which 19 were waited for; matrix products, arithmetic and copies ran while one was open for 1% of the time, Pallas kernels for 49%

profile of v5, /device:TPU:0, one launch (start us, length us, event | category | flops | bytes accessed | tf_op | source)
XLA Modules:
  0.0 376.1 jit_solution(4198538333374170153)
XLA Ops:
  3.4 23.1 %attn_fwd.1 = (bf16[2,768,512]{2,1,0:T(8,128)(2,1)}, bf16[2,512,768]{2,1,0:T(8,128)(2,1)}, bf16[2,512,768]{2,1,0:T(8,128)(2,1)}, bf16[2,512,768]{2,1,0:T(8,128)(...) custom-call(s32[2,8]{1,0:T(2,128)} %len_ref.9, ...), custom_call_target="tpu_custom_call" | custom-call | flops 99999997952 | bytes 1 | tf_op jit(solution)/shard_map/attn_fwd/pallas_call | solution.py:174
  26.5 23.3 %ffn.2 = (f32[4608,256]{1,0:T(8,128)}, f32[2304,256]{1,0:T(8,128)}, f32[2304,256]{1,0:T(8,128)}, f32[1024,768]{1,0:T(8,128)}, f32[1024,768]{1,0:T(8,128)}) custom-call(s32[30]{0:T(128)} %dynamic-slice_bitcast_fusion.info_ref, s32[2,8]{1,0:T(2,128)} %len_ref.9, bf16[1024,768]{1,0:T(8,128)(2,1)} %bitcast.33, bf16[1024,768]{1,0:T(8,128)(2,1)} %bitcast.25, ...), custom_call_target="tpu_custom_call" | custom-call | flops 99999997952 | bytes 1 | tf_op jit(solution)/shard_map/ffn/pallas_call | solution.py:399
  50.4 4.4 %collective-permute-done.refs_1_ = f32[2304,256]{1,0:T(8,128)} collective-permute-done((f32[2304,256]{1,0:T(8,128)}, f32[2304,256]{1,0:T(8,128)}, u32[]{:S(2)}, u32[]{:S(2)}) %collective-permute-start) | collective-permute-done | bytes 2359328 | tf_op jit(solution)/shard_map/ppermute | solution.py:659
  54.9 4.1 %add_shares.25.refs_6_ = f32[2304,256]{1,0:T(8,128)} custom-call(s32[30]{0:T(128)} %dynamic-slice_bitcast_fusion.info_ref, f32[4608,256]{1,0:T(8,128)} %get-tuple-element.78.refs_0_.refs_2_.refs_4_, f32[2304,256]{1,0:T(8,128)} %collective-permute-done.refs_1_, f32[4608,256]{1,0:T(8,128)} %get-tuple-element.78.refs_0_.refs_2_.refs_4_), custom_call_target="tpu_custom_call" | custom-call | flops 1 | bytes 1 | tf_op jit(solution)/shard_map/add_shares/pallas_call | solution.py:683
  61.9 28.1 %ffn.3 = (f32[4608,256]{1,0:T(8,128)}, f32[2304,256]{1,0:T(8,128)}, f32[2304,256]{1,0:T(8,128)}, bf16[1024,768]{1,0:T(8,128)(2,1)}, f32[1024,768]{1,0:T(8,128)},...) custom-call(s32[30]{0:T(128)} %dynamic-slice_bitcast_fusion.info_ref, s32[2,8]{1,0:T(2,128)} %len_ref.9, ...), custom_call_target="tpu_custom_call" | custom-call | flops 99999997952 | bytes 1 | tf_op jit(solution)/shard_map/ffn/pallas_call | solution.py:399
  91.9 3.8 %add_shares.26.refs_1_ = f32[1152,256]{1,0:T(8,128)} custom-call(s32[30]{0:T(128)} %dynamic-slice_bitcast_fusion.info_ref, f32[4608,256]{1,0:T(8,128)} %get-tuple-element.78.refs_0_.refs_2_.refs_4_, f32[2304,256]{1,0:T(8,128)} %collective-permute-done.1.refs_1_.refs_5_, f32[2304,256]{1,0:T(8,128)} %collective-permute-done.2.refs_2_.refs_6_, ...), custom_call_target="tpu_custom_call" | custom-call | flops 1 | bytes 1 | tf_op jit(solution)/shard_map/add_shares/pallas_call | solution.py:683
  97.3 21.6 %attn_bwd.2 = (bf16[2,512,384]{2,1,0:T(8,128)(2,1)}, bf16[2,512,384]{2,1,0:T(8,128)(2,1)}, bf16[2,512,384]{2,1,0:T(8,128)(2,1)}, f32[3,2,768]{2,1,0:T(2,128)}, f32[1920,384]{1,0:T(8,128)}, /*index=5*/f32[1920,384]{1,0:T(8,128)}) custom-call(s32[30]{0:T(128)} %dynamic-slice_bitcast_fusion.info_ref, s32[2,8]{1,0:T(2,128)} %len_ref.9, ...), custom_call_target="tpu_custom_call" | custom-call | flops 99999997952 | bytes 1 | tf_op jit(solution)/shard_map/attn_bwd/pallas_call | solution.py:544
  118.9 4.2 %add_shares.27.refs_8_ = f32[2304,256]{1,0:T(8,128)} custom-call(s32[30]{0:T(128)} %dynamic-slice_bitcast_fusion.info_ref, f32[4608,256]{1,0:T(8,128)} %get-tuple-element.90.refs_3_.refs_0_.refs_4_, f32[2304,256]{1,0:T(8,128)} %collective-permute-done.4.refs_1_, f32[1920,384]{1,0:T(8,128)} %get-tuple-element.95.refs_2_.refs_0_.refs_4_), custom_call_target="tpu_custom_call" | custom-call | flops 1 | bytes 1 | tf_op jit(solution)/shard_map/add_shares/pallas_call | solution.py:683
  123.6 4.1 %add_shares.28 = (f32[576,256]{1,0:T(8,128)}, f32[576,256]{1,0:T(8,128)}) custom-call(s32[30]{0:T(128)} %dynamic-slice_bitcast_fusion.info_ref, f32[4608,256]{1,0:T(8,128)} %get-tuple-element.78.refs_0_.refs_2_.refs_4_, f32[2304,256]{1,0:T(8,128)} %collective-permute-done.1.refs_1_.refs_5_, f32[2304,256]{1,0:T(8,128)} %collective-permute-done.2.refs_2_.refs_6_, ...), custom_call_target="tpu_custom_call" | custom-call | flops 1 | bytes 1 | tf_op jit(solution)/shard_map/add_shares/pallas_call | solution.py:683
  129.3 20.4 %attn_bwd.3 = (bf16[2,512,384]{2,1,0:T(8,128)(2,1)}, bf16[2,512,384]{2,1,0:T(8,128)(2,1)}, bf16[2,512,384]{2,1,0:T(8,128)(2,1)}, f32[3,2,768]{2,1,0:T(2,128)}, f32[1152,384]{1,0:T(8,128)}, /*index=5*/f32[1152,384]{1,0:T(8,128)}) custom-call(s32[30]{0:T(128)} %dynamic-slice_bitcast_fusion.info_ref, s32[2,8]{1,0:T(2,128)} %len_ref.9, ...), custom_call_target="tpu_custom_call" | custom-call | flops 99999997952 | bytes 1 | tf_op jit(solution)/shard_map/attn_bwd/pallas_call | solution.py:544
  158.0 3.8 %add_shares.30.refs_2_ = f32[1152,256]{1,0:T(8,128)} custom-call(s32[30]{0:T(128)} %dynamic-slice_bitcast_fusion.info_ref, f32[4608,256]{1,0:T(8,128)} %get-tuple-element.90.refs_3_.refs_0_.refs_4_, f32[2304,256]{1,0:T(8,128)} %collective-permute-done.8.refs_1_.refs_5_, f32[2304,256]{1,0:T(8,128)} %collective-permute-done.9.refs_2_.refs_6_, ...), custom_call_target="tpu_custom_call" | custom-call | flops 1 | bytes 1 | tf_op jit(solution)/shard_map/add_shares/pallas_call | solution.py:683
  166.1 4.3 %collective-permute-done.6.refs_1_ = f32[288,256]{1,0:T(8,128)S(1)} collective-permute-done((f32[288,256]{1,0:T(8,128)}, f32[288,256]{1,0:T(8,128)S(1)}, u32[]{:S(2)}, u32[]{:S(2)}) %collective-permute-start.6) | collective-permute-done | bytes 294944 | tf_op jit(solution)/shard_map/ppermute | solution.py:655
  178.3 4.2 %add_shares.34 = (f32[576,256]{1,0:T(8,128)}, f32[576,256]{1,0:T(8,128)}) custom-call(s32[30]{0:T(128)} %dynamic-slice_bitcast_fusion.info_ref, f32[4608,256]{1,0:T(8,128)} %get-tuple-element.90.refs_3_.refs_0_.refs_4_, f32[2304,256]{1,0:T(8,128)} %collective-permute-done.8.refs_1_.refs_5_, f32[2304,256]{1,0:T(8,128)} %collective-permute-done.9.refs_2_.refs_6_, ...), custom_call_target="tpu_custom_call" | custom-call | flops 1 | bytes 1 | tf_op jit(solution)/shard_map/add_shares/pallas_call | solution.py:683
  190.8 9.7 %tokgrad.1 = (bf16[1024,768]{1,0:T(8,128)(2,1)}, f32[1,768]{1,0:T(1,128)}) custom-call(bf16[1024,768]{1,0:T(8,128)(2,1)} %bitcast.27, f32[1024,768]{1,0:T(8,128)} %get-tuple-element.81.dres_ref, bf16[768]{0:T(1024)(128)(2,1)} %gain_ref.1, bf16[768,768]{1,0:T(8,128)(2,1)} %wq_ref.3, bf16[768,768]{1,0:T(8,128)(2,1)} %wk_ref.3, bf16[768,768]{1,0:T(8,128)(2,1)} %wv_ref.3, ...), custom_call_target="tpu_custom_call" | custom-call | flops 99999997952 | bytes 1 | tf_op jit(solution)/shard_map/tokgrad/pallas_call | solution.py:601
  251.1 4.5 %collective-permute-done.23.refs_1_ = f32[288,256]{1,0:T(8,128)S(1)} collective-permute-done((f32[288,256]{1,0:T(8,128)S(1)}, f32[288,256]{1,0:T(8,128)S(1)}, u32[]{:S(2)}, u32[]{:S(2)}) %collective-permute-start.23) | collective-permute-done | bytes 294944 | tf_op jit(solution)/shard_map/ppermute | solution.py:655
  274.0 4.8 %collective-permute-done.28.refs_1_ = f32[576,256]{1,0:T(8,128)} collective-permute-done((f32[576,256]{1,0:T(8,128)S(1)}, f32[576,256]{1,0:T(8,128)}, u32[]{:S(2)}, u32[]{:S(2)}) %collective-permute-start.28) | collective-permute-done | bytes 589856 | tf_op jit(solution)/shard_map/ppermute | solution.py:655
  291.2 10.5 %collective-permute-done.40.refs_1_ = f32[1152,256]{1,0:T(8,128)S(1)} collective-permute-done((f32[1152,256]{1,0:T(8,128)S(1)}, f32[1152,256]{1,0:T(8,128)S(1)}, u32[]{:S(2)}, u32[]{:S(2)}) %collective-permute-start.40) | collective-permute-done | bytes 1179680 | tf_op jit(solution)/shard_map/ppermute | solution.py:655
  306.3 9.2 %assemble.4 = (f32[768,3072]{1,0:T(8,128)}, f32[3072,768]{1,0:T(8,128)}) custom-call(s32[30]{0:T(128)} %dynamic-slice_bitcast_fusion.info_ref, f32[2304,256]{1,0:T(8,128)} %join.14.refs_0_, f32[2304,256]{1,0:T(8,128)} %collective-permute-done.38.refs_2_.refs_1_, f32[2304,256]{1,0:T(8,128)} %copy-done.7, f32[2304,256]{1,0:T(8,128)} %collective-permute-done.39.refs_3_, ...), custom_call_target="tpu_custom_call" | custom-call | flops 99999997952 | bytes 1 | tf_op jit(solution)/shard_map/assemble/pallas_call | solution.py:876
  316.0 3.7 copy-done.3
  322.6 8.7 %collective-permute-done.42.refs_1_ = f32[240,384]{1,0:T(8,128)S(1)} collective-permute-done((f32[240,384]{1,0:T(8,128)S(1)}, f32[240,384]{1,0:T(8,128)S(1)}, u32[]{:S(2)}, u32[]{:S(2)}) %collective-permute-start.42) | collective-permute-done | bytes 368672 | tf_op jit(solution)/shard_map/ppermute | solution.py:655
  336.0 7.6 %collective-permute-done.43.refs_1_ = f32[480,384]{1,0:T(8,128)S(1)} collective-permute-done((f32[480,384]{1,0:T(8,128)S(1)}, f32[480,384]{1,0:T(8,128)S(1)}, u32[]{:S(2)}, u32[]{:S(2)}) %collective-permute-start.43) | collective-permute-done | bytes 737312 | tf_op jit(solution)/shard_map/ppermute | solution.py:655
  348.2 4.9 %assemble.5 = (f32[768,768]{1,0:T(8,128)}, f32[768,768]{1,0:T(8,128)}, f32[768,768]{1,0:T(8,128)}) custom-call(s32[30]{0:T(128)} %dynamic-slice_bitcast_fusion.info_ref, f32[576,384]{1,0:T(8,128)} %join.19.refs_0_, f32[576,384]{1,0:T(8,128)} %collective-permute-done.47.refs_1_, f32[576,384]{1,0:T(8,128)} %collective-permute-done.34.refs_3_.refs_2_, ...), custom_call_target="tpu_custom_call" | custom-call | flops 99999997952 | bytes 1 | tf_op jit(solution)/shard_map/assemble/pallas_call | solution.py:876
  353.2 9.2 %assemble.7 = (f32[768,3072]{1,0:T(8,128)}, f32[3072,768]{1,0:T(8,128)}) custom-call(s32[30]{0:T(128)} %dynamic-slice_bitcast_fusion.info_ref, f32[2304,256]{1,0:T(8,128)} %join.20.refs_4_.refs_0_, f32[2304,256]{1,0:T(8,128)} %collective-permute-done.49.refs_1_.refs_6_, ...), custom_call_target="tpu_custom_call", output_to_operand_aliasing={{0}: (5, {}), {1}: (6, {})} | custom-call | flops 99999997952 | bytes 1 | tf_op jit(solution)/shard_map/assemble/pallas_call | solution.py:876
  369.3 6.5 %assemble.6 = (f32[768,768]{1,0:T(8,128)}, f32[768,768]{1,0:T(8,128)}, f32[768,768]{1,0:T(8,128)}, f32[768,768]{1,0:T(8,128)}) custom-call(s32[30]{0:T(128)} %dynamic-slice_bitcast_fusion.info_ref, f32[960,384]{1,0:T(8,128)} %join.23.refs_4_.refs_0_, ...), custom_call_target="tpu_custom_call", output_to_operand_aliasing={{0}: (5, {}), {1}: (6, {}), {2}: (7, {})} | custom-call | flops 99999997952 | bytes 1 | tf_op jit(solution)/shard_map/assemble/pallas_call | solution.py:876
  (217 shorter events, 145.9 us)
Async XLA Ops:
  50.4 41.5 %collective-permute-start.1 = (f32[2304,256]{1,0:T(8,128)}, f32[2304,256]{1,0:T(8,128)}, u32[]{:S(2)}, u32[]{:S(2)}) collective-permute-start(f32[2304,256]{1,0:T(8,128)} %get-tuple-element.89), channel_id=1, source_target_pairs={{0,1},{1,0},{2,3},{3,2},{4,5},{5,4},{6,7},{7,6},{8,9},{9,8},{10,11... | collective-permute-start | bytes 7077896 | tf_op jit(solution)/shard_map/ppermute | solution.py:659
  59.0 32.9 %collective-permute-start.2 = (f32[2304,256]{1,0:T(8,128)}, f32[2304,256]{1,0:T(8,128)}, u32[]{:S(2)}, u32[]{:S(2)}) collective-permute-start(f32[2304,256]{1,0:T(8,128)} %add_shares.25.refs_6_), channel_id=1, source_target_pairs={{0,2},{1,5},{2,0},{3,7},{4,6},{5,1},{6,4},{7,3},{8,10},{9,13},{10,... | collective-permute-start | bytes 7077896 | tf_op jit(solution)/shard_map/ppermute | solution.py:655
  90.0 28.9 %collective-permute-start.4 = (f32[2304,256]{1,0:T(8,128)}, f32[2304,256]{1,0:T(8,128)}, u32[]{:S(2)}, u32[]{:S(2)}) collective-permute-start(f32[2304,256]{1,0:T(8,128)} %get-tuple-element.94), channel_id=1, source_target_pairs={{0,1},{1,0},{2,3},{3,2},{4,5},{5,4},{6,7},{7,6},{8,9},{9,8},{10,11... | collective-permute-start | bytes 7077896 | tf_op jit(solution)/shard_map/ppermute | solution.py:659
  90.1 67.9 %collective-permute-start.8 = (f32[2304,256]{1,0:T(8,128)}, f32[2304,256]{1,0:T(8,128)}, u32[]{:S(2)}, u32[]{:S(2)}) collective-permute-start(f32[2304,256]{1,0:T(8,128)} %get-tuple-element.105), channel_id=1, source_target_pairs={{0,1},{1,0},{2,3},{3,2},{4,5},{5,4},{6,7},{7,6},{8,9},{9,8},{10,11... | collective-permute-start | bytes 7077896 | tf_op jit(solution)/shard_map/ppermute | solution.py:659
  95.7 27.8 %collective-permute-start.3 = (f32[1152,256]{1,0:T(8,128)}, f32[1152,256]{1,0:T(8,128)}, u32[]{:S(2)}, u32[]{:S(2)}) collective-permute-start(f32[1152,256]{1,0:T(8,128)} %add_shares.26.refs_1_), channel_id=1, source_target_pairs={{0,4},{1,3},{2,6},{3,1},{4,0},{5,7},{6,2},{7,5},{8,12},{9,11},{10,... | collective-permute-start | bytes 3538952 | tf_op jit(solution)/shard_map/ppermute | solution.py:655
  123.0 34.9 %collective-permute-start.9 = (f32[2304,256]{1,0:T(8,128)}, f32[2304,256]{1,0:T(8,128)}, u32[]{:S(2)}, u32[]{:S(2)}) collective-permute-start(f32[2304,256]{1,0:T(8,128)} %add_shares.27.refs_8_), channel_id=1, source_target_pairs={{0,2},{1,5},{2,0},{3,7},{4,6},{5,1},{6,4},{7,3},{8,10},{9,13},{10,... | collective-permute-start | bytes 7077896 | tf_op jit(solution)/shard_map/ppermute | solution.py:655
  123.6 39.1 %collective-permute-start.7 = (f32[1920,384]{1,0:T(8,128)}, f32[1920,384]{1,0:T(8,128)}, u32[]{:S(2)}, u32[]{:S(2)}) collective-permute-start(f32[1920,384]{1,0:T(8,128)} %get-tuple-element.104), channel_id=1, source_target_pairs={{0,1},{1,0},{2,3},{3,2},{4,5},{5,4},{6,7},{7,6},{8,9},{9,8},{10,11... | collective-permute-start | bytes 8847368 | tf_op jit(solution)/shard_map/ppermute | solution.py:659
  127.7 22.2 %collective-permute-start.5 = (f32[576,256]{1,0:T(8,128)}, f32[576,256]{1,0:T(8,128)}, u32[]{:S(2)}, u32[]{:S(2)}) collective-permute-start(f32[576,256]{1,0:T(8,128)} %get-tuple-element.96.refs_0_), channel_id=1, source_target_pairs={{0,8},{1,9},{2,10},{3,11},{4,12},{5,13},{6,14},{7,15},{8,0},{9,1},... | collective-permute-start | bytes 1769480 | tf_op jit(solution)/shard_map/ppermute | solution.py:655
  149.7 22.6 %collective-permute-start.12 = (f32[1152,384]{1,0:T(8,128)}, f32[1152,384]{1,0:T(8,128)}, u32[]{:S(2)}, u32[]{:S(2)}) collective-permute-start(f32[1152,384]{1,0:T(8,128)} %get-tuple-element.106), channel_id=1, source_target_pairs={{0,1},{1,0},{2,3},{3,2},{4,5},{5,4},{6,7},{7,6},{8,9},{9,8},{10,11... | collective-permute-start | bytes 5308424 | tf_op jit(solution)/shard_map/ppermute | solution.py:659
  175.9 26.8 %collective-permute-start.16 = (f32[576,384]{1,0:T(8,128)}, f32[576,384]{1,0:T(8,128)}, u32[]{:S(2)}, u32[]{:S(2)}) collective-permute-start(f32[576,384]{1,0:T(8,128)} %add_shares.33.refs_0_), channel_id=1, source_target_pairs={{0,2},{1,5},{2,0},{3,7},{4,6},{5,1},{6,4},{7,3},{8,10},{9,13},{10,... | collective-permute-start | bytes 2654216 | tf_op jit(solution)/shard_map/ppermute | solution.py:655
  177.4 47.4 %collective-permute-start.21 = (f32[960,384]{1,0:T(8,128)}, f32[960,384]{1,0:T(8,128)}, u32[]{:S(2)}, u32[]{:S(2)}) collective-permute-start(f32[960,384]{1,0:T(8,128)} %add_shares.31.refs_2_), channel_id=1, source_target_pairs={{0,2},{1,5},{2,0},{3,7},{4,6},{5,1},{6,4},{7,3},{8,10},{9,13},{10,... | collective-permute-start | bytes 4423688 | tf_op jit(solution)/shard_map/ppermute | solution.py:655
  182.5 23.6 %collective-permute-start.15 = (f32[576,256]{1,0:T(8,128)}, f32[576,256]{1,0:T(8,128)}, u32[]{:S(2)}, u32[]{:S(2)}) collective-permute-start(f32[576,256]{1,0:T(8,128)} %get-tuple-element.107.refs_2_), channel_id=1, source_target_pairs={{0,8},{1,9},{2,10},{3,11},{4,12},{5,13},{6,14},{7,15},{8,0},{9,1},... | collective-permute-start | bytes 1769480 | tf_op jit(solution)/shard_map/ppermute | solution.py:655
  190.7 23.9 %collective-permute-start.14 = (f32[576,256]{1,0:T(8,128)}, f32[576,256]{1,0:T(8,128)}, u32[]{:S(2)}, u32[]{:S(2)}) collective-permute-start(f32[576,256]{1,0:T(8,128)} %join.12.refs_6_.refs_0_), channel_id=1, source_target_pairs={{0,8},{1,9},{2,10},{3,11},{4,12},{5,13},{6,14},{7,15},{8,0},{9,1},... | collective-permute-start | bytes 1769480 | tf_op jit(solution)/shard_map/ppermute | solution.py:655
  209.5 24.3 %collective-permute-start.18 = (f32[288,256]{1,0:T(8,128)}, f32[288,256]{1,0:T(8,128)}, u32[]{:S(2)}, u32[]{:S(2)}) collective-permute-start(f32[288,256]{1,0:T(8,128)} %get-tuple-element.114.refs_2_), channel_id=1, source_target_pairs={{0,16},{1,17},{2,18},{3,19},{4,20},{5,21},{6,22},{7,23},{8,24},{9,... | collective-permute-start | bytes 884744 | tf_op jit(solution)/shard_map/ppermute | solution.py:655
  218.0 21.0 %collective-permute-start.25 = (f32[1152,256]{1,0:T(8,128)}, f32[1152,256]{1,0:T(8,128)}, u32[]{:S(2)}, u32[]{:S(2)}) collective-permute-start(f32[1152,256]{1,0:T(8,128)} %copy-done.4), channel_id=1, source_target_pairs={{0,4},{1,3},{2,6},{3,1},{4,0},{5,7},{6,2},{7,5},{8,12},{9,11},{10,... | collective-permute-start | bytes 3538952 | tf_op jit(solution)/shard_map/ppermute | solution.py:655
  228.7 31.8 %collective-permute-start.31 = (f32[480,384]{1,0:T(8,128)}, f32[480,384]{1,0:T(8,128)}, u32[]{:S(2)}, u32[]{:S(2)}) collective-permute-start(f32[480,384]{1,0:T(8,128)} %add_shares.39.refs_0_), channel_id=1, source_target_pairs={{0,4},{1,3},{2,6},{3,1},{4,0},{5,7},{6,2},{7,5},{8,12},{9,11},{10,... | collective-permute-start | bytes 2211848 | tf_op jit(solution)/shard_map/ppermute | solution.py:655
  235.4 20.3 %collective-permute-start.23 = (f32[288,256]{1,0:T(8,128)S(1)}, f32[288,256]{1,0:T(8,128)S(1)}, u32[]{:S(2)}, u32[]{:S(2)}) collective-permute-start(f32[288,256]{1,0:T(8,128)S(1)} %add_shares.41.refs_2_.refs_0_), channel_id=1, source_target_pairs={{0,16},{1,17},{2,18},{3,19},{4,20},{5,21},{6,22},{7,23},{8,24},{9,... | collective-permute-start | bytes 884744 | tf_op jit(solution)/shard_map/ppermute | solution.py:655
  242.5 31.5 %collective-permute-start.38 = (f32[2304,256]{1,0:T(8,128)}, f32[2304,256]{1,0:T(8,128)}, u32[]{:S(2)}, u32[]{:S(2)}) collective-permute-start(f32[2304,256]{1,0:T(8,128)} %join.14.refs_0_), channel_id=1, source_target_pairs={{0,2},{1,5},{2,0},{3,7},{4,6},{5,1},{6,4},{7,3},{8,10},{9,13},{10,... | collective-permute-start | bytes 7077896 | tf_op jit(solution)/shard_map/ppermute | solution.py:655
  258.4 20.4 %collective-permute-start.28 = (f32[576,256]{1,0:T(8,128)S(1)}, f32[576,256]{1,0:T(8,128)}, u32[]{:S(2)}, u32[]{:S(2)}) collective-permute-start(f32[576,256]{1,0:T(8,128)S(1)} %join.15.refs_2_.refs_0_), channel_id=1, source_target_pairs={{0,8},{1,9},{2,10},{3,11},{4,12},{5,13},{6,14},{7,15},{8,0},{9,1},... | collective-permute-start | bytes 1769480 | tf_op jit(solution)/shard_map/ppermute | solution.py:655
  274.0 32.3 %collective-permute-start.39 = (f32[2304,256]{1,0:T(8,128)}, f32[2304,256]{1,0:T(8,128)}, u32[]{:S(2)}, u32[]{:S(2)}) collective-permute-start(f32[2304,256]{1,0:T(8,128)} %collective-permute-done.38.refs_2_.refs_1_), channel_id=1, source_target_pairs={{0,1},{1,0},{2,3},{3,2},{4,5},{5,4},{6,7},{7,6},{8,9},{9,8},{10,11... | collective-permute-start | bytes 7077896 | tf_op jit(solution)/shard_map/ppermute | solution.py:659
  280.8 20.9 %collective-permute-start.40 = (f32[1152,256]{1,0:T(8,128)S(1)}, f32[1152,256]{1,0:T(8,128)S(1)}, u32[]{:S(2)}, u32[]{:S(2)}) collective-permute-start(f32[1152,256]{1,0:T(8,128)S(1)} %join.18.refs_2_.refs_0_), channel_id=1, source_target_pairs={{0,4},{1,3},{2,6},{3,1},{4,0},{5,7},{6,2},{7,5},{8,12},{9,11},{10,... | collective-permute-start | bytes 3538952 | tf_op jit(solution)/shard_map/ppermute | solution.py:655
  289.4 33.2 %collective-permute-start.47 = (f32[576,384]{1,0:T(8,128)}, f32[576,384]{1,0:T(8,128)}, u32[]{:S(2)}, u32[]{:S(2)}) collective-permute-start(f32[576,384]{1,0:T(8,128)} %join.19.refs_0_), channel_id=1, source_target_pairs={{0,2},{1,5},{2,0},{3,7},{4,6},{5,1},{6,4},{7,3},{8,10},{9,13},{10,... | collective-permute-start | bytes 2654216 | tf_op jit(solution)/shard_map/ppermute | solution.py:655
  304.2 31.8 %collective-permute-start.49 = (f32[2304,256]{1,0:T(8,128)}, f32[2304,256]{1,0:T(8,128)}, u32[]{:S(2)}, u32[]{:S(2)}) collective-permute-start(f32[2304,256]{1,0:T(8,128)} %join.20.refs_4_.refs_0_), channel_id=1, source_target_pairs={{0,2},{1,5},{2,0},{3,7},{4,6},{5,1},{6,4},{7,3},{8,10},{9,13},{10,... | collective-permute-start | bytes 7077896 | tf_op jit(solution)/shard_map/ppermute | solution.py:655
  322.6 24.7 %collective-permute-start.48 = (f32[576,384]{1,0:T(8,128)}, f32[576,384]{1,0:T(8,128)S(1)}, u32[]{:S(2)}, u32[]{:S(2)}) collective-permute-start(f32[576,384]{1,0:T(8,128)} %collective-permute-done.47.refs_1_), channel_id=1, source_target_pairs={{0,1},{1,0},{2,3},{3,2},{4,5},{5,4},{6,7},{7,6},{8,9},{9,8},{10,11... | collective-permute-start | bytes 2654216 | tf_op jit(solution)/shard_map/ppermute | solution.py:659
  (61 other events, 532.7 us)

commit v6 on v5

--- a/solution.py
+++ b/solution.py
@@ -432,10 +432,10 @@
     return jnp.sum(total, axis=0, keepdims=True)
 
 
-def attn_bwd_kernel(slabs, first, n_more, info_ref, len_ref, q_ref, k_ref, v_ref, do_ref, lse_ref, band_ref, h1T_ref, *refs):
+def attn_bwd_kernel(slabs, first, n_more, info_ref, len_ref, q_ref, k_ref, v_ref, do_ref, attT_ref, lse_ref, band_ref, h1T_ref, *refs):
     more = refs[:n_more]
-    dq_ref, dk_ref, dv_ref, diag_ref, keep_ref, send_ref = refs[-14:-8]
-    mask_ref, p_ref, low_ref, dp_ref, ds_ref, d_ref, g_ref, sems = refs[-8:]
+    dq_ref, dk_ref, dv_ref, diag_ref, keep_ref, send_ref = refs[-12:-6]
+    mask_ref, low_ref, ds_ref, d_ref, g_ref, sems = refs[-6:]
     pair, pairs = pl.program_id(0), pl.num_programs(0)
     rows, seq = q_ref.shape[:2]
     head = TILE // 2
@@ -460,37 +460,31 @@
     for a in range(2):
         vector = band_ref[pl.ds(2 * (first + pair) + a, 1), :]
         bands.append((vector, band_of(vector)))
-    sides = []
+    sides, sums = [], [{}, {}]
     for n in range(2 * rows):
         row, a = n // 2, n % 2
         qp, kp, vp, dop = q_ref[row], k_ref[row], v_ref[row], do_ref[row]
+        dopT = dop.T
         own = low_half if a == 0 else ~low_half
         qm = jnp.where(own, qp, jnp.zeros_like(qp))
         dom = jnp.where(own, dop, jnp.zeros_like(dop))
         vector, band = bands[a]
         lse = lse_ref[row, pl.ds(2 * (first + pair) + a, 1), :]
-        delta = jnp.zeros((1, seq), F32)
+        part = slice(a * head, (a + 1) * head)
+        delta = jnp.sum(attT_ref[row, part, :].astype(F32) * dopT[part].astype(F32), axis=0, keepdims=True)
+        near = sums[a]
         for ki in range(count):
             some = slice(ki * TILE, (ki + 1) * TILE)
             s = dot(kp[some], qm, NT) + bias_row(band, vector, ki, count) + mask_ref[row, some, :]
             prob = jnp.exp(s - lse)
-            dp = dot(vp[some], dom, NT)
-            delta = delta + jnp.sum(prob * dp, axis=0, keepdims=True)
-            p_ref[n, some, :] = prob
+            ds = prob * (dot(vp[some], dom, NT) - delta)
             low_ref[n, some, :] = prob.astype(BF16)
-            dp_ref[n, some, :] = dp
-        sides.append((qm, dom, delta))
-    sums = [{}, {}]
-    for n, (_, _, delta) in enumerate(sides):
-        near = sums[n % 2]
-        for ki in range(count):
-            some = slice(ki * TILE, (ki + 1) * TILE)
-            ds = p_ref[n, some, :] * (dp_ref[n, some, :] - delta)
             ds_ref[n, some, :] = ds.astype(BF16)
             for qi in range(count):
                 step = max(-2, min(2, ki - qi))
                 tile = ds[:, qi * TILE : (qi + 1) * TILE]
                 near[step] = tile if step not in near else near[step] + tile
+        sides.append((qm, dom))
     for a, near in enumerate(sums):
         zero = jnp.zeros((TILE, TILE), F32)
         band = jnp.concatenate([near[0], near[-1], zero, near[1]], axis=1)
@@ -503,7 +497,7 @@
         dqT, dk, dv = [], None, None
         for a in range(2):
             n = 2 * row + a
-            qm, dom, _ = sides[n]
+            qm, dom = sides[n]
             dva = dot(low_ref[n], dom)
             dka = dot(ds_ref[n], qm)
             dv = dva if dv is None else dv + dva
@@ -532,7 +526,7 @@
         run_all(moves, "wait")
 
 
-def attn_bwd(info, lengths, slabs, q, k, v, do, lse, band, h1T, first, pairs, more, after):
+def attn_bwd(info, lengths, slabs, q, k, v, do, attT, lse, band, h1T, first, pairs, more, after):
     rows, seq, width = q.shape
     cols = pairs * TILE
     half = width // 2 * (3 + sum(m.shape[1] // cols for m in more))
@@ -547,15 +541,13 @@
             num_scalar_prefetch=2,
             grid=(pairs,),
             in_specs=[tall] * 4
-            + [full(lse), full(band), full(h1T)]
+            + [pl.BlockSpec((rows, TILE, seq), lambda p, *_: (0, first + p, 0)), full(lse), full(band), full(h1T)]
             + [full(m) for m in more]
             + unused(after),
             out_specs=[tall_out] * 3 + [pl.BlockSpec((1, 2, 6 * TILE), lambda p, *_: (p, 0, 0))] + [ANYWHERE] * 2,
             scratch_shapes=[
                 pltpu.VMEM((rows, seq, seq), F32),
-                square(F32),
                 square(BF16),
-                square(F32),
                 square(BF16),
                 pltpu.VMEM((3, rows, seq, cols), BF16),
                 pltpu.VMEM((2, half, cols), F32),
@@ -568,7 +560,7 @@
         cost_estimate=COST,
         compiler_params=params(),
         name="attn_bwd",
-    )(info, lengths, q, k, v, do, lse, band, h1T, *more, *after)
+    )(info, lengths, q, k, v, do, attT, lse, band, h1T, *more, *after)
 
 
 def tokgrad_kernel(halves, tok_ref, dres_ref, gain_ref, wq_ref, wk_ref, wv_ref, *refs):
@@ -907,7 +899,7 @@
             outs[out][s * rows : (s + 1) * rows, column : column + source.shape[1]] = source[at : at + rows, :]
 
 
-ORDER = ("F0", "s0", "F1", "s0", "B0", "s1", "s0", "B1", "s0", "s1", "s2", "s0", "D", "s3", "D", "s1", "s0", "T", "s3", "s1", "s0", "D", "m", "s3", "s2", "D", "s3", "s1", "m", "s0", "D", "s3", "s1", "m", "s3", "s2", "s3", "s1", "m", "s3", "D", "m", "s2", "s2", "s3", "s0", "s1", "s0", "s2", "s2", "s2", "s3", "s1", "s1", "s2", "D", "s2")
+ORDER = ("F0", "s0", "F1", "s0", "B0", "s1", "s0", "B1", "s0", "s1", "s2", "s0", "D", "s3", "D", "s1", "s0", "T", "s1", "s3", "s0", "D", "m", "s3", "s2", "D", "s3", "s1", "m", "s0", "D", "s3", "s2", "s1", "m", "s3", "s3", "s1", "m", "s3", "D", "m", "s2", "s2", "s3", "s0", "s1", "s0", "s2", "s2", "s2", "s3", "s1", "s1", "s2", "D", "s2")
 
 
 def on_device(tokens, lengths, attn_gain, wq, wk, wv, wo, table, ffn_gain, w_in, w_out, out_grad, *, size):
@@ -972,7 +964,7 @@
             half = pairs // 2
             more = [] if which else [gwo]
             dq, dk, dv, diag, keep, send = attn_bwd(
-                info, lengths, slabs, q, k, v, tall(datt), lse, band, h1T, which * half, half, more, after
+                info, lengths, slabs, q, k, v, tall(datt), attT, lse, band, h1T, which * half, half, more, after
             )
             ds += [flat(dq), flat(dk), flat(dv)]
             diags.append(diag)

time: 384 us -> 391 us (1.018)
  local copies, waits for them, and re-layouts: 17.6 us -> 23.1 us
    unnamed x70 -> x82, local copies, waits for them, and re-layouts: 14.3 us -> 19.8 us
  transfers between devices with their start and end apart: 51 -> 51, of which waited for: 19 -> 15; matrix products, arithmetic and copies ran while one was open for 1% -> 1% of each run, Pallas kernels for 49% -> 48%
where the time goes in v6:
time: 391 us; the launch traced here: 383 us
  Pallas kernels  236 us (60%)
  waiting for transfers between devices  72 us (18%)
  starting transfers between devices  46.5 us (12%)
  local copies, waits for them, and re-layouts  23.1 us (6%)
    ppermute x36, waiting for transfers between devices, exchange(): return lax.ppermute(x, ('rows', 'blk'), moves)  62.7 us
    pallas_call x25, Pallas kernels, add_shares(): pl.pallas_call(functools.partial(add_kernel, len(sources), outs), grid_sp...  57.1 us
    pallas_call x2, Pallas kernels, ffn_chunk(): pl.pallas_call(functools.partial(ffn_kernel, steps, slabs, not acc, bool(...  51.5 us
    ppermute x36, starting transfers between devices, exchange(): return lax.ppermute(x, ('rows', 'blk'), moves)  44.2 us
    pallas_call x2, Pallas kernels, attn_bwd(): pl.pallas_call(functools.partial(attn_bwd_kernel, slabs, first, len(more)...  40.8 us
    pallas_call x4, Pallas kernels, assemble(): pl.pallas_call(functools.partial(assemble_kernel, spread, len(outs)), gri...  29.8 us
    pallas_call x1, Pallas kernels, attn_fwd(): pl.pallas_call(attn_fwd_kernel, grid_spec=pltpu.PrefetchScalarGridSpec(nu...  23.1 us
    pallas_call x12, Pallas kernels, join(): pl.pallas_call(functools.partial(join_kernel, column, ways), in_specs=[pl...  20 us
  transfers between devices with their start and end apart: 51, of which 15 were waited for; matrix products, arithmetic and copies ran while one was open for 1% of the time, Pallas kernels for 48%

profile of v6, /device:TPU:0, one launch (start us, length us, event | category | flops | bytes accessed | tf_op | source)
XLA Modules:
  0.0 383.4 jit_solution(6282661108439411101)
XLA Ops:
  3.4 23.1 %attn_fwd.1 = (bf16[2,768,512]{2,1,0:T(8,128)(2,1)}, bf16[2,512,768]{2,1,0:T(8,128)(2,1)}, bf16[2,512,768]{2,1,0:T(8,128)(2,1)}, bf16[2,512,768]{2,1,0:T(8,128)(...) custom-call(s32[2,8]{1,0:T(2,128)} %len_ref.9, ...), custom_call_target="tpu_custom_call" | custom-call | flops 99999997952 | bytes 1 | tf_op jit(solution)/shard_map/attn_fwd/pallas_call | solution.py:174
  26.5 23.3 %ffn.2 = (f32[4608,256]{1,0:T(8,128)}, f32[2304,256]{1,0:T(8,128)}, f32[2304,256]{1,0:T(8,128)}, f32[1024,768]{1,0:T(8,128)}, f32[1024,768]{1,0:T(8,128)}) custom-call(s32[30]{0:T(128)} %dynamic-slice_bitcast_fusion.info_ref, s32[2,8]{1,0:T(2,128)} %len_ref.9, bf16[1024,768]{1,0:T(8,128)(2,1)} %bitcast.33, bf16[1024,768]{1,0:T(8,128)(2,1)} %bitcast.25, ...), custom_call_target="tpu_custom_call" | custom-call | flops 99999997952 | bytes 1 | tf_op jit(solution)/shard_map/ffn/pallas_call | solution.py:399
  50.5 4.4 %collective-permute-done.refs_1_ = f32[2304,256]{1,0:T(8,128)} collective-permute-done((f32[2304,256]{1,0:T(8,128)}, f32[2304,256]{1,0:T(8,128)}, u32[]{:S(2)}, u32[]{:S(2)}) %collective-permute-start) | collective-permute-done | bytes 2359328 | tf_op jit(solution)/shard_map/ppermute | solution.py:651
  54.9 4.1 %add_shares.25.refs_6_ = f32[2304,256]{1,0:T(8,128)} custom-call(s32[30]{0:T(128)} %dynamic-slice_bitcast_fusion.info_ref, f32[4608,256]{1,0:T(8,128)} %get-tuple-element.78.refs_0_.refs_2_.refs_4_, f32[2304,256]{1,0:T(8,128)} %collective-permute-done.refs_1_, f32[4608,256]{1,0:T(8,128)} %get-tuple-element.78.refs_0_.refs_2_.refs_4_), custom_call_target="tpu_custom_call" | custom-call | flops 1 | bytes 1 | tf_op jit(solution)/shard_map/add_shares/pallas_call | solution.py:675
  61.9 28.2 %ffn.3 = (f32[4608,256]{1,0:T(8,128)}, f32[2304,256]{1,0:T(8,128)}, f32[2304,256]{1,0:T(8,128)}, bf16[1024,768]{1,0:T(8,128)(2,1)}, f32[1024,768]{1,0:T(8,128)},...) custom-call(s32[30]{0:T(128)} %dynamic-slice_bitcast_fusion.info_ref, s32[2,8]{1,0:T(2,128)} %len_ref.9, ...), custom_call_target="tpu_custom_call" | custom-call | flops 99999997952 | bytes 1 | tf_op jit(solution)/shard_map/ffn/pallas_call | solution.py:399
  91.9 3.8 add_shares.26.refs_1_
  97.3 21.0 %attn_bwd.2 = (bf16[2,512,384]{2,1,0:T(8,128)(2,1)}, bf16[2,512,384]{2,1,0:T(8,128)(2,1)}, bf16[2,512,384]{2,1,0:T(8,128)(2,1)}, f32[3,2,768]{2,1,0:T(2,128)}, f32[1920,384]{1,0:T(8,128)}, /*index=5*/f32[1920,384]{1,0:T(8,128)}) custom-call(s32[30]{0:T(128)} %dynamic-slice_bitcast_fusion.info_ref, s32[2,8]{1,0:T(2,128)} %len_ref.9, ...), custom_call_target="tpu_custom_call" | custom-call | flops 99999997952 | bytes 1 | tf_op jit(solution)/shard_map/attn_bwd/pallas_call | solution.py:538
  118.3 4.2 %add_shares.27.refs_8_ = f32[2304,256]{1,0:T(8,128)} custom-call(s32[30]{0:T(128)} %dynamic-slice_bitcast_fusion.info_ref, f32[4608,256]{1,0:T(8,128)} %get-tuple-element.90.refs_3_.refs_0_.refs_4_, f32[2304,256]{1,0:T(8,128)} %collective-permute-done.4.refs_1_, f32[1920,384]{1,0:T(8,128)} %get-tuple-element.95.refs_2_.refs_0_.refs_4_), custom_call_target="tpu_custom_call" | custom-call | flops 1 | bytes 1 | tf_op jit(solution)/shard_map/add_shares/pallas_call | solution.py:675
  123.0 4.1 %add_shares.28 = (f32[576,256]{1,0:T(8,128)}, f32[576,256]{1,0:T(8,128)}) custom-call(s32[30]{0:T(128)} %dynamic-slice_bitcast_fusion.info_ref, f32[4608,256]{1,0:T(8,128)} %get-tuple-element.78.refs_0_.refs_2_.refs_4_, f32[2304,256]{1,0:T(8,128)} %collective-permute-done.1.refs_1_.refs_5_, f32[2304,256]{1,0:T(8,128)} %collective-permute-done.2.refs_2_.refs_6_, ...), custom_call_target="tpu_custom_call" | custom-call | flops 1 | bytes 1 | tf_op jit(solution)/shard_map/add_shares/pallas_call | solution.py:675
  128.8 19.7 %attn_bwd.3 = (bf16[2,512,384]{2,1,0:T(8,128)(2,1)}, bf16[2,512,384]{2,1,0:T(8,128)(2,1)}, bf16[2,512,384]{2,1,0:T(8,128)(2,1)}, f32[3,2,768]{2,1,0:T(2,128)}, f32[1152,384]{1,0:T(8,128)}, /*index=5*/f32[1152,384]{1,0:T(8,128)}) custom-call(s32[30]{0:T(128)} %dynamic-slice_bitcast_fusion.info_ref, s32[2,8]{1,0:T(2,128)} %len_ref.9, ...), custom_call_target="tpu_custom_call" | custom-call | flops 99999997952 | bytes 1 | tf_op jit(solution)/shard_map/attn_bwd/pallas_call | solution.py:538
  156.8 3.8 add_shares.30.refs_2_
  164.9 4.3 %collective-permute-done.6.refs_1_ = f32[288,256]{1,0:T(8,128)S(1)} collective-permute-done((f32[288,256]{1,0:T(8,128)}, f32[288,256]{1,0:T(8,128)S(1)}, u32[]{:S(2)}, u32[]{:S(2)}) %collective-permute-start.6) | collective-permute-done | bytes 294944 | tf_op jit(solution)/shard_map/ppermute | solution.py:647
  177.1 4.1 %add_shares.34 = (f32[576,256]{1,0:T(8,128)}, f32[576,256]{1,0:T(8,128)}) custom-call(s32[30]{0:T(128)} %dynamic-slice_bitcast_fusion.info_ref, f32[4608,256]{1,0:T(8,128)} %get-tuple-element.90.refs_3_.refs_0_.refs_4_, f32[2304,256]{1,0:T(8,128)} %collective-permute-done.8.refs_1_.refs_5_, f32[2304,256]{1,0:T(8,128)} %collective-permute-done.9.refs_2_.refs_6_, ...), custom_call_target="tpu_custom_call" | custom-call | flops 1 | bytes 1 | tf_op jit(solution)/shard_map/add_shares/pallas_call | solution.py:675
  189.6 9.7 %tokgrad.1 = (bf16[1024,768]{1,0:T(8,128)(2,1)}, f32[1,768]{1,0:T(1,128)}) custom-call(bf16[1024,768]{1,0:T(8,128)(2,1)} %bitcast.27, f32[1024,768]{1,0:T(8,128)} %get-tuple-element.81.dres_ref, bf16[768]{0:T(1024)(128)(2,1)} %gain_ref.1, bf16[768,768]{1,0:T(8,128)(2,1)} %wq_ref.3, bf16[768,768]{1,0:T(8,128)(2,1)} %wk_ref.3, bf16[768,768]{1,0:T(8,128)(2,1)} %wv_ref.3, ...), custom_call_target="tpu_custom_call" | custom-call | flops 99999997952 | bytes 1 | tf_op jit(solution)/shard_map/tokgrad/pallas_call | solution.py:593
  210.3 5.1 %collective-permute-done.14.refs_1_ = f32[576,256]{1,0:T(8,128)} collective-permute-done((f32[576,256]{1,0:T(8,128)}, f32[576,256]{1,0:T(8,128)}, u32[]{:S(2)}, u32[]{:S(2)}) %collective-permute-start.14) | collective-permute-done | bytes 589856 | tf_op jit(solution)/shard_map/ppermute | solution.py:647
  268.3 6.3 %collective-permute-done.31.refs_1_ = f32[144,384]{1,0:T(8,128)S(1)} collective-permute-done((f32[144,384]{1,0:T(8,128)S(1)}, f32[144,384]{1,0:T(8,128)S(1)}, u32[]{:S(2)}, u32[]{:S(2)}) %collective-permute-start.31) | collective-permute-done | bytes 221216 | tf_op jit(solution)/shard_map/ppermute | solution.py:647
  278.7 8.8 %collective-permute-done.29.refs_1_ = f32[576,256]{1,0:T(8,128)S(1)} collective-permute-done((f32[576,256]{1,0:T(8,128)S(1)}, f32[576,256]{1,0:T(8,128)S(1)}, u32[]{:S(2)}, u32[]{:S(2)}) %collective-permute-start.29) | collective-permute-done | bytes 589856 | tf_op jit(solution)/shard_map/ppermute | solution.py:647
  298.7 10.5 %collective-permute-done.40.refs_1_ = f32[1152,256]{1,0:T(8,128)S(1)} collective-permute-done((f32[1152,256]{1,0:T(8,128)S(1)}, f32[1152,256]{1,0:T(8,128)S(1)}, u32[]{:S(2)}, u32[]{:S(2)}) %collective-permute-start.40) | collective-permute-done | bytes 1179680 | tf_op jit(solution)/shard_map/ppermute | solution.py:647
  314.2 9.2 %assemble.4 = (f32[768,3072]{1,0:T(8,128)}, f32[3072,768]{1,0:T(8,128)}) custom-call(s32[30]{0:T(128)} %dynamic-slice_bitcast_fusion.info_ref, f32[2304,256]{1,0:T(8,128)} %join.14.refs_0_, f32[2304,256]{1,0:T(8,128)} %collective-permute-done.38.refs_2_.refs_1_, f32[2304,256]{1,0:T(8,128)} %copy-done.7, f32[2304,256]{1,0:T(8,128)} %collective-permute-done.39.refs_3_, ...), custom_call_target="tpu_custom_call" | custom-call | flops 99999997952 | bytes 1 | tf_op jit(solution)/shard_map/assemble/pallas_call | solution.py:868
  330.3 8.3 %collective-permute-done.42.refs_1_ = f32[240,384]{1,0:T(8,128)S(1)} collective-permute-done((f32[240,384]{1,0:T(8,128)S(1)}, f32[240,384]{1,0:T(8,128)S(1)}, u32[]{:S(2)}, u32[]{:S(2)}) %collective-permute-start.42) | collective-permute-done | bytes 368672 | tf_op jit(solution)/shard_map/ppermute | solution.py:647
  343.1 7.9 %collective-permute-done.43.refs_1_ = f32[480,384]{1,0:T(8,128)S(1)} collective-permute-done((f32[480,384]{1,0:T(8,128)S(1)}, f32[480,384]{1,0:T(8,128)S(1)}, u32[]{:S(2)}, u32[]{:S(2)}) %collective-permute-start.43) | collective-permute-done | bytes 737312 | tf_op jit(solution)/shard_map/ppermute | solution.py:647
  356.0 4.9 %assemble.5 = (f32[768,768]{1,0:T(8,128)}, f32[768,768]{1,0:T(8,128)}, f32[768,768]{1,0:T(8,128)}) custom-call(s32[30]{0:T(128)} %dynamic-slice_bitcast_fusion.info_ref, f32[576,384]{1,0:T(8,128)} %join.19.refs_0_, f32[576,384]{1,0:T(8,128)} %collective-permute-done.47.refs_1_, f32[576,384]{1,0:T(8,128)} %collective-permute-done.34.refs_3_.refs_2_, ...), custom_call_target="tpu_custom_call" | custom-call | flops 99999997952 | bytes 1 | tf_op jit(solution)/shard_map/assemble/pallas_call | solution.py:868
  360.9 9.2 %assemble.7 = (f32[768,3072]{1,0:T(8,128)}, f32[3072,768]{1,0:T(8,128)}) custom-call(s32[30]{0:T(128)} %dynamic-slice_bitcast_fusion.info_ref, f32[2304,256]{1,0:T(8,128)} %join.20.refs_4_.refs_0_, f32[2304,256]{1,0:T(8,128)} %collective-permute-done.49.refs_1_.refs_6_, ...), custom_call_target="tpu_custom_call", output_to_operand_aliasing={{0}: (5, {}), {1}: (6, {})} | custom-call | flops 99999997952 | bytes 1 | tf_op jit(solution)/shard_map/assemble/pallas_call | solution.py:868
  376.7 6.5 %assemble.6 = (f32[768,768]{1,0:T(8,128)}, f32[768,768]{1,0:T(8,128)}, f32[768,768]{1,0:T(8,128)}, f32[768,768]{1,0:T(8,128)}) custom-call(s32[30]{0:T(128)} %dynamic-slice_bitcast_fusion.info_ref, f32[960,384]{1,0:T(8,128)} %join.23.refs_4_.refs_0_, ...), custom_call_target="tpu_custom_call", output_to_operand_aliasing={{0}: (5, {}), {1}: (6, {}), {2}: (7, {})} | custom-call | flops 99999997952 | bytes 1 | tf_op jit(solution)/shard_map/assemble/pallas_call | solution.py:868
  (229 shorter events, 147.3 us)
Async XLA Ops:
  50.4 41.5 %collective-permute-start.1 = (f32[2304,256]{1,0:T(8,128)}, f32[2304,256]{1,0:T(8,128)}, u32[]{:S(2)}, u32[]{:S(2)}) collective-permute-start(f32[2304,256]{1,0:T(8,128)} %get-tuple-element.89), channel_id=1, source_target_pairs={{0,1},{1,0},{2,3},{3,2},{4,5},{5,4},{6,7},{7,6},{8,9},{9,8},{10,11... | collective-permute-start | bytes 7077896 | tf_op jit(solution)/shard_map/ppermute | solution.py:651
  59.0 32.9 %collective-permute-start.2 = (f32[2304,256]{1,0:T(8,128)}, f32[2304,256]{1,0:T(8,128)}, u32[]{:S(2)}, u32[]{:S(2)}) collective-permute-start(f32[2304,256]{1,0:T(8,128)} %add_shares.25.refs_6_), channel_id=1, source_target_pairs={{0,2},{1,5},{2,0},{3,7},{4,6},{5,1},{6,4},{7,3},{8,10},{9,13},{10,... | collective-permute-start | bytes 7077896 | tf_op jit(solution)/shard_map/ppermute | solution.py:647
  90.1 28.3 %collective-permute-start.4 = (f32[2304,256]{1,0:T(8,128)}, f32[2304,256]{1,0:T(8,128)}, u32[]{:S(2)}, u32[]{:S(2)}) collective-permute-start(f32[2304,256]{1,0:T(8,128)} %get-tuple-element.94), channel_id=1, source_target_pairs={{0,1},{1,0},{2,3},{3,2},{4,5},{5,4},{6,7},{7,6},{8,9},{9,8},{10,11... | collective-permute-start | bytes 7077896 | tf_op jit(solution)/shard_map/ppermute | solution.py:651
  90.1 66.6 %collective-permute-start.8 = (f32[2304,256]{1,0:T(8,128)}, f32[2304,256]{1,0:T(8,128)}, u32[]{:S(2)}, u32[]{:S(2)}) collective-permute-start(f32[2304,256]{1,0:T(8,128)} %get-tuple-element.105), channel_id=1, source_target_pairs={{0,1},{1,0},{2,3},{3,2},{4,5},{5,4},{6,7},{7,6},{8,9},{9,8},{10,11... | collective-permute-start | bytes 7077896 | tf_op jit(solution)/shard_map/ppermute | solution.py:651
  95.8 27.3 %collective-permute-start.3 = (f32[1152,256]{1,0:T(8,128)}, f32[1152,256]{1,0:T(8,128)}, u32[]{:S(2)}, u32[]{:S(2)}) collective-permute-start(f32[1152,256]{1,0:T(8,128)} %add_shares.26.refs_1_), channel_id=1, source_target_pairs={{0,4},{1,3},{2,6},{3,1},{4,0},{5,7},{6,2},{7,5},{8,12},{9,11},{10,... | collective-permute-start | bytes 3538952 | tf_op jit(solution)/shard_map/ppermute | solution.py:647
  122.5 34.3 %collective-permute-start.9 = (f32[2304,256]{1,0:T(8,128)}, f32[2304,256]{1,0:T(8,128)}, u32[]{:S(2)}, u32[]{:S(2)}) collective-permute-start(f32[2304,256]{1,0:T(8,128)} %add_shares.27.refs_8_), channel_id=1, source_target_pairs={{0,2},{1,5},{2,0},{3,7},{4,6},{5,1},{6,4},{7,3},{8,10},{9,13},{10,... | collective-permute-start | bytes 7077896 | tf_op jit(solution)/shard_map/ppermute | solution.py:647
  123.0 38.4 %collective-permute-start.7 = (f32[1920,384]{1,0:T(8,128)}, f32[1920,384]{1,0:T(8,128)}, u32[]{:S(2)}, u32[]{:S(2)}) collective-permute-start(f32[1920,384]{1,0:T(8,128)} %get-tuple-element.104), channel_id=1, source_target_pairs={{0,1},{1,0},{2,3},{3,2},{4,5},{5,4},{6,7},{7,6},{8,9},{9,8},{10,11... | collective-permute-start | bytes 8847368 | tf_op jit(solution)/shard_map/ppermute | solution.py:651
  127.2 21.6 %collective-permute-start.5 = (f32[576,256]{1,0:T(8,128)}, f32[576,256]{1,0:T(8,128)}, u32[]{:S(2)}, u32[]{:S(2)}) collective-permute-start(f32[576,256]{1,0:T(8,128)} %get-tuple-element.96.refs_0_), channel_id=1, source_target_pairs={{0,8},{1,9},{2,10},{3,11},{4,12},{5,13},{6,14},{7,15},{8,0},{9,1},... | collective-permute-start | bytes 1769480 | tf_op jit(solution)/shard_map/ppermute | solution.py:647
  148.5 22.6 %collective-permute-start.12 = (f32[1152,384]{1,0:T(8,128)}, f32[1152,384]{1,0:T(8,128)}, u32[]{:S(2)}, u32[]{:S(2)}) collective-permute-start(f32[1152,384]{1,0:T(8,128)} %get-tuple-element.106), channel_id=1, source_target_pairs={{0,1},{1,0},{2,3},{3,2},{4,5},{5,4},{6,7},{7,6},{8,9},{9,8},{10,11... | collective-permute-start | bytes 5308424 | tf_op jit(solution)/shard_map/ppermute | solution.py:651
  174.8 32.3 %collective-permute-start.15 = (f32[576,384]{1,0:T(8,128)}, f32[576,384]{1,0:T(8,128)}, u32[]{:S(2)}, u32[]{:S(2)}) collective-permute-start(f32[576,384]{1,0:T(8,128)} %add_shares.33.refs_0_), channel_id=1, source_target_pairs={{0,2},{1,5},{2,0},{3,7},{4,6},{5,1},{6,4},{7,3},{8,10},{9,13},{10,... | collective-permute-start | bytes 2654216 | tf_op jit(solution)/shard_map/ppermute | solution.py:647
  176.3 51.2 %collective-permute-start.21 = (f32[960,384]{1,0:T(8,128)}, f32[960,384]{1,0:T(8,128)}, u32[]{:S(2)}, u32[]{:S(2)}) collective-permute-start(f32[960,384]{1,0:T(8,128)} %add_shares.31.refs_2_), channel_id=1, source_target_pairs={{0,2},{1,5},{2,0},{3,7},{4,6},{5,1},{6,4},{7,3},{8,10},{9,13},{10,... | collective-permute-start | bytes 4423688 | tf_op jit(solution)/shard_map/ppermute | solution.py:647
  181.3 20.4 %collective-permute-start.16 = (f32[576,256]{1,0:T(8,128)}, f32[576,256]{1,0:T(8,128)}, u32[]{:S(2)}, u32[]{:S(2)}) collective-permute-start(f32[576,256]{1,0:T(8,128)} %get-tuple-element.107.refs_2_), channel_id=1, source_target_pairs={{0,8},{1,9},{2,10},{3,11},{4,12},{5,13},{6,14},{7,15},{8,0},{9,1},... | collective-permute-start | bytes 1769480 | tf_op jit(solution)/shard_map/ppermute | solution.py:647
  189.5 25.9 %collective-permute-start.14 = (f32[576,256]{1,0:T(8,128)}, f32[576,256]{1,0:T(8,128)}, u32[]{:S(2)}, u32[]{:S(2)}) collective-permute-start(f32[576,256]{1,0:T(8,128)} %join.12.refs_6_.refs_0_), channel_id=1, source_target_pairs={{0,8},{1,9},{2,10},{3,11},{4,12},{5,13},{6,14},{7,15},{8,0},{9,1},... | collective-permute-start | bytes 1769480 | tf_op jit(solution)/shard_map/ppermute | solution.py:647
  204.7 32.0 %collective-permute-start.18 = (f32[288,256]{1,0:T(8,128)}, f32[288,256]{1,0:T(8,128)}, u32[]{:S(2)}, u32[]{:S(2)}) collective-permute-start(f32[288,256]{1,0:T(8,128)} %get-tuple-element.114.refs_3_), channel_id=1, source_target_pairs={{0,16},{1,17},{2,18},{3,19},{4,20},{5,21},{6,22},{7,23},{8,24},{9,... | collective-permute-start | bytes 884744 | tf_op jit(solution)/shard_map/ppermute | solution.py:647
  219.8 21.8 %collective-permute-start.26 = (f32[1152,256]{1,0:T(8,128)}, f32[1152,256]{1,0:T(8,128)}, u32[]{:S(2)}, u32[]{:S(2)}) collective-permute-start(f32[1152,256]{1,0:T(8,128)} %copy-done.4), channel_id=1, source_target_pairs={{0,4},{1,3},{2,6},{3,1},{4,0},{5,7},{6,2},{7,5},{8,12},{9,11},{10,... | collective-permute-start | bytes 3538952 | tf_op jit(solution)/shard_map/ppermute | solution.py:647
  231.3 25.1 %collective-permute-start.24 = (f32[480,384]{1,0:T(8,128)}, f32[480,384]{1,0:T(8,128)}, u32[]{:S(2)}, u32[]{:S(2)}) collective-permute-start(f32[480,384]{1,0:T(8,128)} %add_shares.39.refs_0_), channel_id=1, source_target_pairs={{0,4},{1,3},{2,6},{3,1},{4,0},{5,7},{6,2},{7,5},{8,12},{9,11},{10,... | collective-permute-start | bytes 2211848 | tf_op jit(solution)/shard_map/ppermute | solution.py:647
  238.3 21.4 %collective-permute-start.23 = (f32[288,256]{1,0:T(8,128)S(1)}, f32[288,256]{1,0:T(8,128)S(1)}, u32[]{:S(2)}, u32[]{:S(2)}) collective-permute-start(f32[288,256]{1,0:T(8,128)S(1)} %add_shares.41.refs_2_.refs_0_), channel_id=1, source_target_pairs={{0,16},{1,17},{2,18},{3,19},{4,20},{5,21},{6,22},{7,23},{8,24},{9,... | collective-permute-start | bytes 884744 | tf_op jit(solution)/shard_map/ppermute | solution.py:647
  245.2 33.4 %collective-permute-start.38 = (f32[2304,256]{1,0:T(8,128)}, f32[2304,256]{1,0:T(8,128)}, u32[]{:S(2)}, u32[]{:S(2)}) collective-permute-start(f32[2304,256]{1,0:T(8,128)} %join.14.refs_0_), channel_id=1, source_target_pairs={{0,2},{1,5},{2,0},{3,7},{4,6},{5,1},{6,4},{7,3},{8,10},{9,13},{10,... | collective-permute-start | bytes 7077896 | tf_op jit(solution)/shard_map/ppermute | solution.py:647
  266.3 21.1 %collective-permute-start.29 = (f32[576,256]{1,0:T(8,128)S(1)}, f32[576,256]{1,0:T(8,128)S(1)}, u32[]{:S(2)}, u32[]{:S(2)}) collective-permute-start(f32[576,256]{1,0:T(8,128)S(1)} %join.15.refs_2_.refs_0_), channel_id=1, source_target_pairs={{0,8},{1,9},{2,10},{3,11},{4,12},{5,13},{6,14},{7,15},{8,0},{9,1},... | collective-permute-start | bytes 1769480 | tf_op jit(solution)/shard_map/ppermute | solution.py:647
  278.7 35.5 %collective-permute-start.39 = (f32[2304,256]{1,0:T(8,128)}, f32[2304,256]{1,0:T(8,128)}, u32[]{:S(2)}, u32[]{:S(2)}) collective-permute-start(f32[2304,256]{1,0:T(8,128)} %collective-permute-done.38.refs_2_.refs_1_), channel_id=1, source_target_pairs={{0,1},{1,0},{2,3},{3,2},{4,5},{5,4},{6,7},{7,6},{8,9},{9,8},{10,11... | collective-permute-start | bytes 7077896 | tf_op jit(solution)/shard_map/ppermute | solution.py:651
  288.3 20.9 %collective-permute-start.40 = (f32[1152,256]{1,0:T(8,128)S(1)}, f32[1152,256]{1,0:T(8,128)S(1)}, u32[]{:S(2)}, u32[]{:S(2)}) collective-permute-start(f32[1152,256]{1,0:T(8,128)S(1)} %join.18.refs_2_.refs_0_), channel_id=1, source_target_pairs={{0,4},{1,3},{2,6},{3,1},{4,0},{5,7},{6,2},{7,5},{8,12},{9,11},{10,... | collective-permute-start | bytes 3538952 | tf_op jit(solution)/shard_map/ppermute | solution.py:647
  296.8 33.5 %collective-permute-start.47 = (f32[576,384]{1,0:T(8,128)}, f32[576,384]{1,0:T(8,128)}, u32[]{:S(2)}, u32[]{:S(2)}) collective-permute-start(f32[576,384]{1,0:T(8,128)} %join.19.refs_0_), channel_id=1, source_target_pairs={{0,2},{1,5},{2,0},{3,7},{4,6},{5,1},{6,4},{7,3},{8,10},{9,13},{10,... | collective-permute-start | bytes 2654216 | tf_op jit(solution)/shard_map/ppermute | solution.py:647
  311.7 31.4 %collective-permute-start.49 = (f32[2304,256]{1,0:T(8,128)}, f32[2304,256]{1,0:T(8,128)}, u32[]{:S(2)}, u32[]{:S(2)}) collective-permute-start(f32[2304,256]{1,0:T(8,128)} %join.20.refs_4_.refs_0_), channel_id=1, source_target_pairs={{0,2},{1,5},{2,0},{3,7},{4,6},{5,1},{6,4},{7,3},{8,10},{9,13},{10,... | collective-permute-start | bytes 7077896 | tf_op jit(solution)/shard_map/ppermute | solution.py:647
  330.3 24.7 %collective-permute-start.48 = (f32[576,384]{1,0:T(8,128)}, f32[576,384]{1,0:T(8,128)S(1)}, u32[]{:S(2)}, u32[]{:S(2)}) collective-permute-start(f32[576,384]{1,0:T(8,128)} %collective-permute-done.47.refs_1_), channel_id=1, source_target_pairs={{0,1},{1,0},{2,3},{3,2},{4,5},{5,4},{6,7},{7,6},{8,9},{9,8},{10,11... | collective-permute-start | bytes 2654216 | tf_op jit(solution)/shard_map/ppermute | solution.py:651
  (67 other events, 570.0 us)
